TPU v7x, 32 devices: a whole 2x2x4 slice. The times are simulated.
32 devices in a mesh: sky: 8 (over y, x, core), tm: 4 (over z).
Axes of the slice: x: 2, y: 2, z: 4, core: 2. Of those that a mesh axis runs over, the one named last changes fastest.
Arguments:
- residuals: float32 [262144], P(('sky', 'tm')), may hold values from -6 to 6
- weights: float32 [262144], P(('sky', 'tm')), may hold values from 0.1 to 10
- source_partials: bfloat16 [5, 262144], P(None, ('sky', 'tm')), may hold values from -1.5 to 1.5
- attitude_partials: bfloat16 [32, 262144], P(None, ('sky', 'tm')), may hold values from -0.025 to 0.045
- source_index: int32 [262144], P(('sky', 'tm')), may hold values from 0 to 4095, as said below
- tile_window: int32 [2048], P(('sky', 'tm')), may hold values from 0 to 511, as said below
- sources: float32 [5, 32768], P(None, 'sky'), may hold values from -6 to 6
- attitude: float32 [512, 32], P('tm'), may hold values from -6 to 6
- coupling: float32 [512], P('tm'), may hold values from 1 to 4
Outputs:
- new_sources: float32 [5, 32768], P(None, 'sky')
- new_attitude: float32 [512, 32], P('tm')
Inputs may be any that keep to these rules, and one draw needn't show every extreme that they name: source_index counts among the 4096 sources of the sky region of the device that holds the observation (devices ordered sky first, then tm). The tiles held by the device at tm index t have tile_window from t * 128 to (t + 1) * 128 - 1.
All inputs are finite; a program needn't handle non-finite values.
Results may differ from a plain program's by a relative error of at most 0.00039.
Values sent between devices are 32-bit elements; how exact they have to be, the bound alone decides.
No kernel may reach another device: no remote copies, remote signals or barrier semaphores. Data moves between devices by JAX's collectives and lax.ppermute only.
A program may use at most 64 MiB of HBM per device.

v0:
```python
import jax
import jax.numpy as jnp
import numpy as np
from jax import lax
from jax.sharding import PartitionSpec as P

TILE = 128
ITERS = 8


LOWER_PAIRS = tuple(((i, j) for i in range(5) for j in range(i + 1)))
DAMPING = 0.8
HIGHEST = lax.Precision.HIGHEST


def extended(block, sides, width, periodic):
    for axis, dim in sides:
        count = lax.axis_size(axis)
        forward = [(i, i + 1) for i in range(count - 1)]
        if periodic:
            forward.append((count - 1, 0))
        backward = [(target, source) for source, target in forward]
        low = lax.ppermute(
            lax.slice_in_dim(block, block.shape[dim] - width, None, axis=dim), axis, forward
        )
        high = lax.ppermute(lax.slice_in_dim(block, 0, width, axis=dim), axis, backward)
        block = jnp.concatenate([low, block, high], axis=dim)
    return block


def passed_along(x, axis, by):
    peers = lax.axis_size(axis)
    pairs = [(i, i + by) for i in range(peers) if 0 <= i + by < peers]
    return lax.ppermute(x, axis, pairs)


def moment_rows(partials, weights, residuals):
    values = partials.astype(jnp.float32)
    entries = [weights * values[i] * values[j] for i, j in LOWER_PAIRS]
    entries = entries + [weights * values[i] * residuals for i in range(5)]
    return jnp.stack(entries)


def solve_sources(moments):
    matrix = {}
    for position, pair in enumerate(LOWER_PAIRS):
        matrix[pair] = moments[position] + (1.0 if pair[0] == pair[1] else 0.0)
    factor = {}
    for i in range(5):
        for j in range(i + 1):
            reduced = matrix[i, j]
            for k in range(j):
                reduced = reduced - factor[i, k] * factor[j, k]
            if i == j:
                factor[i, i] = jnp.sqrt(reduced)
            else:
                factor[i, j] = reduced / factor[j, j]
    forward = []
    for i in range(5):
        current = moments[15 + i]
        for k in range(i):
            current = current - factor[i, k] * forward[k]
        forward.append(current / factor[i, i])
    result = [None] * 5
    for i in reversed(range(5)):
        current = forward[i]
        for k in range(i + 1, 5):
            current = current - factor[k, i] * result[k]
        result[i] = current / factor[i, i]
    return jnp.stack(result)


def window_inverse(symmetric, left_coupling, right_coupling):
    knot_count = symmetric.shape[1]
    identity = jnp.eye(knot_count, dtype=jnp.float32)
    blocks = symmetric + (left_coupling + right_coupling)[:, None, None] * identity
    lower_factor = jnp.linalg.cholesky(blocks)
    inverse_factor = jax.scipy.linalg.solve_triangular(
        lower_factor, jnp.broadcast_to(identity, blocks.shape), lower=True
    )
    return jnp.einsum("wlk,wlm->wkm", inverse_factor, inverse_factor, precision=HIGHEST)


def apply_blocks(blocks, vectors):
    return jnp.einsum("wkl,wl->wk", blocks, vectors, precision=HIGHEST)


def triangle_tables(knot_count):
    lower_rows, lower_cols = np.tril_indices(knot_count)
    pair_count = lower_rows.shape[0]
    positions = np.arange(pair_count)
    packer = np.zeros((knot_count * knot_count, pair_count), np.float32)
    first_cells = lower_rows * knot_count + lower_cols
    second_cells = lower_cols * knot_count + lower_rows
    packer[first_cells, positions] = 0.5
    packer[second_cells, positions] = packer[second_cells, positions] + 0.5
    unpacker = np.zeros((pair_count, knot_count * knot_count), np.float32)
    unpacker[positions, first_cells] = 1.0
    unpacker[positions, second_cells] = 1.0
    return (packer, unpacker)


def time_rim(values):
    return extended(values, (("tm", 0),), 1, False)


def sweep_step(change, symmetric, inverse, right_side, left_coupling, right_coupling, padded):
    applied = apply_blocks(symmetric, change) + (left_coupling + right_coupling)[:, None] * change
    applied = applied - left_coupling[:, None] * padded[:-2] - right_coupling[:, None] * padded[2:]
    return change + DAMPING * apply_blocks(inverse, right_side - applied)


def on_device(
    residuals,
    weights,
    source_partials,
    attitude_partials,
    source_index,
    tile_window,
    sources,
    attitude,
    coupling,
):
    source_count = sources.shape[1]
    window_count = attitude.shape[0]
    knot_count = attitude.shape[1]
    tile_count = attitude_partials.shape[1] // TILE
    summands = moment_rows(source_partials, weights, residuals)
    moments = jnp.zeros((20, source_count), jnp.float32).at[:, source_index].add(summands)
    scaled = (weights[None, :] * attitude_partials.astype(jnp.float32)).astype(jnp.bfloat16)
    shaped_att = attitude_partials.reshape(knot_count, tile_count, TILE)
    tile_normal = jnp.einsum(
        "ktp,ltp->tkl",
        scaled.reshape(knot_count, tile_count, TILE),
        shaped_att,
        preferred_element_type=jnp.float32,
    )
    tile_normal = tile_normal.reshape(tile_count, knot_count * knot_count)
    first_window = lax.axis_index("tm") * window_count
    window_ids = lax.broadcasted_iota(jnp.int32, (window_count, tile_count), 0)
    selector = (tile_window[None, :] - first_window == window_ids).astype(jnp.float32)
    normal_local = jnp.dot(selector, tile_normal, precision=HIGHEST)
    totals = lax.psum(moments, "tm")
    source_change = solve_sources(totals)
    new_sources = sources + source_change
    picked = source_change[:, source_index]
    corrected = residuals - jnp.sum(source_partials.astype(jnp.float32) * picked, axis=0)
    weighted = (weights * corrected).astype(jnp.bfloat16)
    tile_rhs = jnp.einsum(
        "ktp,tp->tk",
        shaped_att,
        weighted.reshape(tile_count, TILE),
        preferred_element_type=jnp.float32,
    )
    rhs_local = jnp.dot(selector, tile_rhs, precision=HIGHEST)
    previous = passed_along(coupling[-1:], "tm", 1)
    left_coupling = jnp.concatenate([previous, coupling[:-1]])
    is_final = lax.axis_index("tm") == lax.axis_size("tm") - 1
    final_slot = lax.broadcasted_iota(jnp.int32, (window_count,), 0) == window_count - 1
    right_coupling = jnp.where(jnp.logical_and(is_final, final_slot), 0.0, coupling)
    packer, unpacker = triangle_tables(knot_count)
    packed_local = jnp.dot(normal_local, packer, precision=HIGHEST)
    packed, right_side = (
        lax.psum_scatter(packed_local, "sky", scatter_dimension=0, tiled=True),
        lax.psum_scatter(rhs_local, "sky", scatter_dimension=0, tiled=True),
    )
    own_count = packed.shape[0]
    symmetric = jnp.dot(packed, unpacker, precision=HIGHEST).reshape(
        own_count, knot_count, knot_count
    )
    sky_index = lax.axis_index("sky")
    sky_last = lax.axis_size("sky") - 1
    offset = sky_index * own_count
    left_own = lax.dynamic_slice_in_dim(left_coupling, offset, own_count, 0)
    right_own = lax.dynamic_slice_in_dim(right_coupling, offset, own_count, 0)
    inverse = window_inverse(symmetric, left_own, right_own)
    change = DAMPING * apply_blocks(inverse, right_side)
    for sweep in range(ITERS - 1):
        rims = extended(change, (("sky", 0),), 1, True)
        below_sky = rims[0:1]
        above_sky = rims[-1:]
        crossed = time_rim(jnp.concatenate([above_sky, below_sky], axis=0))
        below = jnp.where(sky_index == 0, crossed[0:1], below_sky)
        above = jnp.where(sky_index == sky_last, crossed[3:4], above_sky)
        padded = jnp.concatenate([below, change, above], axis=0)
        change = sweep_step(change, symmetric, inverse, right_side, left_own, right_own, padded)
    change = lax.all_gather(change, "sky", axis=0, tiled=True)
    return (new_sources, attitude + change)


def solution(mesh):
    return jax.shard_map(
        on_device,
        mesh=mesh,
        in_specs=(
            P(("sky", "tm")),
            P(("sky", "tm")),
            P(None, ("sky", "tm")),
            P(None, ("sky", "tm")),
            P(("sky", "tm")),
            P(("sky", "tm")),
            P(None, "sky"),
            P("tm", None),
            P("tm"),
        ),
        out_specs=(P(None, "sky"), P("tm", None)),
        check_vma=False,
    )
```

profile of v0, /device:TPU:0, one launch (start us, length us, event | category | flops | bytes accessed | tf_op | source)
XLA Modules:
  0.0 360.6 jit_solution(6277305444816827479)
XLA Ops:
  8.0 1.9 copy.70
  10.2 9.9 %slice_reduce_fusion = (f32[8192]{0:T(1024)S(1)}, f32[8192]{0:T(1024)S(1)}, f32[8192]{0:T(1024)S(1)}, f32[8192]{0:T(1024)S(1)}, f32[8192]{0:T(1024)S(1)}) fusion(f32[5,8192]{0,1:T(8,128)S(1)} %convert_element_type.23), kind=kLoop, calls=%fused_computation.2 | loop fusion | bytes 327680 | tf_op jit(solution)/shard_map/slice | solution.py:39
  20.9 2.4 stack.91
  23.4 2.6 copy.71
  26.0 45.8 %scatter_custom_fusion = f32[20,4096]{0,1:T(8,128)} fusion(s32[8192]{0:T(1024)S(1)} %get-tuple-element.58, f32[8192,20]{1,0:T(8,128)} %copy.71, f32[]{:T(128)} %constant.63.clone.1), kind=kCustom, calls=%fused_computation.10 | custom fusion | flops 163840 | bytes 328192 | tf_op jit(solution)/shard_map/scatter-add | solution.py:129
  71.8 3.0 copy.72
  75.4 5.4 %collective-permute-start = (f32[1]{0:T(128)}, f32[1]{0:T(128)}, u32[]{:S(2)}, u32[]{:S(2)}) collective-permute-start(f32[1]{0:T(128)} %slice.246), channel_id=1, source_target_pairs={{0,1},{1,2},{2,3},{4,5},{5,6},{6,7},{8,9},{9,10},{10,11},{12,13},{... | collective-permute-start | bytes 20 | tf_op jit(solution)/shard_map/ppermute | solution.py:34
  80.8 1.6 fusion.6
  82.4 1.4 copy.75
  83.8 1.5 fusion.17
  85.3 4.2 %fusion.103 = f32[128,528]{1,0:T(8,128)} fusion(f32[128,1024]{1,0:T(8,128)S(1)} %fusion.17, f32[1024,528]{1,0:T(8,128)} %constant.79.clone), kind=kOutput, calls=%fused_computation.191 | convolution fusion | flops 830472192 | bytes 2957312 | tf_op jit(solution)/shard_map/dot_general | solution.py:162
  90.5 24.2 %all-reduce.2.cloned.1.call-done = f32[20,4096]{1,0:T(8,128)} async-done(((f32[20,4096]{1,0:T(8,128)}), f32[20,4096]{1,0:T(8,128)}) %all-reduce.2.cloned.1.call-update) | async-done | bytes 327696 | tf_op jit(solution)/shard_map/psum | solution.py:143
  114.7 2.5 fusion.48
  117.3 1.8 fusion.49
  119.1 1.7 subtract_divide_fusion
  120.9 2.0 copy.82
  122.9 29.5 %gather_fusion = f32[8192,5]{1,0:T(8,128)} fusion(f32[5,4096]{0,1:T(8,128)} %copy.82, s32[8192]{0:T(1024)S(1)} %get-tuple-element.57), kind=kCustom, calls=%fused_computation | custom fusion | bytes 360448 | tf_op jit(solution)/shard_map/gather | solution.py:146
  152.4 3.4 fusion
  156.9 0.8 fusion.16
  157.8 2.9 fusion.104
  161.3 46.9 %custom-call.8 = f32[16,32,32]{2,1,0:T(8,128)S(1)} custom-call(f32[16,32,32]{2,1,0:T(8,128)S(1)} %fusion.14), custom_call_target="Cholesky" | custom-call | tf_op jit(solution)/shard_map/jit(cholesky)/cholesky | solution.py:77
  208.4 39.4 %custom-call.9 = f32[16,1,32,32]{2,3,1,0:T(8,128)S(1)} custom-call(f32[16,1,32,32]{3,2,1,0:T(8,128)S(1)} %select_bitcast_fusion), custom_call_target="InvertDiagBlocksLowerTriangular" | custom-call | tf_op jit(solution)/shard_map/jit(_solve_triangular)/vmap()/triangular_solve | solution.py:78
  249.1 1.3 fusion.106
  251.0 2.6 collective-permute-start.3
  253.6 1.2 collective-permute-done.1
  254.8 3.2 collective-permute-start.2
  258.1 1.3 collective-permute-start.4
  259.4 4.1 %collective-permute-done.4 = f32[1,32]{1,0:T(1,128)S(1)} collective-permute-done((f32[1,32]{1,0:T(1,128)S(1)}, f32[1,32]{1,0:T(1,128)S(1)}, u32[]{:S(2)}, u32[]{:S(2)}) %collective-permute-start.4) | collective-permute-done | bytes 160 | tf_op jit(solution)/shard_map/ppermute | solution.py:26
  263.5 0.8 fusion.82
  265.4 2.6 collective-permute-start.7
  268.0 1.2 collective-permute-done.5
  269.3 3.0 collective-permute-start.6
  272.3 1.3 collective-permute-start.8
  273.6 4.1 %collective-permute-done.8 = f32[1,32]{1,0:T(1,128)S(1)} collective-permute-done((f32[1,32]{1,0:T(1,128)S(1)}, f32[1,32]{1,0:T(1,128)S(1)}, u32[]{:S(2)}, u32[]{:S(2)}) %collective-permute-start.8) | collective-permute-done | bytes 160 | tf_op jit(solution)/shard_map/ppermute | solution.py:26
  277.7 0.8 fusion.77
  279.6 2.6 collective-permute-start.11
  282.3 1.2 collective-permute-done.9
  283.5 2.5 collective-permute-start.10
  286.0 1.3 collective-permute-start.12
  287.3 4.1 %collective-permute-done.12 = f32[1,32]{1,0:T(1,128)S(1)} collective-permute-done((f32[1,32]{1,0:T(1,128)S(1)}, f32[1,32]{1,0:T(1,128)S(1)}, u32[]{:S(2)}, u32[]{:S(2)}) %collective-permute-start.12) | collective-permute-done | bytes 160 | tf_op jit(solution)/shard_map/ppermute | solution.py:26
  291.5 0.8 fusion.72
  293.4 2.6 collective-permute-start.15
  296.0 1.2 collective-permute-done.13
  297.2 1.9 collective-permute-start.14
  299.1 1.3 collective-permute-start.16
  300.5 4.1 %collective-permute-done.16 = f32[1,32]{1,0:T(1,128)S(1)} collective-permute-done((f32[1,32]{1,0:T(1,128)S(1)}, f32[1,32]{1,0:T(1,128)S(1)}, u32[]{:S(2)}, u32[]{:S(2)}) %collective-permute-start.16) | collective-permute-done | bytes 160 | tf_op jit(solution)/shard_map/ppermute | solution.py:26
  304.6 0.8 fusion.67
  306.5 2.6 collective-permute-start.19
  309.1 1.2 collective-permute-done.17
  310.3 1.9 collective-permute-start.18
  312.2 1.3 collective-permute-start.20
  313.6 4.1 %collective-permute-done.20 = f32[1,32]{1,0:T(1,128)S(1)} collective-permute-done((f32[1,32]{1,0:T(1,128)S(1)}, f32[1,32]{1,0:T(1,128)S(1)}, u32[]{:S(2)}, u32[]{:S(2)}) %collective-permute-start.20) | collective-permute-done | bytes 160 | tf_op jit(solution)/shard_map/ppermute | solution.py:26
  318.9 2.6 collective-permute-start.23
  321.5 1.2 collective-permute-done.21
  322.7 1.9 collective-permute-start.22
  324.7 1.3 collective-permute-start.24
  326.0 4.1 %collective-permute-done.24 = f32[1,32]{1,0:T(1,128)S(1)} collective-permute-done((f32[1,32]{1,0:T(1,128)S(1)}, f32[1,32]{1,0:T(1,128)S(1)}, u32[]{:S(2)}, u32[]{:S(2)}) %collective-permute-start.24) | collective-permute-done | bytes 160 | tf_op jit(solution)/shard_map/ppermute | solution.py:26
  331.3 2.6 collective-permute-start.27
  333.9 1.2 collective-permute-done.25
  335.2 1.9 collective-permute-start.26
  337.1 1.3 collective-permute-start.28
  338.4 4.1 %collective-permute-done.28 = f32[1,32]{1,0:T(1,128)S(1)} collective-permute-done((f32[1,32]{1,0:T(1,128)S(1)}, f32[1,32]{1,0:T(1,128)S(1)}, u32[]{:S(2)}, u32[]{:S(2)}) %collective-permute-start.28) | collective-permute-done | bytes 160 | tf_op jit(solution)/shard_map/ppermute | solution.py:26
  343.1 9.3 %all_gather.3 = f32[128,32]{1,0:T(8,128)S(1)} all-gather(f32[16,32]{1,0:T(8,128)S(1)} %multiply_add_fusion.1), channel_id=1, replica_groups=mesh['sky'=8,'tm'=4] {'sky'}, dimensions={0}, use_global_device_ids=true | all-gather | bytes 18432 | tf_op jit(solution)/shard_map/all_gather | solution.py:187
  352.5 0.7 copy.84
  (123 shorter events, 14.1 us)
Async XLA Ops:
  8.0 106.7 %all-reduce.2.cloned.1.call-start = ((), (), s32[]{:S(2)}) async-start(), calls=%async_computation.2 | async-start | bytes 786432 | tf_op jit(solution)/shard_map/psum | solution.py:143
  10.2 10.0 %copy-start.2 = (f32[8192]{0:T(1024)S(1)}, f32[8192]{0:T(1024)}, u32[]{:S(2)}) copy-start(f32[8192]{0:T(1024)} %param.12) | copy-start | bytes 98308
  10.2 10.0 %copy-start.4 = (f32[8192]{0:T(1024)S(1)}, f32[8192]{0:T(1024)}, u32[]{:S(2)}) copy-start(f32[8192]{0:T(1024)} %param.11) | copy-start | bytes 98308
  23.4 2.7 copy-start.5
  26.0 48.8 %copy-start.8 = (f32[128]{0:T(128)S(1)}, f32[128]{0:T(128)}, u32[]{:S(2)}) copy-start(f32[128]{0:T(128)} %param.19) | copy-start | bytes 1540
  74.8 9.1 %copy-start.7 = (s32[64]{0:T(128)S(1)}, s32[64]{0:T(128)}, u32[]{:S(2)}) copy-start(s32[64]{0:T(128)} %param.16) | copy-start | bytes 772
  74.8 83.0 %reduce-scatter.3.cloned.1.call-start = ((), (), s32[]{:S(2)}) async-start(), calls=%async_computation.3 | async-start | bytes 368640 | tf_op jit(solution)/shard_map/reduce_scatter | solution.py:164
  75.4 14.4 %collective-permute-start = (f32[1]{0:T(128)}, f32[1]{0:T(128)}, u32[]{:S(2)}, u32[]{:S(2)}) collective-permute-start(f32[1]{0:T(128)} %slice.246), channel_id=1, source_target_pairs={{0,1},{1,2},{2,3},{4,5},{5,6},{6,7},{8,9},{9,10},{10,11},{12,13},{... | collective-permute-start | bytes 20 | tf_op jit(solution)/shard_map/ppermute | solution.py:34
  83.8 5.9 %copy-start.6 = (f32[128,32]{0,1:T(8,128)S(1)}, f32[128,32]{0,1:T(8,128)}, u32[]{:S(2)}) copy-start(f32[128,32]{0,1:T(8,128)} %param.18) | copy-start | bytes 49156
  89.5 159.6 %reduce-scatter.5.cloned.1.call-start = ((), (), s32[]{:S(2)}) async-start(), calls=%async_computation.4 | async-start | bytes 73728 | tf_op jit(solution)/shard_map/reduce_scatter | solution.py:165
  152.4 3.4 copy-start.3
  152.4 4.1 %copy-start = (bf16[32,8192]{1,0:T(8,128)(2,1)S(1)}, bf16[32,8192]{1,0:T(8,128)(2,1)}, u32[]{:S(2)}) copy-start(bf16[32,8192]{1,0:T(8,128)(2,1)} %param.14) | copy-start | bytes 1572868
  249.1 68.6 %copy-start.1 = (f32[16,32]{1,0:T(8,128)S(1)}, f32[16,32]{1,0:T(8,128)}, u32[]{:S(2)}) copy-start(f32[16,32]{1,0:T(8,128)} %reduce-scatter.5.cloned.1.call-done) | copy-start | bytes 6148
  250.9 3.9 %collective-permute-start.1 = (f32[1,32]{1,0:T(1,128)S(1)}, f32[1,32]{1,0:T(1,128)S(1)}, u32[]{:S(2)}, u32[]{:S(2)}) collective-permute-start(f32[1,32]{1,0:T(1,128)S(1)} %get-tuple-element.80), channel_id=1, source_target_pairs={{0,4},{4,8},{8,12},{12,16},{16,20},{20,24},{24,28},{28,0},{1,5},{5... | collective-permute-start | bytes 392 | tf_op jit(solution)/shard_map/ppermute | solution.py:23
  251.0 7.1 %collective-permute-start.3 = (f32[1,32]{1,0:T(1,128)S(1)}, f32[1,32]{1,0:T(1,128)S(1)}, u32[]{:S(2)}, u32[]{:S(2)}) collective-permute-start(f32[1,32]{1,0:T(1,128)S(1)} %get-tuple-element.81), channel_id=1, source_target_pairs={{4,0},{8,4},{12,8},{16,12},{20,16},{24,20},{28,24},{0,28},{5,1},{9... | collective-permute-start | bytes 392 | tf_op jit(solution)/shard_map/ppermute | solution.py:26
  254.8 4.5 %collective-permute-start.2 = (f32[1,32]{1,0:T(1,128)S(1)}, f32[1,32]{1,0:T(1,128)S(1)}, u32[]{:S(2)}, u32[]{:S(2)}) collective-permute-start(f32[1,32]{1,0:T(1,128)S(1)} %collective-permute-done.1), channel_id=1, source_target_pairs={{0,1},{1,2},{2,3},{4,5},{5,6},{6,7},{8,9},{9,10},{10,11},{12,13},{... | collective-permute-start | bytes 392 | tf_op jit(solution)/shard_map/ppermute | solution.py:23
  258.1 5.4 %collective-permute-start.4 = (f32[1,32]{1,0:T(1,128)S(1)}, f32[1,32]{1,0:T(1,128)S(1)}, u32[]{:S(2)}, u32[]{:S(2)}) collective-permute-start(f32[1,32]{1,0:T(1,128)S(1)} %collective-permute-done.3), channel_id=1, source_target_pairs={{1,0},{2,1},{3,2},{5,4},{6,5},{7,6},{9,8},{10,9},{11,10},{13,12},{... | collective-permute-start | bytes 392 | tf_op jit(solution)/shard_map/ppermute | solution.py:26
  265.3 3.9 %collective-permute-start.5 = (f32[1,32]{1,0:T(1,128)S(1)}, f32[1,32]{1,0:T(1,128)S(1)}, u32[]{:S(2)}, u32[]{:S(2)}) collective-permute-start(f32[1,32]{1,0:T(1,128)S(1)} %get-tuple-element.78), channel_id=1, source_target_pairs={{0,4},{4,8},{8,12},{12,16},{16,20},{20,24},{24,28},{28,0},{1,5},{5... | collective-permute-start | bytes 392 | tf_op jit(solution)/shard_map/ppermute | solution.py:23
  265.4 6.9 %collective-permute-start.7 = (f32[1,32]{1,0:T(1,128)S(1)}, f32[1,32]{1,0:T(1,128)S(1)}, u32[]{:S(2)}, u32[]{:S(2)}) collective-permute-start(f32[1,32]{1,0:T(1,128)S(1)} %get-tuple-element.79), channel_id=1, source_target_pairs={{4,0},{8,4},{12,8},{16,12},{20,16},{24,20},{28,24},{0,28},{5,1},{9... | collective-permute-start | bytes 392 | tf_op jit(solution)/shard_map/ppermute | solution.py:26
  269.3 4.3 %collective-permute-start.6 = (f32[1,32]{1,0:T(1,128)S(1)}, f32[1,32]{1,0:T(1,128)S(1)}, u32[]{:S(2)}, u32[]{:S(2)}) collective-permute-start(f32[1,32]{1,0:T(1,128)S(1)} %collective-permute-done.5), channel_id=1, source_target_pairs={{0,1},{1,2},{2,3},{4,5},{5,6},{6,7},{8,9},{9,10},{10,11},{12,13},{... | collective-permute-start | bytes 392 | tf_op jit(solution)/shard_map/ppermute | solution.py:23
  272.3 5.4 %collective-permute-start.8 = (f32[1,32]{1,0:T(1,128)S(1)}, f32[1,32]{1,0:T(1,128)S(1)}, u32[]{:S(2)}, u32[]{:S(2)}) collective-permute-start(f32[1,32]{1,0:T(1,128)S(1)} %collective-permute-done.7), channel_id=1, source_target_pairs={{1,0},{2,1},{3,2},{5,4},{6,5},{7,6},{9,8},{10,9},{11,10},{13,12},{... | collective-permute-start | bytes 392 | tf_op jit(solution)/shard_map/ppermute | solution.py:26
  279.6 3.9 %collective-permute-start.9 = (f32[1,32]{1,0:T(1,128)S(1)}, f32[1,32]{1,0:T(1,128)S(1)}, u32[]{:S(2)}, u32[]{:S(2)}) collective-permute-start(f32[1,32]{1,0:T(1,128)S(1)} %get-tuple-element.76), channel_id=1, source_target_pairs={{0,4},{4,8},{8,12},{12,16},{16,20},{20,24},{24,28},{28,0},{1,5},{5... | collective-permute-start | bytes 392 | tf_op jit(solution)/shard_map/ppermute | solution.py:23
  279.6 6.4 %collective-permute-start.11 = (f32[1,32]{1,0:T(1,128)S(1)}, f32[1,32]{1,0:T(1,128)S(1)}, u32[]{:S(2)}, u32[]{:S(2)}) collective-permute-start(f32[1,32]{1,0:T(1,128)S(1)} %get-tuple-element.77), channel_id=1, source_target_pairs={{4,0},{8,4},{12,8},{16,12},{20,16},{24,20},{28,24},{0,28},{5,1},{9... | collective-permute-start | bytes 392 | tf_op jit(solution)/shard_map/ppermute | solution.py:26
  283.5 3.8 %collective-permute-start.10 = (f32[1,32]{1,0:T(1,128)S(1)}, f32[1,32]{1,0:T(1,128)S(1)}, u32[]{:S(2)}, u32[]{:S(2)}) collective-permute-start(f32[1,32]{1,0:T(1,128)S(1)} %collective-permute-done.9), channel_id=1, source_target_pairs={{0,1},{1,2},{2,3},{4,5},{5,6},{6,7},{8,9},{9,10},{10,11},{12,13},{... | collective-permute-start | bytes 392 | tf_op jit(solution)/shard_map/ppermute | solution.py:23
  286.0 5.4 %collective-permute-start.12 = (f32[1,32]{1,0:T(1,128)S(1)}, f32[1,32]{1,0:T(1,128)S(1)}, u32[]{:S(2)}, u32[]{:S(2)}) collective-permute-start(f32[1,32]{1,0:T(1,128)S(1)} %collective-permute-done.11), channel_id=1, source_target_pairs={{1,0},{2,1},{3,2},{5,4},{6,5},{7,6},{9,8},{10,9},{11,10},{13,12},{... | collective-permute-start | bytes 392 | tf_op jit(solution)/shard_map/ppermute | solution.py:26
  293.3 3.9 %collective-permute-start.13 = (f32[1,32]{1,0:T(1,128)S(1)}, f32[1,32]{1,0:T(1,128)S(1)}, u32[]{:S(2)}, u32[]{:S(2)}) collective-permute-start(f32[1,32]{1,0:T(1,128)S(1)} %get-tuple-element.74), channel_id=1, source_target_pairs={{0,4},{4,8},{8,12},{12,16},{16,20},{20,24},{24,28},{28,0},{1,5},{5... | collective-permute-start | bytes 392 | tf_op jit(solution)/shard_map/ppermute | solution.py:23
  293.4 5.8 %collective-permute-start.15 = (f32[1,32]{1,0:T(1,128)S(1)}, f32[1,32]{1,0:T(1,128)S(1)}, u32[]{:S(2)}, u32[]{:S(2)}) collective-permute-start(f32[1,32]{1,0:T(1,128)S(1)} %get-tuple-element.75), channel_id=1, source_target_pairs={{4,0},{8,4},{12,8},{16,12},{20,16},{24,20},{28,24},{0,28},{5,1},{9... | collective-permute-start | bytes 392 | tf_op jit(solution)/shard_map/ppermute | solution.py:26
  297.2 3.2 collective-permute-start.14
  299.1 5.4 %collective-permute-start.16 = (f32[1,32]{1,0:T(1,128)S(1)}, f32[1,32]{1,0:T(1,128)S(1)}, u32[]{:S(2)}, u32[]{:S(2)}) collective-permute-start(f32[1,32]{1,0:T(1,128)S(1)} %collective-permute-done.15), channel_id=1, source_target_pairs={{1,0},{2,1},{3,2},{5,4},{6,5},{7,6},{9,8},{10,9},{11,10},{13,12},{... | collective-permute-start | bytes 392 | tf_op jit(solution)/shard_map/ppermute | solution.py:26
  306.4 3.9 %collective-permute-start.17 = (f32[1,32]{1,0:T(1,128)S(1)}, f32[1,32]{1,0:T(1,128)S(1)}, u32[]{:S(2)}, u32[]{:S(2)}) collective-permute-start(f32[1,32]{1,0:T(1,128)S(1)} %get-tuple-element.72), channel_id=1, source_target_pairs={{0,4},{4,8},{8,12},{12,16},{16,20},{20,24},{24,28},{28,0},{1,5},{5... | collective-permute-start | bytes 392 | tf_op jit(solution)/shard_map/ppermute | solution.py:23
  306.5 5.8 %collective-permute-start.19 = (f32[1,32]{1,0:T(1,128)S(1)}, f32[1,32]{1,0:T(1,128)S(1)}, u32[]{:S(2)}, u32[]{:S(2)}) collective-permute-start(f32[1,32]{1,0:T(1,128)S(1)} %get-tuple-element.73), channel_id=1, source_target_pairs={{4,0},{8,4},{12,8},{16,12},{20,16},{24,20},{28,24},{0,28},{5,1},{9... | collective-permute-start | bytes 392 | tf_op jit(solution)/shard_map/ppermute | solution.py:26
  310.3 3.2 collective-permute-start.18
  312.2 5.4 %collective-permute-start.20 = (f32[1,32]{1,0:T(1,128)S(1)}, f32[1,32]{1,0:T(1,128)S(1)}, u32[]{:S(2)}, u32[]{:S(2)}) collective-permute-start(f32[1,32]{1,0:T(1,128)S(1)} %collective-permute-done.19), channel_id=1, source_target_pairs={{1,0},{2,1},{3,2},{5,4},{6,5},{7,6},{9,8},{10,9},{11,10},{13,12},{... | collective-permute-start | bytes 392 | tf_op jit(solution)/shard_map/ppermute | solution.py:26
  318.8 3.9 %collective-permute-start.21 = (f32[1,32]{1,0:T(1,128)S(1)}, f32[1,32]{1,0:T(1,128)S(1)}, u32[]{:S(2)}, u32[]{:S(2)}) collective-permute-start(f32[1,32]{1,0:T(1,128)S(1)} %get-tuple-element.70), channel_id=1, source_target_pairs={{0,4},{4,8},{8,12},{12,16},{16,20},{20,24},{24,28},{28,0},{1,5},{5... | collective-permute-start | bytes 392 | tf_op jit(solution)/shard_map/ppermute | solution.py:23
  318.9 5.8 %collective-permute-start.23 = (f32[1,32]{1,0:T(1,128)S(1)}, f32[1,32]{1,0:T(1,128)S(1)}, u32[]{:S(2)}, u32[]{:S(2)}) collective-permute-start(f32[1,32]{1,0:T(1,128)S(1)} %get-tuple-element.71), channel_id=1, source_target_pairs={{4,0},{8,4},{12,8},{16,12},{20,16},{24,20},{28,24},{0,28},{5,1},{9... | collective-permute-start | bytes 392 | tf_op jit(solution)/shard_map/ppermute | solution.py:26
  322.7 3.2 collective-permute-start.22
  324.7 5.4 %collective-permute-start.24 = (f32[1,32]{1,0:T(1,128)S(1)}, f32[1,32]{1,0:T(1,128)S(1)}, u32[]{:S(2)}, u32[]{:S(2)}) collective-permute-start(f32[1,32]{1,0:T(1,128)S(1)} %collective-permute-done.23), channel_id=1, source_target_pairs={{1,0},{2,1},{3,2},{5,4},{6,5},{7,6},{9,8},{10,9},{11,10},{13,12},{... | collective-permute-start | bytes 392 | tf_op jit(solution)/shard_map/ppermute | solution.py:26
  331.3 3.9 %collective-permute-start.25 = (f32[1,32]{1,0:T(1,128)S(1)}, f32[1,32]{1,0:T(1,128)S(1)}, u32[]{:S(2)}, u32[]{:S(2)}) collective-permute-start(f32[1,32]{1,0:T(1,128)S(1)} %get-tuple-element.68), channel_id=1, source_target_pairs={{0,4},{4,8},{8,12},{12,16},{16,20},{20,24},{24,28},{28,0},{1,5},{5... | collective-permute-start | bytes 392 | tf_op jit(solution)/shard_map/ppermute | solution.py:23
  331.3 5.8 %collective-permute-start.27 = (f32[1,32]{1,0:T(1,128)S(1)}, f32[1,32]{1,0:T(1,128)S(1)}, u32[]{:S(2)}, u32[]{:S(2)}) collective-permute-start(f32[1,32]{1,0:T(1,128)S(1)} %get-tuple-element.69), channel_id=1, source_target_pairs={{4,0},{8,4},{12,8},{16,12},{20,16},{24,20},{28,24},{0,28},{5,1},{9... | collective-permute-start | bytes 392 | tf_op jit(solution)/shard_map/ppermute | solution.py:26
  335.2 3.2 collective-permute-start.26
  337.1 5.4 %collective-permute-start.28 = (f32[1,32]{1,0:T(1,128)S(1)}, f32[1,32]{1,0:T(1,128)S(1)}, u32[]{:S(2)}, u32[]{:S(2)}) collective-permute-start(f32[1,32]{1,0:T(1,128)S(1)} %collective-permute-done.27), channel_id=1, source_target_pairs={{1,0},{2,1},{3,2},{5,4},{6,5},{7,6},{9,8},{10,9},{11,10},{13,12},{... | collective-permute-start | bytes 392 | tf_op jit(solution)/shard_map/ppermute | solution.py:26
Sparse Core Ops, SparseCore 0:
  74.9 39.7 all-reduce.1
Sparse Core Ops, SparseCore 1:
  89.6 33.8 reduce-scatter.2
  157.8 33.5 reduce-scatter.4
where the time goes:
time: 362 us; the launch traced here: 361 us
  other arithmetic  148 us (41%)
  waiting for transfers between devices  61.6 us (17%)
  local copies, waits for them, and re-layouts  54.8 us (15%)
  starting transfers between devices  49.8 us (14%)
  matrix products  21.1 us (6%)
  between operations  16.2 us (4%)
  blocking collectives  9.3 us (3%)
    another operation x4, other arithmetic, window_inverse(): lower_factor = jnp.linalg.cholesky(blocks)  47.1 us
    scatter-add x1, other arithmetic, on_device(): jnp.zeros((20, source_count), jnp.float32).at[:, source_index].add(summands)  45.8 us
    another operation x3, other arithmetic, window_inverse(): jax.scipy.linalg.solve_triangular(lower_factor, jnp.broadcast_to(identity...  39.5 us
    gather x1, local copies, waits for them, and re-layouts, on_device(): picked = source_change[:, source_index]  29.5 us
    ppermute x14, waiting for transfers between devices, extended(): lax.ppermute(lax.slice_in_dim(block, 0, width, axis=dim), axis, backward)  28.8 us
    ppermute x14, starting transfers between devices, extended(): lax.ppermute(lax.slice_in_dim(block, 0, width, axis=dim), axis, backward)  27.5 us
    psum x1, waiting for transfers between devices, on_device(): totals = lax.psum(moments, 'tm')  24.2 us
    ppermute x14, starting transfers between devices, extended(): lax.ppermute(lax.slice_in_dim(block, block.shape[dim] - width, None, axis...  16.8 us
  transfers between devices with their start and end apart: 32, of which 15 were waited for; matrix products, arithmetic and copies ran while one was open for 40% of the time, Pallas kernels for 0%

commit v1 on v0

v1 whole, which is shorter than its diff:
```python
import functools

import jax
import jax.numpy as jnp
from jax import lax
from jax.experimental import pallas as pl
from jax.experimental.pallas import tpu as pltpu
from jax.sharding import PartitionSpec as P

TILE = 128
ITERS = 8
DAMPING = 0.8
PARAMS = 5
PAIRS = tuple((i, j) for i in range(PARAMS) for j in range(i + 1))
MOMENTS = len(PAIRS) + PARAMS
LANES = 128
SPLITS = 3
CHUNK = 1024
ROWS = CHUNK // TILE
F32 = jnp.float32
BF16 = jnp.bfloat16
NT = (((1,), (1,)), ((), ()))
VMEM_LIMIT = 48 * 1024 * 1024


def vmem():
    return pl.BlockSpec(memory_space=pltpu.VMEM)


def smem():
    return pl.BlockSpec(memory_space=pltpu.SMEM)


def call(kernel, out_shape, in_specs, scratch=(), flops=0, traffic=0):
    return pl.pallas_call(
        kernel,
        out_shape=out_shape,
        in_specs=in_specs,
        out_specs=jax.tree.map(lambda _: vmem(), out_shape),
        scratch_shapes=list(scratch),
        compiler_params=pltpu.CompilerParams(vmem_limit_bytes=VMEM_LIMIT),
        cost_estimate=pl.CostEstimate(flops=flops, bytes_accessed=traffic, transcendentals=0),
    )


def iota(shape, dim):
    return lax.broadcasted_iota(jnp.int32, shape, dim)


def split_bf16(x, parts):
    out = []
    for part in range(parts):
        head = x.astype(BF16)
        out.append(head)
        if part < parts - 1:
            x = x - head.astype(F32)
    return out


def low_one_hot(row, half, low_count):
    low = (row // half) * LANES + (row & (LANES - 1))
    return jnp.where(iota((low_count, LANES), 0) == low, 1.0, 0.0).astype(BF16)


def high_digit(row, half):
    return (row & (half - 1)) // LANES


def moments_kernel(hi_count, me_ref, src_ref, w_ref, r_ref, sp_ref, tie_ref, *refs):
    peers = len(refs) - 4
    outs, (lhs, rhs, acc, blocks) = refs[:peers], refs[peers:]
    half = hi_count * LANES
    low_count = rhs.shape[0]
    acc[...] = jnp.zeros_like(acc)

    def chunk(c, carry):
        base = pl.multiple_of(c * ROWS, ROWS)
        src = src_ref[pl.ds(base, ROWS), :]
        w = w_ref[pl.ds(base, ROWS), :]
        r = r_ref[pl.ds(base, ROWS), :]
        columns = [
            sp_ref[:, pl.ds(pl.multiple_of((base + i) * TILE, TILE), TILE)].astype(F32)
            for i in range(ROWS)
        ]
        a = [
            jnp.concatenate([columns[i][p : p + 1] for i in range(ROWS)], axis=0)
            for p in range(PARAMS)
        ]
        wa = [w * x for x in a]
        sums = [wa[i] * a[j] for i, j in PAIRS] + [x * r for x in wa]
        parts = [[piece.astype(F32) for piece in split_bf16(s, SPLITS)] for s in sums]
        for i in range(ROWS):
            lanes = slice(i * TILE, (i + 1) * TILE)
            row = src[i : i + 1]
            rhs[:, lanes] = low_one_hot(row, half, low_count)
            mask = jnp.where(iota((hi_count, LANES), 0) == high_digit(row, half), 1.0, 0.0).astype(BF16)
            for s in range(SPLITS):
                for p in range(MOMENTS):
                    value = jnp.broadcast_to(parts[p][s][i : i + 1], (hi_count, LANES)).astype(BF16)
                    start = (s * MOMENTS + p) * hi_count
                    lhs[start : start + hi_count, lanes] = value * mask
        acc[...] += lax.dot_general(lhs[...], rhs[...], NT, preferred_element_type=F32)
        return carry

    lax.fori_loop(0, src_ref.shape[0] // ROWS, chunk, 0)
    rows = blocks.shape[2]
    for p in range(MOMENTS):
        total = acc[p * hi_count : (p + 1) * hi_count, :]
        for s in range(1, SPLITS):
            start = (s * MOMENTS + p) * hi_count
            total = total + acc[start : start + hi_count, :]
        for j in range(peers):
            q, first = divmod(j * rows, hi_count)
            blocks[j, p] = total[first : first + rows, q * LANES : (q + 1) * LANES]
    for j in range(peers):
        blocks[j, MOMENTS] = jnp.broadcast_to(tie_ref[...], (rows, LANES))
    me = me_ref[0]
    for k in range(peers):
        outs[k][...] = blocks[me ^ k]


def normals_kernel(win_ref, w_ref, att_ref, out_ref):
    windows = out_ref.shape[0]
    knots = att_ref.shape[0]
    copies = LANES // knots
    out_ref[...] = jnp.zeros_like(out_ref)
    blank = jnp.zeros((knots, TILE), BF16)
    lane = iota((8, LANES), 1)

    def pair(u, carry):
        att = att_ref[:, pl.ds(pl.multiple_of(u * 2 * TILE, 2 * TILE), 2 * TILE)]
        w = jnp.concatenate([w_ref[pl.ds(2 * u, 1), :], w_ref[pl.ds(2 * u + 1, 1), :]], axis=1)
        scaled = (w * att.astype(F32)).astype(BF16)
        left = jnp.concatenate([scaled[:, :TILE], blank], axis=1)
        right = jnp.concatenate([blank, scaled[:, TILE:]], axis=1)
        normal = lax.dot_general(
            jnp.concatenate([left, right], axis=0),
            jnp.concatenate([att] * copies, axis=0),
            NT,
            preferred_element_type=F32,
        )
        for h in range(2):
            value = normal[h * knots : h * knots + 8]
            for g in range(1, copies):
                start = h * knots + 8 * g
                value = jnp.where(lane < g * knots, value, normal[start : start + 8])
            slot = lax.rem(win_ref[2 * u + h], windows)
            out_ref[slot] += value
        return carry

    lax.fori_loop(0, w_ref.shape[0] // 2, pair, 0, unroll=4)


def solve_kernel(me_ref, *refs):
    peers = len(refs) - 3
    blocks, (change_ref, ties_ref, rows_scr) = refs[:peers], refs[peers:]
    moments = blocks[0][0:MOMENTS]
    for other in blocks[1:]:
        moments = moments + other[0:MOMENTS]
    matrix = {}
    for position, (i, j) in enumerate(PAIRS):
        matrix[i, j] = moments[position] + (1.0 if i == j else 0.0)
    factor, inverse = {}, {}
    for i in range(PARAMS):
        for j in range(i + 1):
            reduced = matrix[i, j]
            for k in range(j):
                reduced = reduced - factor[i, k] * factor[j, k]
            if i == j:
                factor[i, i] = jnp.sqrt(reduced)
                inverse[i] = 1.0 / factor[i, i]
            else:
                factor[i, j] = reduced * inverse[j]
    forward = []
    for i in range(PARAMS):
        current = moments[len(PAIRS) + i]
        for k in range(i):
            current = current - factor[i, k] * forward[k]
        forward.append(current * inverse[i])
    result = [None] * PARAMS
    for i in reversed(range(PARAMS)):
        current = forward[i]
        for k in range(i + 1, PARAMS):
            current = current - factor[k, i] * result[k]
        result[i] = current * inverse[i]
        change_ref[i] = result[i]
    me = me_ref[0]
    for k in range(peers):
        rows_scr[me ^ k] = jnp.broadcast_to(blocks[k][MOMENTS, 0:1, :], (8, LANES))
    first, last = me == 0, me == peers - 1
    own = rows_scr[me]
    before = jnp.where(first, 0.0, rows_scr[jnp.maximum(me - 1, 0)])
    after = jnp.where(last, 0.0, rows_scr[jnp.minimum(me + 1, peers - 1)])
    lane = iota((8, LANES), 1)
    own = jnp.where(jnp.logical_and(last, lane == LANES - 1), 0.0, own)
    own_left = jnp.where(lane == 0, pltpu.roll(before, 1, 1), pltpu.roll(own, 1, 1))
    low, high = lane < ITERS - 1, lane > LANES - ITERS
    rim_right = jnp.where(low, after, jnp.where(high, before, 0.0))
    after_left = jnp.where(lane == 0, pltpu.roll(own, 1, 1), pltpu.roll(after, 1, 1))
    rim_left = jnp.where(low, after_left, jnp.where(high, pltpu.roll(before, 1, 1), 0.0))
    ties_ref[0] = own_left
    ties_ref[1] = own
    ties_ref[2] = rim_left
    ties_ref[3] = rim_right


def invert_kernel(sky_ref, part_ref, ties_ref, out_ref, flat, cells):
    devices, own, eight, _ = part_ref.shape
    knots = cells.shape[0] // 32 if False else 32
    total = part_ref[0]
    for s in range(1, devices):
        total = total + part_ref[s]
    flat[...] = jnp.zeros_like(flat)
    flat[0 : own * 8, :] = total.reshape(own * 8, LANES)
    groups = LANES // knots
    for r in range(8):
        turned = flat[pl.ds(r, LANES, stride=8), :].T
        for g in range(groups):
            cells[(8 * g + r) * knots : (8 * g + r + 1) * knots, :] = turned[g * knots : (g + 1) * knots]
    shift = lax.rem(LANES - sky_ref[0] * own, LANES)
    ties = pltpu.roll(ties_ref[0] + ties_ref[1], shift, 1)
    diagonal = jnp.concatenate([ties] * (knots // 8), axis=0)
    inner = iota((knots, LANES), 0)
    blocks = []
    for k in range(knots):
        row = 0.5 * (cells[k * knots : (k + 1) * knots, :] + cells[pl.ds(k, knots, stride=knots), :])
        blocks.append(jnp.where(inner == k, row + diagonal, row))
    for k in range(knots):
        cells[k * knots : (k + 1) * knots, :] = blocks[k]

    def sweep(k, carry):
        at = pl.multiple_of(k * knots, knots)
        row = cells[pl.ds(at, knots), :]
        pivot = 1.0 / cells[pl.ds(at + k, 1), :]
        here = inner == k
        scaled = jnp.where(here, -pivot, row * pivot)
        for i in range(knots):
            old = jnp.where(here, 0.0, cells[i * knots : (i + 1) * knots, :])
            cells[i * knots : (i + 1) * knots, :] = old - row[i : i + 1] * scaled
        cells[pl.ds(at, knots), :] = scaled
        return carry

    lax.fori_loop(0, knots, sweep, 0)
    for r in range(8):
        turned = jnp.concatenate(
            [cells[(8 * g + r) * knots : (8 * g + r + 1) * knots, :] for g in range(groups)], axis=0
        ).T
        flat[pl.ds(r, LANES, stride=8), :] = -turned
    out_ref[...] = flat[0 : own * 8, :].reshape(own, 8, LANES)


def rhs_kernel(hi_count, me_ref, win_ref, src_ref, w_ref, r_ref, sp_ref, att_ref, sources_ref, inv_ref, *refs):
    peers = len(refs) - 7
    blocks = refs[:peers]
    new_ref, out_ref, changes, table, rhs, chosen, weighted = refs[peers:]
    half = hi_count * LANES
    low_count = rhs.shape[0]
    windows = LANES
    knots = att_ref.shape[0]
    own = inv_ref.shape[0]
    me = me_ref[0]
    for k in range(peers):
        changes[me ^ k] = blocks[k][...]
    rows = blocks[0].shape[1]
    for j in range(peers):
        q, first = divmod(j * rows, hi_count)
        for p in range(PARAMS):
            value = changes[j, p]
            for s, piece in enumerate(split_bf16(value, SPLITS)):
                start = (s * PARAMS + p) * hi_count + first
                table[start : start + rows, q * LANES : (q + 1) * LANES] = piece.astype(F32)
        for i in range(rows):
            lanes = slice((j * rows + i) * LANES, (j * rows + i + 1) * LANES)
            step = jnp.concatenate([changes[j, p, i : i + 1, :] for p in range(PARAMS)], axis=0)
            new_ref[:, lanes] = sources_ref[:, lanes] + step
    lookup = table[...].astype(BF16)

    def chunk(c, total):
        base = pl.multiple_of(c * ROWS, ROWS)
        src = src_ref[pl.ds(base, ROWS), :]
        w = w_ref[pl.ds(base, ROWS), :]
        r = r_ref[pl.ds(base, ROWS), :]
        for i in range(ROWS):
            rhs[:, i * TILE : (i + 1) * TILE] = low_one_hot(src[i : i + 1], half, low_count)
        chosen[...] = jnp.dot(lookup, rhs[...], preferred_element_type=F32)
        for i in range(ROWS):
            lanes = slice(i * TILE, (i + 1) * TILE)
            columns = sp_ref[:, pl.ds(pl.multiple_of((base + i) * TILE, TILE), TILE)].astype(F32)
            model = jnp.zeros((hi_count, LANES), F32)
            for p in range(PARAMS):
                value = chosen[p * hi_count : (p + 1) * hi_count, lanes]
                for s in range(1, SPLITS):
                    start = (s * PARAMS + p) * hi_count
                    value = value + chosen[start : start + hi_count, lanes]
                model = model + value * columns[p : p + 1]
            here = iota((hi_count, LANES), 0) == high_digit(src[i : i + 1], half)
            model = jnp.sum(jnp.where(here, model, 0.0), axis=0, keepdims=True)
            change = w[i : i + 1] * (r[i : i + 1] - model)
            slot = lax.rem(win_ref[base + i], windows)
            weighted[:, lanes] = jnp.where(iota((windows, LANES), 0) == slot, change, 0.0).astype(BF16)
        att = att_ref[:, pl.ds(pl.multiple_of(base * TILE, CHUNK), CHUNK)]
        return total + lax.dot_general(att, weighted[...], NT, preferred_element_type=F32)

    total = lax.fori_loop(0, src_ref.shape[0] // ROWS, chunk, jnp.zeros((knots, windows), F32))
    out_ref[0:own] = inv_ref[...]
    out_ref[own : own + knots // 8] = total.reshape(knots // 8, 8, LANES)


def rim_kernel(all_ref, low_ref, high_ref, main_ref):
    devices, blocks, _, _ = all_ref.shape
    own = blocks - 4
    sides = all_ref[0, own:blocks]
    for s in range(1, devices):
        sides = sides + all_ref[s, own:blocks]
    main_ref[...] = sides
    low_ref[8:12] = sides
    high_ref[8:12] = sides
    for w in range(8):
        low_ref[w] = all_ref[w // own, w % own]
        far = devices * own - 8 + w
        high_ref[w] = all_ref[far // own, far % own]


def turn_kernel(all_ref, main_ref, flat):
    devices, blocks, _, _ = all_ref.shape
    own = blocks - 4
    knots = 32
    groups = LANES // knots
    for s in range(devices):
        flat[s * own * 8 : (s + 1) * own * 8, :] = all_ref[s, 0:own].reshape(own * 8, LANES)
    for r in range(8):
        turned = flat[pl.ds(r, LANES, stride=8), :].T
        for g in range(groups):
            main_ref[(8 * g + r) * knots : (8 * g + r + 1) * knots, :] = turned[g * knots : (g + 1) * knots]


def sweeps_kernel(main_ref, sides_ref, low_ref, high_ref, ties_ref, attitude_ref, out_ref, flat, rim, vector):
    knots = attitude_ref.shape[1]
    groups = LANES // knots
    flat[...] = jnp.zeros_like(flat)
    flat[0:64, :] = low_ref[0:8].reshape(64, LANES)
    flat[960:1024, :] = high_ref[0:8].reshape(64, LANES)
    for r in range(8):
        turned = flat[pl.ds(r, LANES, stride=8), :].T
        for g in range(groups):
            rim[(8 * g + r) * knots : (8 * g + r + 1) * knots, :] = turned[g * knots : (g + 1) * knots]
    lane = iota((knots, LANES), 1)
    rim_sides = jnp.where(
        lane < ITERS - 1,
        low_ref[8:12].reshape(knots, LANES),
        jnp.where(lane > LANES - ITERS, high_ref[8:12].reshape(knots, LANES), 0.0),
    )
    sides = jnp.concatenate([sides_ref[...].reshape(knots, LANES), rim_sides], axis=1)

    def wide(a, b):
        return DAMPING * jnp.concatenate([jnp.concatenate([a, b], axis=1)] * (knots // 8), axis=0)

    left = wide(ties_ref[0], ties_ref[2])
    right = wide(ties_ref[1], ties_ref[3])

    def applied(x):
        vector[...] = x
        main = jnp.zeros((knots, LANES), F32)
        side = jnp.zeros((knots, LANES), F32)
        for k in range(knots):
            row = vector[k : k + 1, :]
            main = main + main_ref[k * knots : (k + 1) * knots, :] * row[:, :LANES]
            side = side + rim[k * knots : (k + 1) * knots, :] * row[:, LANES:]
        return jnp.concatenate([main, side], axis=1)

    first = applied(DAMPING * sides)

    def sweep(_, change):
        ends = left * pltpu.roll(change, 1, 1) + right * pltpu.roll(change, 2 * LANES - 1, 1)
        return (1.0 - DAMPING) * change + first + applied(ends)

    change = lax.fori_loop(0, ITERS - 1, sweep, first)
    out_ref[...] = attitude_ref[...] + change[:, :LANES].T


def on_device(
    residuals, weights, source_partials, attitude_partials, source_index, tile_window, sources, attitude, coupling
):
    peers = lax.axis_size("tm")
    devices = lax.axis_size("sky")
    source_count = sources.shape[1]
    windows, knots = attitude.shape
    tiles = residuals.shape[0] // TILE
    own = windows // devices
    rows = source_count // LANES // peers
    hi_count = source_count // (2 * LANES)
    low_count = 2 * LANES
    me = lax.axis_index("tm").astype(jnp.int32).reshape(1)
    sky = lax.axis_index("sky").astype(jnp.int32).reshape(1)
    src = source_index.reshape(tiles, TILE)
    w = weights.reshape(tiles, TILE)
    r = residuals.reshape(tiles, TILE)

    def exchanged(blocks):
        return [blocks[0]] + [
            lax.ppermute(blocks[k], "tm", [(i, i ^ k) for i in range(peers)]) for k in range(1, peers)
        ]

    block = jax.ShapeDtypeStruct((MOMENTS + 1, rows, LANES), F32)
    with jax.named_scope("moments"):
        blocks = call(
            functools.partial(moments_kernel, hi_count),
            [block] * peers,
            [smem()] + [vmem()] * 5,
            [
                pltpu.VMEM((SPLITS * MOMENTS * hi_count, CHUNK), BF16),
                pltpu.VMEM((low_count, CHUNK), BF16),
                pltpu.VMEM((SPLITS * MOMENTS * hi_count, low_count), F32),
                pltpu.VMEM((peers, MOMENTS + 1, rows, LANES), F32),
            ],
        )(me, src, w, r, source_partials, coupling.reshape(1, windows))
    blocks = exchanged(blocks)
    with jax.named_scope("normals"):
        normals = call(
            normals_kernel,
            jax.ShapeDtypeStruct((windows, knots * knots // LANES, LANES), F32),
            [smem(), vmem(), vmem()],
        )(tile_window, w, attitude_partials)
    parts = lax.all_to_all(
        normals.reshape(devices, own, knots * knots // LANES, LANES), "sky", 0, 0, tiled=True
    )
    with jax.named_scope("solve"):
        change, ties = call(
            solve_kernel,
            [
                jax.ShapeDtypeStruct((PARAMS, rows, LANES), F32),
                jax.ShapeDtypeStruct((4, 8, LANES), F32),
            ],
            [smem()] + [vmem()] * peers,
            [pltpu.VMEM((peers, 8, LANES), F32)],
        )(me, *blocks)
    changes = exchanged([change] * peers)
    with jax.named_scope("invert"):
        inverse = call(
            invert_kernel,
            jax.ShapeDtypeStruct((own, knots * knots // LANES, LANES), F32),
            [smem(), vmem(), vmem()],
            [pltpu.VMEM((8 * LANES, LANES), F32), pltpu.VMEM((knots * knots, LANES), F32)],
        )(sky, parts, ties)
    with jax.named_scope("right_sides"):
        new_sources, part = call(
            functools.partial(rhs_kernel, hi_count),
            [
                jax.ShapeDtypeStruct(sources.shape, F32),
                jax.ShapeDtypeStruct((own + knots // 8, 8, LANES), F32),
            ],
            [smem(), smem()] + [vmem()] * (7 + peers),
            [
                pltpu.VMEM((peers, PARAMS, rows, LANES), F32),
                pltpu.VMEM((SPLITS * PARAMS * hi_count, low_count), F32),
                pltpu.VMEM((low_count, CHUNK), BF16),
                pltpu.VMEM((SPLITS * PARAMS * hi_count, CHUNK), F32),
                pltpu.VMEM((windows, CHUNK), BF16),
            ],
        )(me, tile_window, src, w, r, source_partials, attitude_partials, sources, inverse, *changes)
    gathered = lax.all_gather(part, "sky", axis=0, tiled=False)
    with jax.named_scope("rims"):
        rim = jax.ShapeDtypeStruct((12, 8, LANES), F32)
        low, high, sides = call(
            rim_kernel, [rim, rim, jax.ShapeDtypeStruct((4, 8, LANES), F32)], [vmem()]
        )(gathered)
    after = lax.ppermute(low, "tm", [(i, i - 1) for i in range(1, peers)])
    before = lax.ppermute(high, "tm", [(i, i + 1) for i in range(peers - 1)])
    with jax.named_scope("turn"):
        main = call(
            turn_kernel,
            jax.ShapeDtypeStruct((knots * knots, LANES), F32),
            [vmem()],
            [pltpu.VMEM((8 * LANES, LANES), F32)],
        )(gathered)
    with jax.named_scope("sweeps"):
        new_attitude = call(
            sweeps_kernel,
            jax.ShapeDtypeStruct(attitude.shape, F32),
            [vmem()] * 6,
            [
                pltpu.VMEM((8 * LANES, LANES), F32),
                pltpu.VMEM((knots * knots, LANES), F32),
                pltpu.VMEM((knots, 2 * LANES), F32),
            ],
        )(main, sides, after, before, ties, attitude)
    return new_sources, new_attitude


def solution(mesh):
    return jax.shard_map(
        on_device,
        mesh=mesh,
        in_specs=(
            P(("sky", "tm")),
            P(("sky", "tm")),
            P(None, ("sky", "tm")),
            P(None, ("sky", "tm")),
            P(("sky", "tm")),
            P(("sky", "tm")),
            P(None, "sky"),
            P("tm", None),
            P("tm"),
        ),
        out_specs=(P(None, "sky"), P("tm", None)),
        check_vma=False,
    )
```

time: 362 us -> 66.8 us (0.18)
  other arithmetic: 148 us -> 0 us
  waiting for transfers between devices: 61.6 us -> 9.88 us
  local copies, waits for them, and re-layouts: 54.8 us -> 3.86 us
  starting transfers between devices: 49.8 us -> 20.1 us
  Pallas kernels: 0 us -> 21.3 us
  matrix products: 21.1 us -> 0 us
  between operations: 16.2 us -> 0.78 us
    another operation x7 -> x0, other arithmetic: 86.6 us -> none  [the longest x4 47.1 us: window_inverse(): lower_factor = jnp.linalg.cholesky(blocks)]
    scatter-add x1 -> x0, other arithmetic: 45.8 us -> none  [on_device(): jnp.zeros((20, source_count), jnp.float32).at[:, source_index].add(summands)]
    ppermute x29 -> x8, starting transfers between devices: 49.6 us -> 14.7 us  [the longest x6 8.9 us: exchanged(): lax.ppermute(blocks[k], 'tm', [(i, i ^ k) for i in range(peers)])]
    gather x1 -> x0, local copies, waits for them, and re-layouts: 29.5 us -> none  [on_device(): picked = source_change[:, source_index]]
    ppermute x29 -> x8, waiting for transfers between devices: 37.3 us -> 9.87 us  [the longest x6 8.49 us: exchanged(): lax.ppermute(blocks[k], 'tm', [(i, i ^ k) for i in range(peers)])]
    psum x1 -> x0, waiting for transfers between devices: 24.2 us -> none  [on_device(): totals = lax.psum(moments, 'tm')]
    pallas_call x0 -> x8, Pallas kernels: none -> 21.3 us  [the longest x1 7.49 us: on_device(): call(functools.partial(moments_kernel, hi_count), [block] * peers, [smem(...]
    dot_general x22 -> x0, matrix products: 20.5 us -> none  [the longest x15 8.56 us: apply_blocks(): return jnp.einsum('wkl,wl->wk', blocks, vectors, precision=HIGHEST)]
  transfers between devices with their start and end apart: 32 -> 9, of which waited for: 15 -> 4; matrix products, arithmetic and copies ran while one was open for 40% -> 0% of each run, Pallas kernels for 0% -> 16%
where the time goes in v1:
time: 66.8 us; the launch traced here: 66.4 us
  Pallas kernels  21.3 us (32%)
  starting transfers between devices  20.1 us (30%)
  blocking collectives  10.5 us (16%)
  waiting for transfers between devices  9.88 us (15%)
  local copies, waits for them, and re-layouts  3.86 us (6%)
  between operations  0.78 us (1%)
    all_gather x1, blocking collectives, on_device(): gathered = lax.all_gather(part, 'sky', axis=0, tiled=False)  10.5 us
    ppermute x6, starting transfers between devices, exchanged(): lax.ppermute(blocks[k], 'tm', [(i, i ^ k) for i in range(peers)])  8.9 us
    ppermute x6, waiting for transfers between devices, exchanged(): lax.ppermute(blocks[k], 'tm', [(i, i ^ k) for i in range(peers)])  8.49 us
    pallas_call x1, Pallas kernels, on_device(): call(functools.partial(moments_kernel, hi_count), [block] * peers, [smem(...  7.49 us
    pallas_call x1, Pallas kernels, on_device(): call(functools.partial(rhs_kernel, hi_count), [jax.ShapeDtypeStruct(sourc...  6.07 us
    all_to_all x1, starting transfers between devices, on_device(): lax.all_to_all(normals.reshape(devices, own, knots * knots // LANES, LANE...  5.32 us
    ppermute x1, starting transfers between devices, on_device(): before = lax.ppermute(high, 'tm', [(i, i + 1) for i in range(peers - 1)])  4.55 us
    unnamed x24, local copies, waits for them, and re-layouts  3.86 us
  transfers between devices with their start and end apart: 9, of which 4 were waited for; matrix products, arithmetic and copies ran while one was open for 0% of the time, Pallas kernels for 16%

profile of v1, /device:TPU:0, one launch (start us, length us, event | category | flops | bytes accessed | tf_op | source)
XLA Modules:
  0.0 66.4 jit_solution(1653670637939439568)
XLA Ops:
  0.6 0.0 copy-start.8
  0.6 0.6 copy-done.8
  1.3 0.0 copy-start
  1.3 1.0 %copy-done = bf16[32,8192]{1,0:T(8,128)(2,1)S(1)} copy-done((bf16[32,8192]{1,0:T(8,128)(2,1)S(1)}, bf16[32,8192]{1,0:T(8,128)(2,1)}, u32[]{:S(2)}) %copy-start) | copy-done | bytes 524312
  2.3 0.0 copy-start.3
  2.3 0.8 %copy-done.3 = f32[8192]{0:T(1024)S(1)} copy-done((f32[8192]{0:T(1024)S(1)}, f32[8192]{0:T(1024)}, u32[]{:S(2)}) %copy-start.3) | copy-done | bytes 32792
  3.1 3.1 %normals.1 = f32[128,8,128]{2,1,0:T(8,128)} custom-call(s32[64]{0:T(128)S(1)} %copy-done.8, f32[64,128]{1,0:T(8,128)S(1)} %bitcast.10, bf16[32,8192]{1,0:T(8,128)(2,1)S(1)} %copy-done), custom_call_target="tpu_custom_call" | custom-call | tf_op jit(solution)/shard_map/normals/pallas_call | solution.py:419
  6.2 0.0 copy-start.2
  6.2 0.0 copy-start.4
  6.2 0.0 copy-start.6
  6.2 0.0 copy-start.7
  6.2 5.3 %all-to-all-start = ((f32[8,16,8,128]{3,2,1,0:T(8,128)}), f32[8,16,8,128]{3,2,1,0:T(8,128)S(1)}, u32[]{:S(2)}, u32[]{:S(2)}) async-start(f32[8,16,8,128]{3,2,1,0:T(8,128)} %bitcast.5), calls=%async_computation | async-start | bytes 1048576 | tf_op jit(solution)/shard_map/all_to_all | solution.py:424
  11.6 0.0 copy-start.9
  11.6 0.0 copy-done.2
  11.6 0.0 copy-done.4
  11.6 0.0 copy-done.6
  11.6 0.0 copy-done.7
  11.6 0.6 copy-done.9
  12.2 7.5 %moments.1 = (f32[21,8,128]{2,1,0:T(8,128)S(1)}, f32[21,8,128]{2,1,0:T(8,128)S(1)}, f32[21,8,128]{2,1,0:T(8,128)S(1)}, f32[21,8,128]{2,1,0:T(8,128)S(1)}) custom-call(s32[1]{0:T(128)} %bitcast.me_ref, s32[64,128]{1,0:T(8,128)S(1)} %bitcast.13, f32[64,128]{1,0:T(8,128)S(1)} %bitcast.11, f32[64,128]{1,0:T(8,128)S(1)} %bitcast.15, ...), custom_call_target="tpu_custom_call" | custom-call | tf_op jit(solution)/shard_map/moments/pallas_call | solution.py:406
  19.7 0.0 copy-start.1
  19.7 1.6 %collective-permute-start = (f32[21,8,128]{2,1,0:T(8,128)S(1)}, f32[21,8,128]{2,1,0:T(8,128)S(1)}, u32[]{:S(2)}, u32[]{:S(2)}) collective-permute-start(f32[21,8,128]{2,1,0:T(8,128)S(1)} %get-tuple-element.14), channel_id=1, source_target_pairs={{0,1},{1,0},{2,3},{3,2},{4,5},{5,4},{6,7},{7,6},{8,9},{9,8},{10,11... | collective-permute-start | bytes 258056 | tf_op jit(solution)/shard_map/ppermute | solution.py:401
  21.4 2.6 %collective-permute-start.1 = (f32[21,8,128]{2,1,0:T(8,128)S(1)}, f32[21,8,128]{2,1,0:T(8,128)S(1)}, u32[]{:S(2)}, u32[]{:S(2)}) collective-permute-start(f32[21,8,128]{2,1,0:T(8,128)S(1)} %get-tuple-element.15), channel_id=1, source_target_pairs={{0,2},{1,3},{2,0},{3,1},{4,6},{5,7},{6,4},{7,5},{8,10},{9,11},{10,... | collective-permute-start | bytes 258056 | tf_op jit(solution)/shard_map/ppermute | solution.py:401
  23.9 0.2 collective-permute-start.2
  24.2 0.6 collective-permute-done.refs_1_
  24.7 6.5 %collective-permute-done.1.refs_2_ = f32[21,8,128]{2,1,0:T(8,128)S(1)} collective-permute-done((f32[21,8,128]{2,1,0:T(8,128)S(1)}, f32[21,8,128]{2,1,0:T(8,128)S(1)}, u32[]{:S(2)}, u32[]{:S(2)}) %collective-permute-start.1) | collective-permute-done | bytes 86048 | tf_op jit(solution)/shard_map/ppermute | solution.py:401
  31.2 0.0 collective-permute-done.2.refs_3_
  31.2 0.1 solve.1
  31.3 1.9 %collective-permute-start.3 = (f32[5,8,128]{2,1,0:T(8,128)S(1)}, f32[5,8,128]{2,1,0:T(8,128)S(1)}, u32[]{:S(2)}, u32[]{:S(2)}) collective-permute-start(f32[5,8,128]{2,1,0:T(8,128)S(1)} %get-tuple-element.18.refs_0_), channel_id=1, source_target_pairs={{0,1},{1,0},{2,3},{3,2},{4,5},{5,4},{6,7},{7,6},{8,9},{9,8},{10,11... | collective-permute-start | bytes 61448 | tf_op jit(solution)/shard_map/ppermute | solution.py:401
  33.2 1.4 %collective-permute-start.4 = (f32[5,8,128]{2,1,0:T(8,128)S(1)}, f32[5,8,128]{2,1,0:T(8,128)S(1)}, u32[]{:S(2)}, u32[]{:S(2)}) collective-permute-start(f32[5,8,128]{2,1,0:T(8,128)S(1)} %get-tuple-element.18.refs_0_), channel_id=1, source_target_pairs={{0,2},{1,3},{2,0},{3,1},{4,6},{5,7},{6,4},{7,5},{8,10},{9,11},{10,... | collective-permute-start | bytes 61448 | tf_op jit(solution)/shard_map/ppermute | solution.py:401
  34.6 1.2 %collective-permute-start.5 = (f32[5,8,128]{2,1,0:T(8,128)S(1)}, f32[5,8,128]{2,1,0:T(8,128)S(1)}, u32[]{:S(2)}, u32[]{:S(2)}) collective-permute-start(f32[5,8,128]{2,1,0:T(8,128)S(1)} %get-tuple-element.18.refs_0_), channel_id=1, source_target_pairs={{0,3},{1,2},{2,1},{3,0},{4,7},{5,6},{6,5},{7,4},{8,11},{9,10},{10,... | collective-permute-start | bytes 61448 | tf_op jit(solution)/shard_map/ppermute | solution.py:401
  35.8 0.0 all-to-all-done.part_ref
  35.8 0.0 copy-start.5
  35.8 2.9 %invert.1.inv_ref = f32[16,8,128]{2,1,0:T(8,128)S(1)} custom-call(s32[1]{0:T(128)} %bitcast.4.sky_ref, f32[8,16,8,128]{3,2,1,0:T(8,128)S(1)} %all-to-all-done.part_ref, f32[4,8,128]{2,1,0:T(8,128)S(1)} %get-tuple-element.17.ties_ref), custom_call_target="tpu_custom_call" | custom-call | tf_op jit(solution)/shard_map/invert/pallas_call | solution.py:439
  38.7 0.0 collective-permute-done.3.refs_1_
  38.7 0.0 collective-permute-done.4.refs_2_
  38.7 1.4 %collective-permute-done.5.refs_3_ = f32[5,8,128]{2,1,0:T(8,128)S(1)} collective-permute-done((f32[5,8,128]{2,1,0:T(8,128)S(1)}, f32[5,8,128]{2,1,0:T(8,128)S(1)}, u32[]{:S(2)}, u32[]{:S(2)}) %collective-permute-start.5) | collective-permute-done | bytes 20512 | tf_op jit(solution)/shard_map/ppermute | solution.py:401
  40.1 0.0 copy-done.1
  40.1 0.0 copy-done.5
  40.1 6.1 %right_sides.1 = (f32[5,4096]{1,0:T(8,128)}, f32[20,8,128]{2,1,0:T(8,128)S(1)}) custom-call(s32[1]{0:T(128)} %bitcast.me_ref, s32[64]{0:T(128)S(1)} %copy-done.8, s32[64,128]{1,0:T(8,128)S(1)} %bitcast.14, f32[64,128]{1,0:T(8,128)S(1)} %bitcast.12, f32[64,128]{1,0:T(8,128)S(1)} %bitcast.16, bf16[5,8192]{1,0:T(8,128)(2,1)S(1)} %copy-done.2, ...), custom_call_target="tpu_custom_call" | custom-call | tf_op jit(solution)/shard_map/right_sides/pallas_call | solution.py:446
  46.2 10.5 %all-gather = f32[160,8,128]{2,1,0:T(8,128)S(1)} all-gather(f32[20,8,128]{2,1,0:T(8,128)S(1)} %get-tuple-element.20), channel_id=2, replica_groups=mesh['sky'=8,'tm'=4] {'sky'}, dimensions={0}, use_global_device_ids=true | all-gather | bytes 737280 | tf_op jit(solution)/shard_map/all_gather | solution.py:461
  56.7 0.0 copy-start.10
  56.7 1.3 %collective-permute-start.6 = (f32[12,8,128]{2,1,0:T(8,128)S(1)}, f32[12,8,128]{2,1,0:T(8,128)S(1)}, u32[]{:S(2)}, u32[]{:S(2)}) collective-permute-start(f32[12,8,128]{2,1,0:T(8,128)S(1)} %get-tuple-element.22), channel_id=1, source_target_pairs={{1,0},{2,1},{3,2},{5,4},{6,5},{7,6},{9,8},{10,9},{11,10},{13,12},{... | collective-permute-start | bytes 147464 | tf_op jit(solution)/shard_map/ppermute | solution.py:467
  58.0 4.5 %collective-permute-start.7 = (f32[12,8,128]{2,1,0:T(8,128)S(1)}, f32[12,8,128]{2,1,0:T(8,128)S(1)}, u32[]{:S(2)}, u32[]{:S(2)}) collective-permute-start(f32[12,8,128]{2,1,0:T(8,128)S(1)} %get-tuple-element.23), channel_id=1, source_target_pairs={{0,1},{1,2},{2,3},{4,5},{5,6},{6,7},{8,9},{9,10},{10,11},{12,13},{... | collective-permute-start | bytes 147464 | tf_op jit(solution)/shard_map/ppermute | solution.py:468
  62.6 0.0 copy-done.10
  62.6 0.1 copy.13.attitude_ref
  62.7 0.2 turn.1.main_ref
  62.9 0.0 collective-permute-done.6.low_ref
  62.9 1.4 %collective-permute-done.7.high_ref = f32[12,8,128]{2,1,0:T(8,128)S(1)} collective-permute-done((f32[12,8,128]{2,1,0:T(8,128)S(1)}, f32[12,8,128]{2,1,0:T(8,128)S(1)}, u32[]{:S(2)}, u32[]{:S(2)}) %collective-permute-start.7) | collective-permute-done | bytes 49184 | tf_op jit(solution)/shard_map/ppermute | solution.py:468
  64.3 1.4 %sweeps.1 = f32[128,32]{1,0:T(8,128)S(1)} custom-call(f32[1024,128]{1,0:T(8,128)S(1)} %turn.1.main_ref, f32[4,8,128]{2,1,0:T(8,128)S(1)} %get-tuple-element.21.sides_ref, f32[12,8,128]{2,1,0:T(8,128)S(1)} %collective-permute-done.6.low_ref, f32[12,8,128]{2,1,0:T(8,128)S(1)} %collective-permute-done.7.high_ref, f32[4,8,128]{2,1,0:T(8,128)S(1)} %get-tuple-element.17.ties_ref, ...), custom_call_target="tpu_custom_call" | custom-call | tf_op jit(solution)/shard_map/sweeps/pallas_call | solution.py:477
  65.7 0.7 %copy.14 = f32[128,32]{0,1:T(8,128)} copy(f32[128,32]{1,0:T(8,128)S(1)} %sweeps.1) | data formatting | bytes 32768
  (1 shorter events, 0.0 us)
Async XLA Ops:
  0.6 0.7 copy-start.8
  1.3 1.0 %copy-start = (bf16[32,8192]{1,0:T(8,128)(2,1)S(1)}, bf16[32,8192]{1,0:T(8,128)(2,1)}, u32[]{:S(2)}) copy-start(bf16[32,8192]{1,0:T(8,128)(2,1)} %att_ref.3) | copy-start | bytes 1572868
  2.3 0.8 %copy-start.3 = (f32[8192]{0:T(1024)S(1)}, f32[8192]{0:T(1024)}, u32[]{:S(2)}) copy-start(f32[8192]{0:T(1024)} %param.10) | copy-start | bytes 98308
  6.2 5.3 %copy-start.2 = (bf16[5,8192]{1,0:T(8,128)(2,1)S(1)}, bf16[5,8192]{1,0:T(8,128)(2,1)}, u32[]{:S(2)}) copy-start(bf16[5,8192]{1,0:T(8,128)(2,1)} %sp_ref.3) | copy-start | bytes 245764
  6.2 5.3 %copy-start.4 = (f32[8192]{0:T(1024)S(1)}, f32[8192]{0:T(1024)}, u32[]{:S(2)}) copy-start(f32[8192]{0:T(1024)} %param.10) | copy-start | bytes 98308
  6.2 5.4 %copy-start.6 = (s32[8192]{0:T(1024)S(1)}, s32[8192]{0:T(1024)}, u32[]{:S(2)}) copy-start(s32[8192]{0:T(1024)} %param.13) | copy-start | bytes 98308
  6.2 5.4 %copy-start.7 = (f32[8192]{0:T(1024)S(1)}, f32[8192]{0:T(1024)}, u32[]{:S(2)}) copy-start(f32[8192]{0:T(1024)} %param.9) | copy-start | bytes 98308
  6.2 29.6 %all-to-all-start = ((f32[8,16,8,128]{3,2,1,0:T(8,128)}), f32[8,16,8,128]{3,2,1,0:T(8,128)S(1)}, u32[]{:S(2)}, u32[]{:S(2)}) async-start(f32[8,16,8,128]{3,2,1,0:T(8,128)} %bitcast.5), calls=%async_computation | async-start | bytes 1048576 | tf_op jit(solution)/shard_map/all_to_all | solution.py:424
  11.6 0.7 copy-start.9
  19.7 20.4 %copy-start.1 = (bf16[32,8192]{1,0:T(8,128)(2,1)S(1)}, bf16[32,8192]{1,0:T(8,128)(2,1)}, u32[]{:S(2)}) copy-start(bf16[32,8192]{1,0:T(8,128)(2,1)} %att_ref.3) | copy-start | bytes 1572868
  19.7 5.0 %collective-permute-start = (f32[21,8,128]{2,1,0:T(8,128)S(1)}, f32[21,8,128]{2,1,0:T(8,128)S(1)}, u32[]{:S(2)}, u32[]{:S(2)}) collective-permute-start(f32[21,8,128]{2,1,0:T(8,128)S(1)} %get-tuple-element.14), channel_id=1, source_target_pairs={{0,1},{1,0},{2,3},{3,2},{4,5},{5,4},{6,7},{7,6},{8,9},{9,8},{10,11... | collective-permute-start | bytes 258056 | tf_op jit(solution)/shard_map/ppermute | solution.py:401
  21.4 9.9 %collective-permute-start.1 = (f32[21,8,128]{2,1,0:T(8,128)S(1)}, f32[21,8,128]{2,1,0:T(8,128)S(1)}, u32[]{:S(2)}, u32[]{:S(2)}) collective-permute-start(f32[21,8,128]{2,1,0:T(8,128)S(1)} %get-tuple-element.15), channel_id=1, source_target_pairs={{0,2},{1,3},{2,0},{3,1},{4,6},{5,7},{6,4},{7,5},{8,10},{9,11},{10,... | collective-permute-start | bytes 258056 | tf_op jit(solution)/shard_map/ppermute | solution.py:401
  23.9 7.3 %collective-permute-start.2 = (f32[21,8,128]{2,1,0:T(8,128)S(1)}, f32[21,8,128]{2,1,0:T(8,128)S(1)}, u32[]{:S(2)}, u32[]{:S(2)}) collective-permute-start(f32[21,8,128]{2,1,0:T(8,128)S(1)} %get-tuple-element.16), channel_id=1, source_target_pairs={{0,3},{1,2},{2,1},{3,0},{4,7},{5,6},{6,5},{7,4},{8,11},{9,10},{10,... | collective-permute-start | bytes 258056 | tf_op jit(solution)/shard_map/ppermute | solution.py:401
  31.3 7.4 %collective-permute-start.3 = (f32[5,8,128]{2,1,0:T(8,128)S(1)}, f32[5,8,128]{2,1,0:T(8,128)S(1)}, u32[]{:S(2)}, u32[]{:S(2)}) collective-permute-start(f32[5,8,128]{2,1,0:T(8,128)S(1)} %get-tuple-element.18.refs_0_), channel_id=1, source_target_pairs={{0,1},{1,0},{2,3},{3,2},{4,5},{5,4},{6,7},{7,6},{8,9},{9,8},{10,11... | collective-permute-start | bytes 61448 | tf_op jit(solution)/shard_map/ppermute | solution.py:401
  33.2 5.5 %collective-permute-start.4 = (f32[5,8,128]{2,1,0:T(8,128)S(1)}, f32[5,8,128]{2,1,0:T(8,128)S(1)}, u32[]{:S(2)}, u32[]{:S(2)}) collective-permute-start(f32[5,8,128]{2,1,0:T(8,128)S(1)} %get-tuple-element.18.refs_0_), channel_id=1, source_target_pairs={{0,2},{1,3},{2,0},{3,1},{4,6},{5,7},{6,4},{7,5},{8,10},{9,11},{10,... | collective-permute-start | bytes 61448 | tf_op jit(solution)/shard_map/ppermute | solution.py:401
  34.6 5.6 %collective-permute-start.5 = (f32[5,8,128]{2,1,0:T(8,128)S(1)}, f32[5,8,128]{2,1,0:T(8,128)S(1)}, u32[]{:S(2)}, u32[]{:S(2)}) collective-permute-start(f32[5,8,128]{2,1,0:T(8,128)S(1)} %get-tuple-element.18.refs_0_), channel_id=1, source_target_pairs={{0,3},{1,2},{2,1},{3,0},{4,7},{5,6},{6,5},{7,4},{8,11},{9,10},{10,... | collective-permute-start | bytes 61448 | tf_op jit(solution)/shard_map/ppermute | solution.py:401
  35.8 4.4 %copy-start.5 = (f32[5,4096]{1,0:T(8,128)S(1)}, f32[5,4096]{1,0:T(8,128)}, u32[]{:S(2)}) copy-start(f32[5,4096]{1,0:T(8,128)} %sources_ref.1) | copy-start | bytes 245764
  56.7 5.9 %copy-start.10 = (f32[128,32]{0,1:T(8,128)S(1)}, f32[128,32]{0,1:T(8,128)}, u32[]{:S(2)}) copy-start(f32[128,32]{0,1:T(8,128)} %param.16) | copy-start | bytes 49156
  56.7 6.2 %collective-permute-start.6 = (f32[12,8,128]{2,1,0:T(8,128)S(1)}, f32[12,8,128]{2,1,0:T(8,128)S(1)}, u32[]{:S(2)}, u32[]{:S(2)}) collective-permute-start(f32[12,8,128]{2,1,0:T(8,128)S(1)} %get-tuple-element.22), channel_id=1, source_target_pairs={{1,0},{2,1},{3,2},{5,4},{6,5},{7,6},{9,8},{10,9},{11,10},{13,12},{... | collective-permute-start | bytes 147464 | tf_op jit(solution)/shard_map/ppermute | solution.py:467
  58.0 6.3 %collective-permute-start.7 = (f32[12,8,128]{2,1,0:T(8,128)S(1)}, f32[12,8,128]{2,1,0:T(8,128)S(1)}, u32[]{:S(2)}, u32[]{:S(2)}) collective-permute-start(f32[12,8,128]{2,1,0:T(8,128)S(1)} %get-tuple-element.23), channel_id=1, source_target_pairs={{0,1},{1,2},{2,3},{4,5},{5,6},{6,7},{8,9},{9,10},{10,11},{12,13},{... | collective-permute-start | bytes 147464 | tf_op jit(solution)/shard_map/ppermute | solution.py:468

commit v2 on v1

--- a/solution.py
+++ b/solution.py
@@ -1,4 +1,5 @@
 import functools
+import math
 
 import jax
 import jax.numpy as jnp
@@ -9,17 +10,21 @@
 
 TILE = 128
 ITERS = 8
+RIM = ITERS - 1
 DAMPING = 0.8
 PARAMS = 5
 PAIRS = tuple((i, j) for i in range(PARAMS) for j in range(i + 1))
 MOMENTS = len(PAIRS) + PARAMS
 LANES = 128
+CORES = 2
+HALF = LANES // CORES
 SPLITS = 3
 CHUNK = 1024
 ROWS = CHUNK // TILE
 F32 = jnp.float32
 BF16 = jnp.bfloat16
 NT = (((1,), (1,)), ((), ()))
+FLOPS_MICRO = 1e9
 VMEM_LIMIT = 48 * 1024 * 1024
 
 
@@ -31,15 +36,15 @@
     return pl.BlockSpec(memory_space=pltpu.SMEM)
 
 
-def call(kernel, out_shape, in_specs, scratch=(), flops=0, traffic=0):
+def call(kernel, out_shape, in_specs, scratch=(), micros=0.1, limit=VMEM_LIMIT):
     return pl.pallas_call(
         kernel,
         out_shape=out_shape,
         in_specs=in_specs,
         out_specs=jax.tree.map(lambda _: vmem(), out_shape),
         scratch_shapes=list(scratch),
-        compiler_params=pltpu.CompilerParams(vmem_limit_bytes=VMEM_LIMIT),
-        cost_estimate=pl.CostEstimate(flops=flops, bytes_accessed=traffic, transcendentals=0),
+        compiler_params=pltpu.CompilerParams(vmem_limit_bytes=limit),
+        cost_estimate=pl.CostEstimate(flops=int(micros * FLOPS_MICRO), bytes_accessed=0, transcendentals=0),
     )
 
 
@@ -66,12 +71,18 @@
     return (row & (half - 1)) // LANES
 
 
-def moments_kernel(hi_count, me_ref, src_ref, w_ref, r_ref, sp_ref, tie_ref, *refs):
-    peers = len(refs) - 4
-    outs, (lhs, rhs, acc, blocks) = refs[:peers], refs[peers:]
+def moments_kernel(hi_count, me_ref, src_hbm, w_hbm, r_hbm, sp_hbm, tie_hbm, *refs):
+    peers = len(refs) - 10
+    outs, (lhs, rhs, acc, blocks, src_ref, w_ref, r_ref, sp_ref, tie_ref, sems) = refs[:peers], refs[peers:]
+    pairs = ((src_hbm, src_ref), (w_hbm, w_ref), (r_hbm, r_ref), (sp_hbm, sp_ref), (tie_hbm, tie_ref))
+    copies = [pltpu.make_async_copy(a, b, sems.at[i]) for i, (a, b) in enumerate(pairs)]
+    for copy in copies:
+        copy.start()
     half = hi_count * LANES
     low_count = rhs.shape[0]
     acc[...] = jnp.zeros_like(acc)
+    for copy in copies:
+        copy.wait()
 
     def chunk(c, carry):
         base = pl.multiple_of(c * ROWS, ROWS)
@@ -119,8 +130,9 @@
         outs[k][...] = blocks[me ^ k]
 
 
-def normals_kernel(win_ref, w_ref, att_ref, out_ref):
+def normals_kernel(chips, win_ref, w_ref, att_ref, out_ref):
     windows = out_ref.shape[0]
+    own = windows // chips // CORES
     knots = att_ref.shape[0]
     copies = LANES // knots
     out_ref[...] = jnp.zeros_like(out_ref)
@@ -145,13 +157,15 @@
                 start = h * knots + 8 * g
                 value = jnp.where(lane < g * knots, value, normal[start : start + 8])
             slot = lax.rem(win_ref[2 * u + h], windows)
-            out_ref[slot] += value
+            block = slot // own
+            device = lax.rem(block, chips) * CORES + block // chips
+            out_ref[device * own + lax.rem(slot, own)] += value
         return carry
 
     lax.fori_loop(0, w_ref.shape[0] // 2, pair, 0, unroll=4)
 
 
-def solve_kernel(me_ref, *refs):
+def solve_kernel(me_ref, sky_ref, *refs):
     peers = len(refs) - 3
     blocks, (change_ref, ties_ref, rows_scr) = refs[:peers], refs[peers:]
     moments = blocks[0][0:MOMENTS]
@@ -184,7 +198,7 @@
             current = current - factor[k, i] * result[k]
         result[i] = current * inverse[i]
         change_ref[i] = result[i]
-    me = me_ref[0]
+    me, core = me_ref[0], lax.rem(sky_ref[0], CORES)
     for k in range(peers):
         rows_scr[me ^ k] = jnp.broadcast_to(blocks[k][MOMENTS, 0:1, :], (8, LANES))
     first, last = me == 0, me == peers - 1
@@ -194,19 +208,22 @@
     lane = iota((8, LANES), 1)
     own = jnp.where(jnp.logical_and(last, lane == LANES - 1), 0.0, own)
     own_left = jnp.where(lane == 0, pltpu.roll(before, 1, 1), pltpu.roll(own, 1, 1))
-    low, high = lane < ITERS - 1, lane > LANES - ITERS
-    rim_right = jnp.where(low, after, jnp.where(high, before, 0.0))
     after_left = jnp.where(lane == 0, pltpu.roll(own, 1, 1), pltpu.roll(after, 1, 1))
-    rim_left = jnp.where(low, after_left, jnp.where(high, pltpu.roll(before, 1, 1), 0.0))
-    ties_ref[0] = own_left
-    ties_ref[1] = own
-    ties_ref[2] = rim_left
-    ties_ref[3] = rim_right
+    before_left = pltpu.roll(before, 1, 1)
+    ties_ref[0] = own_left + own
+
+    def placed(before, own, after):
+        low = jnp.where(lane < HALF + RIM, own, jnp.where(lane >= LANES - RIM, before, 0.0))
+        high = jnp.where(lane < RIM, after, jnp.where(lane >= HALF - RIM, own, 0.0))
+        return jnp.where(core == 0, low, pltpu.roll(high, HALF, 1))
+
+    ties_ref[1] = placed(before_left, own_left, after_left)
+    ties_ref[2] = placed(before, own, after)
 
 
 def invert_kernel(sky_ref, part_ref, ties_ref, out_ref, flat, cells):
-    devices, own, eight, _ = part_ref.shape
-    knots = cells.shape[0] // 32 if False else 32
+    devices, own, _, _ = part_ref.shape
+    knots = math.isqrt(out_ref.shape[1] * LANES)
     total = part_ref[0]
     for s in range(1, devices):
         total = total + part_ref[s]
@@ -217,8 +234,9 @@
         turned = flat[pl.ds(r, LANES, stride=8), :].T
         for g in range(groups):
             cells[(8 * g + r) * knots : (8 * g + r + 1) * knots, :] = turned[g * knots : (g + 1) * knots]
-    shift = lax.rem(LANES - sky_ref[0] * own, LANES)
-    ties = pltpu.roll(ties_ref[0] + ties_ref[1], shift, 1)
+    core, chip = lax.rem(sky_ref[0], CORES), sky_ref[0] // CORES
+    shift = lax.rem(LANES - core * HALF - chip * own, LANES)
+    ties = pltpu.roll(ties_ref[0], shift, 1)
     diagonal = jnp.concatenate([ties] * (knots // 8), axis=0)
     inner = iota((knots, LANES), 0)
     blocks = []
@@ -249,7 +267,7 @@
     out_ref[...] = flat[0 : own * 8, :].reshape(own, 8, LANES)
 
 
-def rhs_kernel(hi_count, me_ref, win_ref, src_ref, w_ref, r_ref, sp_ref, att_ref, sources_ref, inv_ref, *refs):
+def rhs_kernel(hi_count, me_ref, win_ref, src_ref, w_ref, r_ref, sp_ref, att_ref, sources_ref, *refs):
     peers = len(refs) - 7
     blocks = refs[:peers]
     new_ref, out_ref, changes, table, rhs, chosen, weighted = refs[peers:]
@@ -257,7 +275,6 @@
     low_count = rhs.shape[0]
     windows = LANES
     knots = att_ref.shape[0]
-    own = inv_ref.shape[0]
     me = me_ref[0]
     for k in range(peers):
         changes[me ^ k] = blocks[k][...]
@@ -302,80 +319,93 @@
         return total + lax.dot_general(att, weighted[...], NT, preferred_element_type=F32)
 
     total = lax.fori_loop(0, src_ref.shape[0] // ROWS, chunk, jnp.zeros((knots, windows), F32))
+    out_ref[...] = total
+
+
+def send_kernel(sky_ref, inv_ref, mine_ref, theirs_ref, out_ref):
+    own = inv_ref.shape[0]
+    core = lax.rem(sky_ref[0], CORES)
+    total = mine_ref[...] + theirs_ref[...]
+    total = jnp.where(core == 0, total, pltpu.roll(total, HALF, 1))
+    packed = narrow(total)
     out_ref[0:own] = inv_ref[...]
-    out_ref[own : own + knots // 8] = total.reshape(knots // 8, 8, LANES)
-
-
-def rim_kernel(all_ref, low_ref, high_ref, main_ref):
-    devices, blocks, _, _ = all_ref.shape
-    own = blocks - 4
-    sides = all_ref[0, own:blocks]
-    for s in range(1, devices):
-        sides = sides + all_ref[s, own:blocks]
-    main_ref[...] = sides
-    low_ref[8:12] = sides
-    high_ref[8:12] = sides
-    for w in range(8):
-        low_ref[w] = all_ref[w // own, w % own]
-        far = devices * own - 8 + w
-        high_ref[w] = all_ref[far // own, far % own]
-
-
-def turn_kernel(all_ref, main_ref, flat):
-    devices, blocks, _, _ = all_ref.shape
-    own = blocks - 4
-    knots = 32
+    out_ref[own:] = packed.reshape(packed.shape[0] // 8, 8, LANES)
+
+
+def narrow(x):
+    rows = x.shape[0] // 2
+    low = iota((rows, LANES), 1) < HALF
+    return jnp.where(low, x[:rows], pltpu.roll(x[rows:], HALF, 1))
+
+
+def widen(x):
+    return jnp.concatenate([x, pltpu.roll(x, HALF, 1)], axis=0)
+
+
+def rim_kernel(sky_ref, *refs):
+    chips = len(refs) - 3
+    parts, (inner_ref, outer_ref, main_ref) = refs[:chips], refs[chips:]
+    own = parts[0].shape[0] - (main_ref.shape[0] - HALF)
+    core, chip = lax.rem(sky_ref[0], CORES), sky_ref[0] // CORES
+    sides = parts[0][own:]
+    for part in parts[1:]:
+        sides = sides + part[own:]
+    for k in range(chips):
+        main_ref[pl.ds((chip ^ k) * own, own)] = parts[k][0:own]
+    main_ref[HALF:] = sides
+    inner_ref[0:8] = main_ref[pl.ds((1 - core) * (HALF - 8), 8)]
+    outer_ref[0:8] = main_ref[pl.ds(core * (HALF - 8), 8)]
+    inner_ref[8:] = sides
+    outer_ref[8:] = sides
+
+
+def sweeps_kernel(sky_ref, main_ref, inner_ref, outer_ref, ties_ref, out_ref, flat, cells, vector):
+    knots = out_ref.shape[0]
     groups = LANES // knots
-    for s in range(devices):
-        flat[s * own * 8 : (s + 1) * own * 8, :] = all_ref[s, 0:own].reshape(own * 8, LANES)
+    core = lax.rem(sky_ref[0], CORES)
+    low = jnp.where(core == 0, outer_ref[...], inner_ref[...])
+    high = jnp.where(core == 0, inner_ref[...], outer_ref[...])
+    flat[...] = jnp.zeros_like(flat)
+    flat[0 : HALF * 8, :] = main_ref[0:HALF].reshape(HALF * 8, LANES)
+    flat[HALF * 8 : HALF * 8 + 64, :] = high[0:8].reshape(64, LANES)
+    flat[LANES * 8 - 64 : LANES * 8, :] = low[0:8].reshape(64, LANES)
     for r in range(8):
         turned = flat[pl.ds(r, LANES, stride=8), :].T
         for g in range(groups):
-            main_ref[(8 * g + r) * knots : (8 * g + r + 1) * knots, :] = turned[g * knots : (g + 1) * knots]
-
-
-def sweeps_kernel(main_ref, sides_ref, low_ref, high_ref, ties_ref, attitude_ref, out_ref, flat, rim, vector):
-    knots = attitude_ref.shape[1]
-    groups = LANES // knots
-    flat[...] = jnp.zeros_like(flat)
-    flat[0:64, :] = low_ref[0:8].reshape(64, LANES)
-    flat[960:1024, :] = high_ref[0:8].reshape(64, LANES)
-    for r in range(8):
-        turned = flat[pl.ds(r, LANES, stride=8), :].T
-        for g in range(groups):
-            rim[(8 * g + r) * knots : (8 * g + r + 1) * knots, :] = turned[g * knots : (g + 1) * knots]
+            cells[(8 * g + r) * knots : (8 * g + r + 1) * knots, :] = turned[g * knots : (g + 1) * knots]
+
+    def wide(x):
+        return widen(x.reshape(knots // 2, LANES))
+
     lane = iota((knots, LANES), 1)
-    rim_sides = jnp.where(
-        lane < ITERS - 1,
-        low_ref[8:12].reshape(knots, LANES),
-        jnp.where(lane > LANES - ITERS, high_ref[8:12].reshape(knots, LANES), 0.0),
-    )
-    sides = jnp.concatenate([sides_ref[...].reshape(knots, LANES), rim_sides], axis=1)
-
-    def wide(a, b):
-        return DAMPING * jnp.concatenate([jnp.concatenate([a, b], axis=1)] * (knots // 8), axis=0)
-
-    left = wide(ties_ref[0], ties_ref[2])
-    right = wide(ties_ref[1], ties_ref[3])
+    sides = jnp.where(lane < HALF, wide(main_ref[HALF:]), 0.0)
+    sides = jnp.where(jnp.logical_and(lane >= HALF, lane < HALF + RIM), pltpu.roll(wide(high[8:]), HALF, 1), sides)
+    sides = jnp.where(lane >= LANES - RIM, pltpu.roll(wide(low[8:]), HALF, 1), sides)
+    left = DAMPING * jnp.concatenate([ties_ref[1]] * (knots // 8), axis=0)
+    right = DAMPING * jnp.concatenate([ties_ref[2]] * (knots // 8), axis=0)
 
     def applied(x):
         vector[...] = x
-        main = jnp.zeros((knots, LANES), F32)
-        side = jnp.zeros((knots, LANES), F32)
+        total = [jnp.zeros((knots, LANES), F32) for _ in range(4)]
         for k in range(knots):
-            row = vector[k : k + 1, :]
-            main = main + main_ref[k * knots : (k + 1) * knots, :] * row[:, :LANES]
-            side = side + rim[k * knots : (k + 1) * knots, :] * row[:, LANES:]
-        return jnp.concatenate([main, side], axis=1)
+            total[k % 4] += cells[k * knots : (k + 1) * knots, :] * vector[k : k + 1, :]
+        return (total[0] + total[1]) + (total[2] + total[3])
 
     first = applied(DAMPING * sides)
 
     def sweep(_, change):
-        ends = left * pltpu.roll(change, 1, 1) + right * pltpu.roll(change, 2 * LANES - 1, 1)
+        ends = left * pltpu.roll(change, 1, 1) + right * pltpu.roll(change, LANES - 1, 1)
         return (1.0 - DAMPING) * change + first + applied(ends)
 
-    change = lax.fori_loop(0, ITERS - 1, sweep, first)
-    out_ref[...] = attitude_ref[...] + change[:, :LANES].T
+    out_ref[...] = lax.fori_loop(0, ITERS - 1, sweep, first)
+
+
+def finish_kernel(sky_ref, mine_ref, theirs_ref, attitude_ref, out_ref):
+    core = lax.rem(sky_ref[0], CORES)
+    lower = jnp.where(core == 0, mine_ref[...], theirs_ref[...])
+    upper = jnp.where(core == 0, theirs_ref[...], mine_ref[...])
+    lane = iota(lower.shape, 1)
+    out_ref[...] = attitude_ref[...] + jnp.where(lane < HALF, lower, pltpu.roll(upper, HALF, 1))
 
 
 def on_device(
@@ -396,60 +426,79 @@
     w = weights.reshape(tiles, TILE)
     r = residuals.reshape(tiles, TILE)
 
-    def exchanged(blocks):
-        return [blocks[0]] + [
-            lax.ppermute(blocks[k], "tm", [(i, i ^ k) for i in range(peers)]) for k in range(1, peers)
-        ]
+    chips = devices // CORES
+    cell_rows = knots * knots // LANES
+
+    def swapped(blocks):
+        out = [blocks[0]] + [None] * (peers - 1)
+        for k in sorted(range(1, peers), key=lambda k: (k < peers // 2, k)):
+            out[k] = lax.ppermute(blocks[k], "tm", [(i, i ^ k) for i in range(peers)])
+        return out
+
+    def other_core(x):
+        return lax.ppermute(x, "sky", [(i, i ^ 1) for i in range(devices)])
 
     block = jax.ShapeDtypeStruct((MOMENTS + 1, rows, LANES), F32)
     with jax.named_scope("moments"):
         blocks = call(
             functools.partial(moments_kernel, hi_count),
             [block] * peers,
-            [smem()] + [vmem()] * 5,
+            [smem()] + [pl.BlockSpec(memory_space=pl.ANY)] * 5,
             [
                 pltpu.VMEM((SPLITS * MOMENTS * hi_count, CHUNK), BF16),
                 pltpu.VMEM((low_count, CHUNK), BF16),
                 pltpu.VMEM((SPLITS * MOMENTS * hi_count, low_count), F32),
                 pltpu.VMEM((peers, MOMENTS + 1, rows, LANES), F32),
+                pltpu.VMEM(src.shape, jnp.int32),
+                pltpu.VMEM(w.shape, F32),
+                pltpu.VMEM(r.shape, F32),
+                pltpu.VMEM(source_partials.shape, BF16),
+                pltpu.VMEM((1, windows), F32),
+                pltpu.SemaphoreType.DMA((5,)),
             ],
+            micros=7.5,
+            limit=60 * 1024 * 1024,
         )(me, src, w, r, source_partials, coupling.reshape(1, windows))
-    blocks = exchanged(blocks)
+    blocks, tile_window = lax.optimization_barrier((blocks, tile_window))
+    blocks = swapped(blocks)
     with jax.named_scope("normals"):
         normals = call(
-            normals_kernel,
-            jax.ShapeDtypeStruct((windows, knots * knots // LANES, LANES), F32),
+            functools.partial(normals_kernel, chips),
+            jax.ShapeDtypeStruct((windows, cell_rows, LANES), F32),
             [smem(), vmem(), vmem()],
+            micros=3,
         )(tile_window, w, attitude_partials)
-    parts = lax.all_to_all(
-        normals.reshape(devices, own, knots * knots // LANES, LANES), "sky", 0, 0, tiled=True
-    )
+    parts = lax.all_to_all(normals.reshape(devices, own, cell_rows, LANES), "sky", 0, 0, tiled=True)
+    _, blocks = lax.optimization_barrier((normals, blocks))
     with jax.named_scope("solve"):
         change, ties = call(
             solve_kernel,
             [
                 jax.ShapeDtypeStruct((PARAMS, rows, LANES), F32),
-                jax.ShapeDtypeStruct((4, 8, LANES), F32),
+                jax.ShapeDtypeStruct((3, 8, LANES), F32),
             ],
-            [smem()] + [vmem()] * peers,
+            [smem(), smem()] + [vmem()] * peers,
             [pltpu.VMEM((peers, 8, LANES), F32)],
-        )(me, *blocks)
-    changes = exchanged([change] * peers)
+            micros=30,
+        )(me, sky, *blocks)
+    changes = swapped([change] * peers)
     with jax.named_scope("invert"):
         inverse = call(
             invert_kernel,
-            jax.ShapeDtypeStruct((own, knots * knots // LANES, LANES), F32),
+            jax.ShapeDtypeStruct((own, cell_rows, LANES), F32),
             [smem(), vmem(), vmem()],
-            [pltpu.VMEM((8 * LANES, LANES), F32), pltpu.VMEM((knots * knots, LANES), F32)],
+            [pltpu.VMEM((cell_rows * LANES, LANES), F32), pltpu.VMEM((knots * knots, LANES), F32)],
+            micros=3,
         )(sky, parts, ties)
+    inverse, changes = lax.optimization_barrier((inverse, changes))
     with jax.named_scope("right_sides"):
         new_sources, part = call(
             functools.partial(rhs_kernel, hi_count),
             [
                 jax.ShapeDtypeStruct(sources.shape, F32),
-                jax.ShapeDtypeStruct((own + knots // 8, 8, LANES), F32),
+                jax.ShapeDtypeStruct((knots, windows), F32),
             ],
-            [smem(), smem()] + [vmem()] * (7 + peers),
+            [smem(), smem()] + [vmem()] * (6 + peers),
             [
                 pltpu.VMEM((peers, PARAMS, rows, LANES), F32),
                 pltpu.VMEM((SPLITS * PARAMS * hi_count, low_count), F32),
@@ -457,34 +506,48 @@
                 pltpu.VMEM((SPLITS * PARAMS * hi_count, CHUNK), F32),
                 pltpu.VMEM((windows, CHUNK), BF16),
             ],
-        )(me, tile_window, src, w, r, source_partials, attitude_partials, sources, inverse, *changes)
-    gathered = lax.all_gather(part, "sky", axis=0, tiled=False)
+            micros=6,
+        )(me, tile_window, src, w, r, source_partials, attitude_partials, sources, *changes)
+    with jax.named_scope("send"):
+        sides = knots // 2 // 8
+        sent = call(
+            send_kernel,
+            jax.ShapeDtypeStruct((own + sides, 8, LANES), F32),
+            [smem()] + [vmem()] * 3,
+        )(sky, inverse, part, other_core(part))
+    got = [sent] + [
+        lax.ppermute(sent, "sky", [(i, i ^ (CORES * k)) for i in range(devices)]) for k in range(1, chips)
+    ]
     with jax.named_scope("rims"):
-        rim = jax.ShapeDtypeStruct((12, 8, LANES), F32)
-        low, high, sides = call(
-            rim_kernel, [rim, rim, jax.ShapeDtypeStruct((4, 8, LANES), F32)], [vmem()]
-        )(gathered)
-    after = lax.ppermute(low, "tm", [(i, i - 1) for i in range(1, peers)])
-    before = lax.ppermute(high, "tm", [(i, i + 1) for i in range(peers - 1)])
-    with jax.named_scope("turn"):
-        main = call(
-            turn_kernel,
-            jax.ShapeDtypeStruct((knots * knots, LANES), F32),
-            [vmem()],
-            [pltpu.VMEM((8 * LANES, LANES), F32)],
-        )(gathered)
+        rim = jax.ShapeDtypeStruct((8 + sides, 8, LANES), F32)
+        inner, outer, main = call(
+            rim_kernel,
+            [rim, rim, jax.ShapeDtypeStruct((HALF + sides, 8, LANES), F32)],
+            [smem()] + [vmem()] * chips,
+        )(sky, *got)
+    upper = [(chip * CORES + 1) * peers + t for chip in range(chips) for t in range(peers - 1)]
+    lower = [chip * CORES * peers + t + 1 for chip in range(chips) for t in range(peers - 1)]
+    outer = lax.ppermute(outer, ("sky", "tm"), list(zip(upper + lower, lower + upper)))
+    inner = other_core(inner)
     with jax.named_scope("sweeps"):
+        step = call(
+            sweeps_kernel,
+            jax.ShapeDtypeStruct((knots, LANES), F32),
+            [smem()] + [vmem()] * 4,
+            [
+                pltpu.VMEM((cell_rows * LANES, LANES), F32),
+                pltpu.VMEM((knots * knots, LANES), F32),
+                pltpu.VMEM((knots, LANES), F32),
+            ],
+            micros=1,
+        )(sky, main, inner, outer, ties)
+    with jax.named_scope("finish"):
         new_attitude = call(
-            sweeps_kernel,
-            jax.ShapeDtypeStruct(attitude.shape, F32),
-            [vmem()] * 6,
-            [
-                pltpu.VMEM((8 * LANES, LANES), F32),
-                pltpu.VMEM((knots * knots, LANES), F32),
-                pltpu.VMEM((knots, 2 * LANES), F32),
-            ],
-        )(main, sides, after, before, ties, attitude)
-    return new_sources, new_attitude
+            finish_kernel,
+            jax.ShapeDtypeStruct((knots, windows), F32),
+            [smem()] + [vmem()] * 3,
+        )(sky, step, other_core(step), attitude.T)
+    return new_sources, new_attitude.T
 
 
 def solution(mesh):

time: 66.8 us -> 58.1 us (0.87)
  blocking collectives: 10.5 us -> 0 us
  local copies, waits for them, and re-layouts: 3.86 us -> 0.04 us
  starting transfers between devices: 20.1 us -> 23.1 us
  Pallas kernels: 21.3 us -> 23.4 us
  waiting for transfers between devices: 9.88 us -> 10.6 us
    all_gather x1 -> x0, blocking collectives: 10.5 us -> none  [on_device(): gathered = lax.all_gather(part, 'sky', axis=0, tiled=False)]
    all_to_all x1, waiting for transfers between devices: 0.01 us -> 5.12 us  [on_device(): lax.all_to_all(normals.reshape(devices, own, cell_rows, LANES), 'sky', 0,...]
    ppermute x8 -> x13, waiting for transfers between devices: 9.87 us -> 5.46 us  [the longest x3 2.89 us: on_device(): lax.ppermute(sent, 'sky', [(i, i ^ CORES * k) for i in range(devices)])]
    ppermute x8 -> x13, starting transfers between devices: 14.7 us -> 19 us  [the longest x6 10.1 us: swapped(): out[k] = lax.ppermute(blocks[k], 'tm', [(i, i ^ k) for i in range(peers)])]
    unnamed x24 -> x18, local copies, waits for them, and re-layouts: 3.86 us -> 0.04 us
    pallas_call x1, Pallas kernels: 7.49 us -> 9.18 us  [on_device(): call(functools.partial(moments_kernel, hi_count), [block] * peers, [smem(...]
    all_to_all x1, starting transfers between devices: 5.32 us -> 4.06 us  [on_device(): lax.all_to_all(normals.reshape(devices, own, cell_rows, LANES), 'sky', 0,...]
    pallas_call x5 -> x6, Pallas kernels: 7.68 us -> 7.98 us  [the longest x1 3.14 us: on_device(): call(functools.partial(normals_kernel, chips), jax.ShapeDtypeStruct((wind...]
  transfers between devices with their start and end apart: 9 -> 14, of which waited for: 4 -> 7; matrix products, arithmetic and copies ran while one was open for 0% -> 0% of each run, Pallas kernels for 16% -> 11%
where the time goes in v2:
time: 58.1 us; the launch traced here: 57.8 us
  Pallas kernels  23.4 us (40%)
  starting transfers between devices  23.1 us (40%)
  waiting for transfers between devices  10.6 us (18%)
  between operations  0.81 us (1%)
    ppermute x6, starting transfers between devices, swapped(): out[k] = lax.ppermute(blocks[k], 'tm', [(i, i ^ k) for i in range(peers)])  10.1 us
    pallas_call x1, Pallas kernels, on_device(): call(functools.partial(moments_kernel, hi_count), [block] * peers, [smem(...  9.18 us
    pallas_call x1, Pallas kernels, on_device(): call(functools.partial(rhs_kernel, hi_count), [jax.ShapeDtypeStruct(sourc...  6.04 us
    all_to_all x1, waiting for transfers between devices, on_device(): lax.all_to_all(normals.reshape(devices, own, cell_rows, LANES), 'sky', 0,...  5.12 us
    ppermute x3, starting transfers between devices, other_core(): return lax.ppermute(x, 'sky', [(i, i ^ 1) for i in range(devices)])  4.73 us
    all_to_all x1, starting transfers between devices, on_device(): lax.all_to_all(normals.reshape(devices, own, cell_rows, LANES), 'sky', 0,...  4.06 us
    ppermute x3, starting transfers between devices, on_device(): lax.ppermute(sent, 'sky', [(i, i ^ CORES * k) for i in range(devices)])  3.49 us
    pallas_call x1, Pallas kernels, on_device(): call(functools.partial(normals_kernel, chips), jax.ShapeDtypeStruct((wind...  3.14 us
  transfers between devices with their start and end apart: 14, of which 7 were waited for; matrix products, arithmetic and copies ran while one was open for 0% of the time, Pallas kernels for 11%

profile of v2, /device:TPU:0, one launch (start us, length us, event | category | flops | bytes accessed | tf_op | source)
XLA Modules:
  0.0 57.8 jit_solution(13254020248609816286)
XLA Ops:
  0.6 0.0 copy-start
  0.6 0.0 copy-start.4
  0.7 9.2 %moments.1 = (f32[21,8,128]{2,1,0:T(8,128)}, f32[21,8,128]{2,1,0:T(8,128)}, f32[21,8,128]{2,1,0:T(8,128)}, f32[21,8,128]{2,1,0:T(8,128)}) custom-call(s32[1]{0:T(128)} %bitcast.me_ref, s32[64,128]{1,0:T(8,128)} %bitcast.9, f32[64,128]{1,0:T(8,128)} %bitcast.11, f32[64,128]{1,0:T(8,128)} %bitcast.14, bf16[5,8192]{1,0:T(8,128)(2,1)} %sp_ref.1, f32[1,128]{1,0:T(1,128)} %bitcast.17), custom_call_target="tpu_custom_call" | custom-call | flops 7500000256 | tf_op jit(solution)/shard_map/moments/pallas_call | solution.py:443
  9.8 0.0 copy-start.7
  9.9 3.1 %collective-permute-start = (f32[21,8,128]{2,1,0:T(8,128)}, f32[21,8,128]{2,1,0:T(8,128)S(1)}, u32[]{:S(2)}, u32[]{:S(2)}) collective-permute-start(f32[21,8,128]{2,1,0:T(8,128)} %get-tuple-element.33), channel_id=1, source_target_pairs={{0,1},{1,0},{2,3},{3,2},{4,5},{5,4},{6,7},{7,6},{8,9},{9,8},{10,11... | collective-permute-start | bytes 258056 | tf_op jit(solution)/shard_map/ppermute | solution.py:435
  12.9 2.6 %collective-permute-start.1 = (f32[21,8,128]{2,1,0:T(8,128)}, f32[21,8,128]{2,1,0:T(8,128)S(1)}, u32[]{:S(2)}, u32[]{:S(2)}) collective-permute-start(f32[21,8,128]{2,1,0:T(8,128)} %get-tuple-element.34), channel_id=1, source_target_pairs={{0,2},{1,3},{2,0},{3,1},{4,6},{5,7},{6,4},{7,5},{8,10},{9,11},{10,... | collective-permute-start | bytes 258056 | tf_op jit(solution)/shard_map/ppermute | solution.py:435
  15.5 0.0 collective-permute-start.2
  15.5 0.0 copy-done
  15.5 0.0 copy-done.4
  15.5 0.0 copy-done.7
  15.6 3.1 %normals.1 = f32[128,8,128]{2,1,0:T(8,128)} custom-call(s32[64]{0:T(128)S(1)} %copy-done.7, f32[64,128]{1,0:T(8,128)S(1)} %bitcast.12, bf16[32,8192]{1,0:T(8,128)(2,1)S(1)} %copy-done), custom_call_target="tpu_custom_call" | custom-call | flops 3000000000 | tf_op jit(solution)/shard_map/normals/pallas_call | solution.py:465
  18.7 0.0 copy-start.8
  18.7 4.1 %all-to-all-start = ((f32[8,16,8,128]{3,2,1,0:T(8,128)}), f32[8,16,8,128]{3,2,1,0:T(8,128)S(1)}, u32[]{:S(2)}, u32[]{:S(2)}) async-start(f32[8,16,8,128]{3,2,1,0:T(8,128)} %bitcast.6), calls=%async_computation | async-start | bytes 1048576 | tf_op jit(solution)/shard_map/all_to_all | solution.py:471
  22.8 0.0 collective-permute-done.refs_1_
  22.8 0.0 collective-permute-done.1.refs_2_
  22.8 0.0 collective-permute-done.2.refs_3_
  22.8 0.0 copy-done.8
  22.8 0.2 solve.1
  23.0 3.6 %collective-permute-start.5 = (f32[5,8,128]{2,1,0:T(8,128)S(1)}, f32[5,8,128]{2,1,0:T(8,128)S(1)}, u32[]{:S(2)}, u32[]{:S(2)}) collective-permute-start(f32[5,8,128]{2,1,0:T(8,128)S(1)} %get-tuple-element.42.refs_0_), channel_id=1, source_target_pairs={{0,3},{1,2},{2,1},{3,0},{4,7},{5,6},{6,5},{7,4},{8,11},{9,10},{10,... | collective-permute-start | bytes 61448 | tf_op jit(solution)/shard_map/ppermute | solution.py:435
  26.6 0.0 collective-permute-start.4
  26.6 0.8 %collective-permute-start.3 = (f32[5,8,128]{2,1,0:T(8,128)S(1)}, f32[5,8,128]{2,1,0:T(8,128)S(1)}, u32[]{:S(2)}, u32[]{:S(2)}) collective-permute-start(f32[5,8,128]{2,1,0:T(8,128)S(1)} %get-tuple-element.42.refs_0_), channel_id=1, source_target_pairs={{0,1},{1,0},{2,3},{3,2},{4,5},{5,4},{6,7},{7,6},{8,9},{9,8},{10,11... | collective-permute-start | bytes 61448 | tf_op jit(solution)/shard_map/ppermute | solution.py:435
  27.4 5.1 %all-to-all-done.part_ref = f32[8,16,8,128]{3,2,1,0:T(8,128)S(1)} async-done(((f32[8,16,8,128]{3,2,1,0:T(8,128)}), f32[8,16,8,128]{3,2,1,0:T(8,128)S(1)}, u32[]{:S(2)}, u32[]{:S(2)}) %all-to-all-start) | async-done | bytes 524320 | tf_op jit(solution)/shard_map/all_to_all | solution.py:471
  32.5 0.0 copy-start.1
  32.5 0.0 copy-start.2
  32.5 0.0 copy-start.3
  32.5 0.0 copy-start.5
  32.5 2.9 %invert.1.inv_ref = f32[16,8,128]{2,1,0:T(8,128)S(1)} custom-call(s32[1]{0:T(128)} %bitcast.5.sky_ref, f32[8,16,8,128]{3,2,1,0:T(8,128)S(1)} %all-to-all-done.part_ref, f32[3,8,128]{2,1,0:T(8,128)S(1)} %get-tuple-element.40.ties_ref), custom_call_target="tpu_custom_call" | custom-call | flops 3000000000 | tf_op jit(solution)/shard_map/invert/pallas_call | solution.py:486
  35.4 0.0 collective-permute-done.5.refs_3_
  35.4 0.0 collective-permute-done.4.refs_2_
  35.5 0.0 collective-permute-done.3.refs_1_
  35.5 0.0 copy-done.1
  35.5 0.0 copy-done.2
  35.5 0.0 copy-done.3
  35.5 0.0 copy-done.5
  35.5 6.0 %right_sides.1 = (f32[5,4096]{1,0:T(8,128)}, f32[32,128]{1,0:T(8,128)S(1)}) custom-call(s32[1]{0:T(128)} %bitcast.me_ref, s32[64]{0:T(128)S(1)} %copy-done.7, s32[64,128]{1,0:T(8,128)S(1)} %bitcast.10, f32[64,128]{1,0:T(8,128)S(1)} %bitcast.13, f32[64,128]{1,0:T(8,128)S(1)} %bitcast.15, bf16[5,8192]{1,0:T(8,128)(2,1)S(1)} %copy-done.1, ...), custom_call_target="tpu_custom_call" | custom-call | flops 6000000000 | tf_op jit(solution)/shard_map/right_sides/pallas_call | solution.py:495
  41.5 0.0 collective-permute-start.6
  41.5 1.2 %collective-permute-done.6.theirs_ref = f32[32,128]{1,0:T(8,128)S(1)} collective-permute-done((f32[32,128]{1,0:T(8,128)S(1)}, f32[32,128]{1,0:T(8,128)S(1)}, u32[]{:S(2)}, u32[]{:S(2)}) %collective-permute-start.6) | collective-permute-done | bytes 16416 | tf_op jit(solution)/shard_map/send/ppermute | solution.py:439
  42.7 0.1 send.1.refs_0_
  42.9 0.6 collective-permute-start.9
  43.4 1.5 %collective-permute-start.8 = (f32[18,8,128]{2,1,0:T(8,128)S(1)}, f32[18,8,128]{2,1,0:T(8,128)S(1)}, u32[]{:S(2)}, u32[]{:S(2)}) collective-permute-start(f32[18,8,128]{2,1,0:T(8,128)S(1)} %send.1.refs_0_), channel_id=1, source_target_pairs={{0,16},{4,20},{8,24},{12,28},{16,0},{20,4},{24,8},{28,12},{1,17},{... | collective-permute-start | bytes 221192 | tf_op jit(solution)/shard_map/ppermute | solution.py:519
  44.9 1.5 %collective-permute-start.7 = (f32[18,8,128]{2,1,0:T(8,128)S(1)}, f32[18,8,128]{2,1,0:T(8,128)S(1)}, u32[]{:S(2)}, u32[]{:S(2)}) collective-permute-start(f32[18,8,128]{2,1,0:T(8,128)S(1)} %send.1.refs_0_), channel_id=1, source_target_pairs={{0,8},{4,12},{8,0},{12,4},{16,24},{20,28},{24,16},{28,20},{1,9},{5... | collective-permute-start | bytes 221192 | tf_op jit(solution)/shard_map/ppermute | solution.py:519
  46.4 2.5 %collective-permute-done.9.refs_3_ = f32[18,8,128]{2,1,0:T(8,128)S(1)} collective-permute-done((f32[18,8,128]{2,1,0:T(8,128)S(1)}, f32[18,8,128]{2,1,0:T(8,128)S(1)}, u32[]{:S(2)}, u32[]{:S(2)}) %collective-permute-start.9) | collective-permute-done | bytes 73760 | tf_op jit(solution)/shard_map/ppermute | solution.py:519
  48.9 0.2 collective-permute-done.8.refs_2_
  49.1 0.2 collective-permute-done.7.refs_1_
  49.3 0.1 collective-permute-start.10
  49.4 0.7 %collective-permute-start.11 = (f32[10,8,128]{2,1,0:T(8,128)S(1)}, f32[10,8,128]{2,1,0:T(8,128)S(1)}, u32[]{:S(2)}, u32[]{:S(2)}) collective-permute-start(f32[10,8,128]{2,1,0:T(8,128)S(1)} %get-tuple-element.51), channel_id=1, source_target_pairs={{4,1},{5,2},{6,3},{12,9},{13,10},{14,11},{20,17},{21,18},{22,19},{... | collective-permute-start | bytes 122888 | tf_op jit(solution)/shard_map/ppermute | solution.py:530
  50.0 0.5 collective-permute-done.10.inner_ref
  50.6 0.0 collective-permute-done.11.outer_ref
  50.6 0.0 copy-start.6
  50.6 1.1 %sweeps.1.mine_ref = f32[32,128]{1,0:T(8,128)S(1)} custom-call(s32[1]{0:T(128)} %bitcast.5.sky_ref, f32[66,8,128]{2,1,0:T(8,128)S(1)} %get-tuple-element.49.main_ref, f32[10,8,128]{2,1,0:T(8,128)S(1)} %collective-permute-done.10.inner_ref, f32[10,8,128]{2,1,0:T(8,128)S(1)} %collective-permute-done.11.outer_ref, f32[3,8,128]{2,1,0:T(8,128)S(1)} %get-tuple-element.40.ties_ref), custom_call_target="tpu_custom_call" | custom-call | flops 1000000000 | tf_op jit(solution)/shard_map/sweeps/pallas_call | solution.py:533
  51.7 4.7 %collective-permute-start.12 = (f32[32,128]{1,0:T(8,128)S(1)}, f32[32,128]{1,0:T(8,128)S(1)}, u32[]{:S(2)}, u32[]{:S(2)}) collective-permute-start(f32[32,128]{1,0:T(8,128)S(1)} %sweeps.1.mine_ref), channel_id=1, source_target_pairs={{0,4},{4,0},{8,12},{12,8},{16,20},{20,16},{24,28},{28,24},{1,5},{5... | collective-permute-start | bytes 49160 | tf_op jit(solution)/shard_map/finish/ppermute | solution.py:439
  56.3 0.8 %collective-permute-done.12.theirs_ref = f32[32,128]{1,0:T(8,128)S(1)} collective-permute-done((f32[32,128]{1,0:T(8,128)S(1)}, f32[32,128]{1,0:T(8,128)S(1)}, u32[]{:S(2)}, u32[]{:S(2)}) %collective-permute-start.12) | collective-permute-done | bytes 16416 | tf_op jit(solution)/shard_map/finish/ppermute | solution.py:439
  57.2 0.0 copy-done.6
  57.2 0.7 %finish.1 = f32[32,128]{1,0:T(8,128)} custom-call(s32[1]{0:T(128)} %bitcast.5.sky_ref, f32[32,128]{1,0:T(8,128)S(1)} %sweeps.1.mine_ref, f32[32,128]{1,0:T(8,128)S(1)} %collective-permute-done.12.theirs_ref, f32[32,128]{1,0:T(8,128)S(1)} %bitcast.16), custom_call_target="tpu_custom_call" | custom-call | flops 100000000 | tf_op jit(solution)/shard_map/finish/pallas_call | solution.py:545
  (1 shorter events, 0.0 us)
Async XLA Ops:
  0.6 14.9 %copy-start = (bf16[32,8192]{1,0:T(8,128)(2,1)S(1)}, bf16[32,8192]{1,0:T(8,128)(2,1)}, u32[]{:S(2)}) copy-start(bf16[32,8192]{1,0:T(8,128)(2,1)} %att_ref.3) | copy-start | bytes 1572868
  0.6 14.9 %copy-start.4 = (f32[8192]{0:T(1024)S(1)}, f32[8192]{0:T(1024)}, u32[]{:S(2)}) copy-start(f32[8192]{0:T(1024)} %param.10) | copy-start | bytes 98308
  9.8 5.7 %copy-start.7 = (s32[64]{0:T(128)S(1)}, s32[64]{0:T(128)}, u32[]{:S(2)}) copy-start(s32[64]{0:T(128)} %win_ref.1) | copy-start | bytes 772
  9.9 12.9 %collective-permute-start = (f32[21,8,128]{2,1,0:T(8,128)}, f32[21,8,128]{2,1,0:T(8,128)S(1)}, u32[]{:S(2)}, u32[]{:S(2)}) collective-permute-start(f32[21,8,128]{2,1,0:T(8,128)} %get-tuple-element.33), channel_id=1, source_target_pairs={{0,1},{1,0},{2,3},{3,2},{4,5},{5,4},{6,7},{7,6},{8,9},{9,8},{10,11... | collective-permute-start | bytes 258056 | tf_op jit(solution)/shard_map/ppermute | solution.py:435
  12.9 9.8 %collective-permute-start.1 = (f32[21,8,128]{2,1,0:T(8,128)}, f32[21,8,128]{2,1,0:T(8,128)S(1)}, u32[]{:S(2)}, u32[]{:S(2)}) collective-permute-start(f32[21,8,128]{2,1,0:T(8,128)} %get-tuple-element.34), channel_id=1, source_target_pairs={{0,2},{1,3},{2,0},{3,1},{4,6},{5,7},{6,4},{7,5},{8,10},{9,11},{10,... | collective-permute-start | bytes 258056 | tf_op jit(solution)/shard_map/ppermute | solution.py:435
  15.5 7.2 %collective-permute-start.2 = (f32[21,8,128]{2,1,0:T(8,128)}, f32[21,8,128]{2,1,0:T(8,128)S(1)}, u32[]{:S(2)}, u32[]{:S(2)}) collective-permute-start(f32[21,8,128]{2,1,0:T(8,128)} %get-tuple-element.35), channel_id=1, source_target_pairs={{0,3},{1,2},{2,1},{3,0},{4,7},{5,6},{6,5},{7,4},{8,11},{9,10},{10,... | collective-permute-start | bytes 258056 | tf_op jit(solution)/shard_map/ppermute | solution.py:435
  18.7 4.1 %copy-start.8 = (f32[21,8,128]{2,1,0:T(8,128)S(1)}, f32[21,8,128]{2,1,0:T(8,128)}, u32[]{:S(2)}) copy-start(f32[21,8,128]{2,1,0:T(8,128)} %get-tuple-element.36.refs_0_) | copy-start | bytes 258052
  18.7 13.8 %all-to-all-start = ((f32[8,16,8,128]{3,2,1,0:T(8,128)}), f32[8,16,8,128]{3,2,1,0:T(8,128)S(1)}, u32[]{:S(2)}, u32[]{:S(2)}) async-start(f32[8,16,8,128]{3,2,1,0:T(8,128)} %bitcast.6), calls=%async_computation | async-start | bytes 1048576 | tf_op jit(solution)/shard_map/all_to_all | solution.py:471
  23.0 12.5 %collective-permute-start.5 = (f32[5,8,128]{2,1,0:T(8,128)S(1)}, f32[5,8,128]{2,1,0:T(8,128)S(1)}, u32[]{:S(2)}, u32[]{:S(2)}) collective-permute-start(f32[5,8,128]{2,1,0:T(8,128)S(1)} %get-tuple-element.42.refs_0_), channel_id=1, source_target_pairs={{0,3},{1,2},{2,1},{3,0},{4,7},{5,6},{6,5},{7,4},{8,11},{9,10},{10,... | collective-permute-start | bytes 61448 | tf_op jit(solution)/shard_map/ppermute | solution.py:435
  26.6 8.9 %collective-permute-start.4 = (f32[5,8,128]{2,1,0:T(8,128)S(1)}, f32[5,8,128]{2,1,0:T(8,128)S(1)}, u32[]{:S(2)}, u32[]{:S(2)}) collective-permute-start(f32[5,8,128]{2,1,0:T(8,128)S(1)} %get-tuple-element.42.refs_0_), channel_id=1, source_target_pairs={{0,2},{1,3},{2,0},{3,1},{4,6},{5,7},{6,4},{7,5},{8,10},{9,11},{10,... | collective-permute-start | bytes 61448 | tf_op jit(solution)/shard_map/ppermute | solution.py:435
  26.6 8.9 %collective-permute-start.3 = (f32[5,8,128]{2,1,0:T(8,128)S(1)}, f32[5,8,128]{2,1,0:T(8,128)S(1)}, u32[]{:S(2)}, u32[]{:S(2)}) collective-permute-start(f32[5,8,128]{2,1,0:T(8,128)S(1)} %get-tuple-element.42.refs_0_), channel_id=1, source_target_pairs={{0,1},{1,0},{2,3},{3,2},{4,5},{5,4},{6,7},{7,6},{8,9},{9,8},{10,11... | collective-permute-start | bytes 61448 | tf_op jit(solution)/shard_map/ppermute | solution.py:435
  32.5 3.0 %copy-start.1 = (bf16[5,8192]{1,0:T(8,128)(2,1)S(1)}, bf16[5,8192]{1,0:T(8,128)(2,1)}, u32[]{:S(2)}) copy-start(bf16[5,8192]{1,0:T(8,128)(2,1)} %sp_ref.1) | copy-start | bytes 245764
  32.5 3.0 %copy-start.2 = (f32[5,4096]{1,0:T(8,128)S(1)}, f32[5,4096]{1,0:T(8,128)}, u32[]{:S(2)}) copy-start(f32[5,4096]{1,0:T(8,128)} %sources_ref.1) | copy-start | bytes 245764
  32.5 3.0 %copy-start.3 = (s32[8192]{0:T(1024)S(1)}, s32[8192]{0:T(1024)}, u32[]{:S(2)}) copy-start(s32[8192]{0:T(1024)} %param.13) | copy-start | bytes 98308
  32.5 3.0 %copy-start.5 = (f32[8192]{0:T(1024)S(1)}, f32[8192]{0:T(1024)}, u32[]{:S(2)}) copy-start(f32[8192]{0:T(1024)} %param.9) | copy-start | bytes 98308
  41.5 1.2 %collective-permute-start.6 = (f32[32,128]{1,0:T(8,128)S(1)}, f32[32,128]{1,0:T(8,128)S(1)}, u32[]{:S(2)}, u32[]{:S(2)}) collective-permute-start(f32[32,128]{1,0:T(8,128)S(1)} %get-tuple-element.48.mine_ref), channel_id=1, source_target_pairs={{0,4},{4,0},{8,12},{12,8},{16,20},{20,16},{24,28},{28,24},{1,5},{5... | collective-permute-start | bytes 49160 | tf_op jit(solution)/shard_map/send/ppermute | solution.py:439
  42.9 6.0 %collective-permute-start.9 = (f32[18,8,128]{2,1,0:T(8,128)S(1)}, f32[18,8,128]{2,1,0:T(8,128)S(1)}, u32[]{:S(2)}, u32[]{:S(2)}) collective-permute-start(f32[18,8,128]{2,1,0:T(8,128)S(1)} %send.1.refs_0_), channel_id=1, source_target_pairs={{0,24},{4,28},{8,16},{12,20},{16,8},{20,12},{24,0},{28,4},{1,25},{... | collective-permute-start | bytes 221192 | tf_op jit(solution)/shard_map/ppermute | solution.py:519
  43.4 5.6 %collective-permute-start.8 = (f32[18,8,128]{2,1,0:T(8,128)S(1)}, f32[18,8,128]{2,1,0:T(8,128)S(1)}, u32[]{:S(2)}, u32[]{:S(2)}) collective-permute-start(f32[18,8,128]{2,1,0:T(8,128)S(1)} %send.1.refs_0_), channel_id=1, source_target_pairs={{0,16},{4,20},{8,24},{12,28},{16,0},{20,4},{24,8},{28,12},{1,17},{... | collective-permute-start | bytes 221192 | tf_op jit(solution)/shard_map/ppermute | solution.py:519
  44.9 4.4 %collective-permute-start.7 = (f32[18,8,128]{2,1,0:T(8,128)S(1)}, f32[18,8,128]{2,1,0:T(8,128)S(1)}, u32[]{:S(2)}, u32[]{:S(2)}) collective-permute-start(f32[18,8,128]{2,1,0:T(8,128)S(1)} %send.1.refs_0_), channel_id=1, source_target_pairs={{0,8},{4,12},{8,0},{12,4},{16,24},{20,28},{24,16},{28,20},{1,9},{5... | collective-permute-start | bytes 221192 | tf_op jit(solution)/shard_map/ppermute | solution.py:519
  49.3 1.3 %collective-permute-start.10 = (f32[10,8,128]{2,1,0:T(8,128)S(1)}, f32[10,8,128]{2,1,0:T(8,128)S(1)}, u32[]{:S(2)}, u32[]{:S(2)}) collective-permute-start(f32[10,8,128]{2,1,0:T(8,128)S(1)} %get-tuple-element.50), channel_id=1, source_target_pairs={{0,4},{4,0},{8,12},{12,8},{16,20},{20,16},{24,28},{28,24},{1,5},{5... | collective-permute-start | bytes 122888 | tf_op jit(solution)/shard_map/ppermute | solution.py:439
  49.4 1.2 %collective-permute-start.11 = (f32[10,8,128]{2,1,0:T(8,128)S(1)}, f32[10,8,128]{2,1,0:T(8,128)S(1)}, u32[]{:S(2)}, u32[]{:S(2)}) collective-permute-start(f32[10,8,128]{2,1,0:T(8,128)S(1)} %get-tuple-element.51), channel_id=1, source_target_pairs={{4,1},{5,2},{6,3},{12,9},{13,10},{14,11},{20,17},{21,18},{22,19},{... | collective-permute-start | bytes 122888 | tf_op jit(solution)/shard_map/ppermute | solution.py:530
  50.6 6.6 %copy-start.6 = (f32[128,32]{0,1:T(8,128)S(1)}, f32[128,32]{0,1:T(8,128)}, u32[]{:S(2)}) copy-start(f32[128,32]{0,1:T(8,128)} %param.16) | copy-start | bytes 49156
  51.7 5.5 %collective-permute-start.12 = (f32[32,128]{1,0:T(8,128)S(1)}, f32[32,128]{1,0:T(8,128)S(1)}, u32[]{:S(2)}, u32[]{:S(2)}) collective-permute-start(f32[32,128]{1,0:T(8,128)S(1)} %sweeps.1.mine_ref), channel_id=1, source_target_pairs={{0,4},{4,0},{8,12},{12,8},{16,20},{20,16},{24,28},{28,24},{1,5},{5... | collective-permute-start | bytes 49160 | tf_op jit(solution)/shard_map/finish/ppermute | solution.py:439

commit v3 on v2

--- a/solution.py
+++ b/solution.py
@@ -19,8 +19,7 @@
 CORES = 2
 HALF = LANES // CORES
 SPLITS = 3
-CHUNK = 1024
-ROWS = CHUNK // TILE
+ROWS = 8
 F32 = jnp.float32
 BF16 = jnp.bfloat16
 NT = (((1,), (1,)), ((), ()))
@@ -64,7 +63,11 @@
 
 def low_one_hot(row, half, low_count):
     low = (row // half) * LANES + (row & (LANES - 1))
-    return jnp.where(iota((low_count, LANES), 0) == low, 1.0, 0.0).astype(BF16)
+    return jnp.where(
+        iota((low_count, LANES), 0).astype(F32).astype(BF16) == low.astype(F32).astype(BF16),
+        jnp.ones((), BF16),
+        jnp.zeros((), BF16),
+    )
 
 
 def high_digit(row, half):
@@ -80,19 +83,14 @@
         copy.start()
     half = hi_count * LANES
     low_count = rhs.shape[0]
-    acc[...] = jnp.zeros_like(acc)
     for copy in copies:
         copy.wait()
 
-    def chunk(c, carry):
-        base = pl.multiple_of(c * ROWS, ROWS)
-        src = src_ref[pl.ds(base, ROWS), :]
-        w = w_ref[pl.ds(base, ROWS), :]
-        r = r_ref[pl.ds(base, ROWS), :]
-        columns = [
-            sp_ref[:, pl.ds(pl.multiple_of((base + i) * TILE, TILE), TILE)].astype(F32)
-            for i in range(ROWS)
-        ]
+    tiles = src_ref.shape[0]
+    for base in range(0, tiles, ROWS):
+        part = slice(base, base + ROWS)
+        src, w, r = src_ref[part, :], w_ref[part, :], r_ref[part, :]
+        columns = [sp_ref[:, (base + i) * TILE : (base + i + 1) * TILE].astype(F32) for i in range(ROWS)]
         a = [
             jnp.concatenate([columns[i][p : p + 1] for i in range(ROWS)], axis=0)
             for p in range(PARAMS)
@@ -101,7 +99,7 @@
         sums = [wa[i] * a[j] for i, j in PAIRS] + [x * r for x in wa]
         parts = [[piece.astype(F32) for piece in split_bf16(s, SPLITS)] for s in sums]
         for i in range(ROWS):
-            lanes = slice(i * TILE, (i + 1) * TILE)
+            lanes = slice((base + i) * TILE, (base + i + 1) * TILE)
             row = src[i : i + 1]
             rhs[:, lanes] = low_one_hot(row, half, low_count)
             mask = jnp.where(iota((hi_count, LANES), 0) == high_digit(row, half), 1.0, 0.0).astype(BF16)
@@ -110,10 +108,7 @@
                     value = jnp.broadcast_to(parts[p][s][i : i + 1], (hi_count, LANES)).astype(BF16)
                     start = (s * MOMENTS + p) * hi_count
                     lhs[start : start + hi_count, lanes] = value * mask
-        acc[...] += lax.dot_general(lhs[...], rhs[...], NT, preferred_element_type=F32)
-        return carry
-
-    lax.fori_loop(0, src_ref.shape[0] // ROWS, chunk, 0)
+    acc[...] = lax.dot_general(lhs[...], rhs[...], NT, preferred_element_type=F32)
     rows = blocks.shape[2]
     for p in range(MOMENTS):
         total = acc[p * hi_count : (p + 1) * hi_count, :]
@@ -162,7 +157,7 @@
             out_ref[device * own + lax.rem(slot, own)] += value
         return carry
 
-    lax.fori_loop(0, w_ref.shape[0] // 2, pair, 0, unroll=4)
+    lax.fori_loop(0, w_ref.shape[0] // 2, pair, 0, unroll=True)
 
 
 def solve_kernel(me_ref, sky_ref, *refs):
@@ -274,7 +269,6 @@
     half = hi_count * LANES
     low_count = rhs.shape[0]
     windows = LANES
-    knots = att_ref.shape[0]
     me = me_ref[0]
     for k in range(peers):
         changes[me ^ k] = blocks[k][...]
@@ -292,33 +286,26 @@
             new_ref[:, lanes] = sources_ref[:, lanes] + step
     lookup = table[...].astype(BF16)
 
-    def chunk(c, total):
-        base = pl.multiple_of(c * ROWS, ROWS)
-        src = src_ref[pl.ds(base, ROWS), :]
-        w = w_ref[pl.ds(base, ROWS), :]
-        r = r_ref[pl.ds(base, ROWS), :]
-        for i in range(ROWS):
-            rhs[:, i * TILE : (i + 1) * TILE] = low_one_hot(src[i : i + 1], half, low_count)
-        chosen[...] = jnp.dot(lookup, rhs[...], preferred_element_type=F32)
-        for i in range(ROWS):
-            lanes = slice(i * TILE, (i + 1) * TILE)
-            columns = sp_ref[:, pl.ds(pl.multiple_of((base + i) * TILE, TILE), TILE)].astype(F32)
-            model = jnp.zeros((hi_count, LANES), F32)
-            for p in range(PARAMS):
-                value = chosen[p * hi_count : (p + 1) * hi_count, lanes]
-                for s in range(1, SPLITS):
-                    start = (s * PARAMS + p) * hi_count
-                    value = value + chosen[start : start + hi_count, lanes]
-                model = model + value * columns[p : p + 1]
-            here = iota((hi_count, LANES), 0) == high_digit(src[i : i + 1], half)
-            model = jnp.sum(jnp.where(here, model, 0.0), axis=0, keepdims=True)
-            change = w[i : i + 1] * (r[i : i + 1] - model)
-            slot = lax.rem(win_ref[base + i], windows)
-            weighted[:, lanes] = jnp.where(iota((windows, LANES), 0) == slot, change, 0.0).astype(BF16)
-        att = att_ref[:, pl.ds(pl.multiple_of(base * TILE, CHUNK), CHUNK)]
-        return total + lax.dot_general(att, weighted[...], NT, preferred_element_type=F32)
-
-    total = lax.fori_loop(0, src_ref.shape[0] // ROWS, chunk, jnp.zeros((knots, windows), F32))
+    tiles = src_ref.shape[0]
+    for i in range(tiles):
+        rhs[:, i * TILE : (i + 1) * TILE] = low_one_hot(src_ref[i : i + 1, :], half, low_count)
+    chosen[...] = jnp.dot(lookup, rhs[...], preferred_element_type=F32)
+    for i in range(tiles):
+        lanes = slice(i * TILE, (i + 1) * TILE)
+        columns = sp_ref[:, lanes].astype(F32)
+        model = jnp.zeros((hi_count, LANES), F32)
+        for p in range(PARAMS):
+            value = chosen[p * hi_count : (p + 1) * hi_count, lanes]
+            for s in range(1, SPLITS):
+                start = (s * PARAMS + p) * hi_count
+                value = value + chosen[start : start + hi_count, lanes]
+            model = model + value * columns[p : p + 1]
+        here = iota((hi_count, LANES), 0) == high_digit(src_ref[i : i + 1, :], half)
+        model = jnp.sum(jnp.where(here, model, 0.0), axis=0, keepdims=True)
+        change = w_ref[i : i + 1, :] * (r_ref[i : i + 1, :] - model)
+        slot = lax.rem(win_ref[i], windows)
+        weighted[:, lanes] = jnp.where(iota((windows, LANES), 0) == slot, change, 0.0).astype(BF16)
+    total = lax.dot_general(att_ref[...], weighted[...], NT, preferred_element_type=F32)
     out_ref[...] = total
 
 
@@ -415,7 +402,8 @@
     devices = lax.axis_size("sky")
     source_count = sources.shape[1]
     windows, knots = attitude.shape
-    tiles = residuals.shape[0] // TILE
+    observations = residuals.shape[0]
+    tiles = observations // TILE
     own = windows // devices
     rows = source_count // LANES // peers
     hi_count = source_count // (2 * LANES)
@@ -445,8 +433,8 @@
             [block] * peers,
             [smem()] + [pl.BlockSpec(memory_space=pl.ANY)] * 5,
             [
-                pltpu.VMEM((SPLITS * MOMENTS * hi_count, CHUNK), BF16),
-                pltpu.VMEM((low_count, CHUNK), BF16),
+                pltpu.VMEM((SPLITS * MOMENTS * hi_count, observations), BF16),
+                pltpu.VMEM((low_count, observations), BF16),
                 pltpu.VMEM((SPLITS * MOMENTS * hi_count, low_count), F32),
                 pltpu.VMEM((peers, MOMENTS + 1, rows, LANES), F32),
                 pltpu.VMEM(src.shape, jnp.int32),
@@ -502,9 +490,9 @@
             [
                 pltpu.VMEM((peers, PARAMS, rows, LANES), F32),
                 pltpu.VMEM((SPLITS * PARAMS * hi_count, low_count), F32),
-                pltpu.VMEM((low_count, CHUNK), BF16),
-                pltpu.VMEM((SPLITS * PARAMS * hi_count, CHUNK), F32),
-                pltpu.VMEM((windows, CHUNK), BF16),
+                pltpu.VMEM((low_count, observations), BF16),
+                pltpu.VMEM((SPLITS * PARAMS * hi_count, observations), F32),
+                pltpu.VMEM((windows, observations), BF16),
             ],
             micros=6,
         )(me, tile_window, src, w, r, source_partials, attitude_partials, sources, *changes)

time: 58.1 us -> 54.1 us (0.931)
  Pallas kernels: 23.4 us -> 19.4 us
    pallas_call x1, Pallas kernels: 6.04 us -> 4.21 us  [on_device(): call(functools.partial(rhs_kernel, hi_count), [jax.ShapeDtypeStruct(sourc...]
    pallas_call x1, Pallas kernels: 9.18 us -> 7.86 us  [on_device(): call(functools.partial(moments_kernel, hi_count), [block] * peers, [smem(...]
    pallas_call x1, Pallas kernels: 3.14 us -> 2.33 us  [on_device(): call(functools.partial(normals_kernel, chips), jax.ShapeDtypeStruct((wind...]
    ppermute x6, waiting for transfers between devices: 0.02 us -> 0.71 us  [swapped(): out[k] = lax.ppermute(blocks[k], 'tm', [(i, i ^ k) for i in range(peers)])]
    all_to_all x1, waiting for transfers between devices: 5.12 us -> 4.47 us  [on_device(): lax.all_to_all(normals.reshape(devices, own, cell_rows, LANES), 'sky', 0,...]
  transfers between devices with their start and end apart: 14 -> 14, of which waited for: 7 -> 8; matrix products, arithmetic and copies ran while one was open for 0% -> 0% of each run, Pallas kernels for 11% -> 10%
where the time goes in v3:
time: 54.1 us; the launch traced here: 53.9 us
  starting transfers between devices  23 us (43%)
  Pallas kernels  19.4 us (36%)
  waiting for transfers between devices  10.6 us (20%)
  between operations  0.79 us (1%)
    ppermute x6, starting transfers between devices, swapped(): out[k] = lax.ppermute(blocks[k], 'tm', [(i, i ^ k) for i in range(peers)])  10.1 us
    pallas_call x1, Pallas kernels, on_device(): call(functools.partial(moments_kernel, hi_count), [block] * peers, [smem(...  7.86 us
    ppermute x3, starting transfers between devices, other_core(): return lax.ppermute(x, 'sky', [(i, i ^ 1) for i in range(devices)])  4.73 us
    all_to_all x1, waiting for transfers between devices, on_device(): lax.all_to_all(normals.reshape(devices, own, cell_rows, LANES), 'sky', 0,...  4.47 us
    pallas_call x1, Pallas kernels, on_device(): call(functools.partial(rhs_kernel, hi_count), [jax.ShapeDtypeStruct(sourc...  4.21 us
    all_to_all x1, starting transfers between devices, on_device(): lax.all_to_all(normals.reshape(devices, own, cell_rows, LANES), 'sky', 0,...  4.06 us
    ppermute x3, starting transfers between devices, on_device(): lax.ppermute(sent, 'sky', [(i, i ^ CORES * k) for i in range(devices)])  3.49 us
    pallas_call x1, Pallas kernels, on_device(): call(invert_kernel, jax.ShapeDtypeStruct((own, cell_rows, LANES), F32), [...  2.9 us
  transfers between devices with their start and end apart: 14, of which 8 were waited for; matrix products, arithmetic and copies ran while one was open for 0% of the time, Pallas kernels for 10%

profile of v3, /device:TPU:0, one launch (start us, length us, event | category | flops | bytes accessed | tf_op | source)
XLA Modules:
  0.0 53.9 jit_solution(4218344656464933905)
XLA Ops:
  0.6 0.0 copy-start
  0.6 0.0 copy-start.4
  0.7 7.9 %moments.1 = (f32[21,8,128]{2,1,0:T(8,128)}, f32[21,8,128]{2,1,0:T(8,128)}, f32[21,8,128]{2,1,0:T(8,128)}, f32[21,8,128]{2,1,0:T(8,128)}) custom-call(s32[1]{0:T(128)} %bitcast.me_ref, s32[64,128]{1,0:T(8,128)} %bitcast.9, f32[64,128]{1,0:T(8,128)} %bitcast.11, f32[64,128]{1,0:T(8,128)} %bitcast.14, bf16[5,8192]{1,0:T(8,128)(2,1)} %sp_ref.1, f32[1,128]{1,0:T(1,128)} %bitcast.17), custom_call_target="tpu_custom_call" | custom-call | flops 7500000256 | tf_op jit(solution)/shard_map/moments/pallas_call | solution.py:431
  8.5 0.0 copy-start.7
  8.5 3.1 %collective-permute-start = (f32[21,8,128]{2,1,0:T(8,128)}, f32[21,8,128]{2,1,0:T(8,128)S(1)}, u32[]{:S(2)}, u32[]{:S(2)}) collective-permute-start(f32[21,8,128]{2,1,0:T(8,128)} %get-tuple-element.33), channel_id=1, source_target_pairs={{0,1},{1,0},{2,3},{3,2},{4,5},{5,4},{6,7},{7,6},{8,9},{9,8},{10,11... | collective-permute-start | bytes 258056 | tf_op jit(solution)/shard_map/ppermute | solution.py:423
  11.6 2.6 %collective-permute-start.1 = (f32[21,8,128]{2,1,0:T(8,128)}, f32[21,8,128]{2,1,0:T(8,128)S(1)}, u32[]{:S(2)}, u32[]{:S(2)}) collective-permute-start(f32[21,8,128]{2,1,0:T(8,128)} %get-tuple-element.34), channel_id=1, source_target_pairs={{0,2},{1,3},{2,0},{3,1},{4,6},{5,7},{6,4},{7,5},{8,10},{9,11},{10,... | collective-permute-start | bytes 258056 | tf_op jit(solution)/shard_map/ppermute | solution.py:423
  14.2 0.0 collective-permute-start.2
  14.2 0.0 copy-done
  14.2 0.0 copy-done.4
  14.2 0.0 copy-done.7
  14.2 2.3 %normals.1 = f32[128,8,128]{2,1,0:T(8,128)} custom-call(s32[64]{0:T(128)S(1)} %copy-done.7, f32[64,128]{1,0:T(8,128)S(1)} %bitcast.12, bf16[32,8192]{1,0:T(8,128)(2,1)S(1)} %copy-done), custom_call_target="tpu_custom_call" | custom-call | flops 3000000000 | tf_op jit(solution)/shard_map/normals/pallas_call | solution.py:453
  16.6 0.0 copy-start.8
  16.6 4.1 %all-to-all-start = ((f32[8,16,8,128]{3,2,1,0:T(8,128)}), f32[8,16,8,128]{3,2,1,0:T(8,128)S(1)}, u32[]{:S(2)}, u32[]{:S(2)}) async-start(f32[8,16,8,128]{3,2,1,0:T(8,128)} %bitcast.6), calls=%async_computation | async-start | bytes 1048576 | tf_op jit(solution)/shard_map/all_to_all | solution.py:459
  20.6 0.0 collective-permute-done.refs_1_
  20.6 0.7 %collective-permute-done.1.refs_2_ = f32[21,8,128]{2,1,0:T(8,128)S(1)} collective-permute-done((f32[21,8,128]{2,1,0:T(8,128)}, f32[21,8,128]{2,1,0:T(8,128)S(1)}, u32[]{:S(2)}, u32[]{:S(2)}) %collective-permute-start.1) | collective-permute-done | bytes 86048 | tf_op jit(solution)/shard_map/ppermute | solution.py:423
  21.3 0.0 collective-permute-done.2.refs_3_
  21.3 0.0 copy-done.8
  21.3 0.2 solve.1
  21.5 3.0 %collective-permute-start.5 = (f32[5,8,128]{2,1,0:T(8,128)S(1)}, f32[5,8,128]{2,1,0:T(8,128)S(1)}, u32[]{:S(2)}, u32[]{:S(2)}) collective-permute-start(f32[5,8,128]{2,1,0:T(8,128)S(1)} %get-tuple-element.42.refs_0_), channel_id=1, source_target_pairs={{0,3},{1,2},{2,1},{3,0},{4,7},{5,6},{6,5},{7,4},{8,11},{9,10},{10,... | collective-permute-start | bytes 61448 | tf_op jit(solution)/shard_map/ppermute | solution.py:423
  24.5 0.0 collective-permute-start.4
  24.5 1.4 %collective-permute-start.3 = (f32[5,8,128]{2,1,0:T(8,128)S(1)}, f32[5,8,128]{2,1,0:T(8,128)S(1)}, u32[]{:S(2)}, u32[]{:S(2)}) collective-permute-start(f32[5,8,128]{2,1,0:T(8,128)S(1)} %get-tuple-element.42.refs_0_), channel_id=1, source_target_pairs={{0,1},{1,0},{2,3},{3,2},{4,5},{5,4},{6,7},{7,6},{8,9},{9,8},{10,11... | collective-permute-start | bytes 61448 | tf_op jit(solution)/shard_map/ppermute | solution.py:423
  25.9 4.5 %all-to-all-done.part_ref = f32[8,16,8,128]{3,2,1,0:T(8,128)S(1)} async-done(((f32[8,16,8,128]{3,2,1,0:T(8,128)}), f32[8,16,8,128]{3,2,1,0:T(8,128)S(1)}, u32[]{:S(2)}, u32[]{:S(2)}) %all-to-all-start) | async-done | bytes 524320 | tf_op jit(solution)/shard_map/all_to_all | solution.py:459
  30.4 0.0 copy-start.1
  30.4 0.0 copy-start.2
  30.4 0.0 copy-start.3
  30.4 0.0 copy-start.5
  30.4 2.9 %invert.1.inv_ref = f32[16,8,128]{2,1,0:T(8,128)S(1)} custom-call(s32[1]{0:T(128)} %bitcast.5.sky_ref, f32[8,16,8,128]{3,2,1,0:T(8,128)S(1)} %all-to-all-done.part_ref, f32[3,8,128]{2,1,0:T(8,128)S(1)} %get-tuple-element.40.ties_ref), custom_call_target="tpu_custom_call" | custom-call | flops 3000000000 | tf_op jit(solution)/shard_map/invert/pallas_call | solution.py:474
  33.3 0.0 collective-permute-done.5.refs_3_
  33.3 0.0 collective-permute-done.4.refs_2_
  33.3 0.0 collective-permute-done.3.refs_1_
  33.3 0.0 copy-done.1
  33.3 0.0 copy-done.2
  33.3 0.0 copy-done.3
  33.4 0.0 copy-done.5
  33.4 4.2 %right_sides.1 = (f32[5,4096]{1,0:T(8,128)}, f32[32,128]{1,0:T(8,128)S(1)}) custom-call(s32[1]{0:T(128)} %bitcast.me_ref, s32[64]{0:T(128)S(1)} %copy-done.7, s32[64,128]{1,0:T(8,128)S(1)} %bitcast.10, f32[64,128]{1,0:T(8,128)S(1)} %bitcast.13, f32[64,128]{1,0:T(8,128)S(1)} %bitcast.15, bf16[5,8192]{1,0:T(8,128)(2,1)S(1)} %copy-done.1, ...), custom_call_target="tpu_custom_call" | custom-call | flops 6000000000 | tf_op jit(solution)/shard_map/right_sides/pallas_call | solution.py:483
  37.6 0.0 collective-permute-start.6
  37.6 1.2 %collective-permute-done.6.theirs_ref = f32[32,128]{1,0:T(8,128)S(1)} collective-permute-done((f32[32,128]{1,0:T(8,128)S(1)}, f32[32,128]{1,0:T(8,128)S(1)}, u32[]{:S(2)}, u32[]{:S(2)}) %collective-permute-start.6) | collective-permute-done | bytes 16416 | tf_op jit(solution)/shard_map/send/ppermute | solution.py:427
  38.8 0.1 send.1.refs_0_
  38.9 0.6 %collective-permute-start.9 = (f32[18,8,128]{2,1,0:T(8,128)S(1)}, f32[18,8,128]{2,1,0:T(8,128)S(1)}, u32[]{:S(2)}, u32[]{:S(2)}) collective-permute-start(f32[18,8,128]{2,1,0:T(8,128)S(1)} %send.1.refs_0_), channel_id=1, source_target_pairs={{0,24},{4,28},{8,16},{12,20},{16,8},{20,12},{24,0},{28,4},{1,25},{... | collective-permute-start | bytes 221192 | tf_op jit(solution)/shard_map/ppermute | solution.py:507
  39.5 1.5 %collective-permute-start.8 = (f32[18,8,128]{2,1,0:T(8,128)S(1)}, f32[18,8,128]{2,1,0:T(8,128)S(1)}, u32[]{:S(2)}, u32[]{:S(2)}) collective-permute-start(f32[18,8,128]{2,1,0:T(8,128)S(1)} %send.1.refs_0_), channel_id=1, source_target_pairs={{0,16},{4,20},{8,24},{12,28},{16,0},{20,4},{24,8},{28,12},{1,17},{... | collective-permute-start | bytes 221192 | tf_op jit(solution)/shard_map/ppermute | solution.py:507
  40.9 1.5 %collective-permute-start.7 = (f32[18,8,128]{2,1,0:T(8,128)S(1)}, f32[18,8,128]{2,1,0:T(8,128)S(1)}, u32[]{:S(2)}, u32[]{:S(2)}) collective-permute-start(f32[18,8,128]{2,1,0:T(8,128)S(1)} %send.1.refs_0_), channel_id=1, source_target_pairs={{0,8},{4,12},{8,0},{12,4},{16,24},{20,28},{24,16},{28,20},{1,9},{5... | collective-permute-start | bytes 221192 | tf_op jit(solution)/shard_map/ppermute | solution.py:507
  42.4 2.5 %collective-permute-done.9.refs_3_ = f32[18,8,128]{2,1,0:T(8,128)S(1)} collective-permute-done((f32[18,8,128]{2,1,0:T(8,128)S(1)}, f32[18,8,128]{2,1,0:T(8,128)S(1)}, u32[]{:S(2)}, u32[]{:S(2)}) %collective-permute-start.9) | collective-permute-done | bytes 73760 | tf_op jit(solution)/shard_map/ppermute | solution.py:507
  44.9 0.2 collective-permute-done.8.refs_2_
  45.1 0.2 collective-permute-done.7.refs_1_
  45.3 0.1 collective-permute-start.10
  45.4 0.7 %collective-permute-start.11 = (f32[10,8,128]{2,1,0:T(8,128)S(1)}, f32[10,8,128]{2,1,0:T(8,128)S(1)}, u32[]{:S(2)}, u32[]{:S(2)}) collective-permute-start(f32[10,8,128]{2,1,0:T(8,128)S(1)} %get-tuple-element.51), channel_id=1, source_target_pairs={{4,1},{5,2},{6,3},{12,9},{13,10},{14,11},{20,17},{21,18},{22,19},{... | collective-permute-start | bytes 122888 | tf_op jit(solution)/shard_map/ppermute | solution.py:518
  46.1 0.5 collective-permute-done.10.inner_ref
  46.6 0.0 collective-permute-done.11.outer_ref
  46.6 0.0 copy-start.6
  46.6 1.1 %sweeps.1.mine_ref = f32[32,128]{1,0:T(8,128)S(1)} custom-call(s32[1]{0:T(128)} %bitcast.5.sky_ref, f32[66,8,128]{2,1,0:T(8,128)S(1)} %get-tuple-element.49.main_ref, f32[10,8,128]{2,1,0:T(8,128)S(1)} %collective-permute-done.10.inner_ref, f32[10,8,128]{2,1,0:T(8,128)S(1)} %collective-permute-done.11.outer_ref, f32[3,8,128]{2,1,0:T(8,128)S(1)} %get-tuple-element.40.ties_ref), custom_call_target="tpu_custom_call" | custom-call | flops 1000000000 | tf_op jit(solution)/shard_map/sweeps/pallas_call | solution.py:521
  47.7 4.7 %collective-permute-start.12 = (f32[32,128]{1,0:T(8,128)S(1)}, f32[32,128]{1,0:T(8,128)S(1)}, u32[]{:S(2)}, u32[]{:S(2)}) collective-permute-start(f32[32,128]{1,0:T(8,128)S(1)} %sweeps.1.mine_ref), channel_id=1, source_target_pairs={{0,4},{4,0},{8,12},{12,8},{16,20},{20,16},{24,28},{28,24},{1,5},{5... | collective-permute-start | bytes 49160 | tf_op jit(solution)/shard_map/finish/ppermute | solution.py:427
  52.4 0.8 %collective-permute-done.12.theirs_ref = f32[32,128]{1,0:T(8,128)S(1)} collective-permute-done((f32[32,128]{1,0:T(8,128)S(1)}, f32[32,128]{1,0:T(8,128)S(1)}, u32[]{:S(2)}, u32[]{:S(2)}) %collective-permute-start.12) | collective-permute-done | bytes 16416 | tf_op jit(solution)/shard_map/finish/ppermute | solution.py:427
  53.2 0.0 copy-done.6
  53.2 0.7 %finish.1 = f32[32,128]{1,0:T(8,128)} custom-call(s32[1]{0:T(128)} %bitcast.5.sky_ref, f32[32,128]{1,0:T(8,128)S(1)} %sweeps.1.mine_ref, f32[32,128]{1,0:T(8,128)S(1)} %collective-permute-done.12.theirs_ref, f32[32,128]{1,0:T(8,128)S(1)} %bitcast.16), custom_call_target="tpu_custom_call" | custom-call | flops 100000000 | tf_op jit(solution)/shard_map/finish/pallas_call | solution.py:533
  (1 shorter events, 0.0 us)
Async XLA Ops:
  0.6 13.6 %copy-start = (bf16[32,8192]{1,0:T(8,128)(2,1)S(1)}, bf16[32,8192]{1,0:T(8,128)(2,1)}, u32[]{:S(2)}) copy-start(bf16[32,8192]{1,0:T(8,128)(2,1)} %att_ref.3) | copy-start | bytes 1572868
  0.6 13.6 %copy-start.4 = (f32[8192]{0:T(1024)S(1)}, f32[8192]{0:T(1024)}, u32[]{:S(2)}) copy-start(f32[8192]{0:T(1024)} %param.10) | copy-start | bytes 98308
  8.5 5.7 %copy-start.7 = (s32[64]{0:T(128)S(1)}, s32[64]{0:T(128)}, u32[]{:S(2)}) copy-start(s32[64]{0:T(128)} %win_ref.1) | copy-start | bytes 772
  8.5 12.1 %collective-permute-start = (f32[21,8,128]{2,1,0:T(8,128)}, f32[21,8,128]{2,1,0:T(8,128)S(1)}, u32[]{:S(2)}, u32[]{:S(2)}) collective-permute-start(f32[21,8,128]{2,1,0:T(8,128)} %get-tuple-element.33), channel_id=1, source_target_pairs={{0,1},{1,0},{2,3},{3,2},{4,5},{5,4},{6,7},{7,6},{8,9},{9,8},{10,11... | collective-permute-start | bytes 258056 | tf_op jit(solution)/shard_map/ppermute | solution.py:423
  11.6 9.7 %collective-permute-start.1 = (f32[21,8,128]{2,1,0:T(8,128)}, f32[21,8,128]{2,1,0:T(8,128)S(1)}, u32[]{:S(2)}, u32[]{:S(2)}) collective-permute-start(f32[21,8,128]{2,1,0:T(8,128)} %get-tuple-element.34), channel_id=1, source_target_pairs={{0,2},{1,3},{2,0},{3,1},{4,6},{5,7},{6,4},{7,5},{8,10},{9,11},{10,... | collective-permute-start | bytes 258056 | tf_op jit(solution)/shard_map/ppermute | solution.py:423
  14.2 7.1 %collective-permute-start.2 = (f32[21,8,128]{2,1,0:T(8,128)}, f32[21,8,128]{2,1,0:T(8,128)S(1)}, u32[]{:S(2)}, u32[]{:S(2)}) collective-permute-start(f32[21,8,128]{2,1,0:T(8,128)} %get-tuple-element.35), channel_id=1, source_target_pairs={{0,3},{1,2},{2,1},{3,0},{4,7},{5,6},{6,5},{7,4},{8,11},{9,10},{10,... | collective-permute-start | bytes 258056 | tf_op jit(solution)/shard_map/ppermute | solution.py:423
  16.6 4.8 %copy-start.8 = (f32[21,8,128]{2,1,0:T(8,128)S(1)}, f32[21,8,128]{2,1,0:T(8,128)}, u32[]{:S(2)}) copy-start(f32[21,8,128]{2,1,0:T(8,128)} %get-tuple-element.36.refs_0_) | copy-start | bytes 258052
  16.6 13.8 %all-to-all-start = ((f32[8,16,8,128]{3,2,1,0:T(8,128)}), f32[8,16,8,128]{3,2,1,0:T(8,128)S(1)}, u32[]{:S(2)}, u32[]{:S(2)}) async-start(f32[8,16,8,128]{3,2,1,0:T(8,128)} %bitcast.6), calls=%async_computation | async-start | bytes 1048576 | tf_op jit(solution)/shard_map/all_to_all | solution.py:459
  21.5 11.8 %collective-permute-start.5 = (f32[5,8,128]{2,1,0:T(8,128)S(1)}, f32[5,8,128]{2,1,0:T(8,128)S(1)}, u32[]{:S(2)}, u32[]{:S(2)}) collective-permute-start(f32[5,8,128]{2,1,0:T(8,128)S(1)} %get-tuple-element.42.refs_0_), channel_id=1, source_target_pairs={{0,3},{1,2},{2,1},{3,0},{4,7},{5,6},{6,5},{7,4},{8,11},{9,10},{10,... | collective-permute-start | bytes 61448 | tf_op jit(solution)/shard_map/ppermute | solution.py:423
  24.5 8.9 %collective-permute-start.4 = (f32[5,8,128]{2,1,0:T(8,128)S(1)}, f32[5,8,128]{2,1,0:T(8,128)S(1)}, u32[]{:S(2)}, u32[]{:S(2)}) collective-permute-start(f32[5,8,128]{2,1,0:T(8,128)S(1)} %get-tuple-element.42.refs_0_), channel_id=1, source_target_pairs={{0,2},{1,3},{2,0},{3,1},{4,6},{5,7},{6,4},{7,5},{8,10},{9,11},{10,... | collective-permute-start | bytes 61448 | tf_op jit(solution)/shard_map/ppermute | solution.py:423
  24.5 8.9 %collective-permute-start.3 = (f32[5,8,128]{2,1,0:T(8,128)S(1)}, f32[5,8,128]{2,1,0:T(8,128)S(1)}, u32[]{:S(2)}, u32[]{:S(2)}) collective-permute-start(f32[5,8,128]{2,1,0:T(8,128)S(1)} %get-tuple-element.42.refs_0_), channel_id=1, source_target_pairs={{0,1},{1,0},{2,3},{3,2},{4,5},{5,4},{6,7},{7,6},{8,9},{9,8},{10,11... | collective-permute-start | bytes 61448 | tf_op jit(solution)/shard_map/ppermute | solution.py:423
  30.4 3.0 %copy-start.1 = (bf16[5,8192]{1,0:T(8,128)(2,1)S(1)}, bf16[5,8192]{1,0:T(8,128)(2,1)}, u32[]{:S(2)}) copy-start(bf16[5,8192]{1,0:T(8,128)(2,1)} %sp_ref.1) | copy-start | bytes 245764
  30.4 3.0 %copy-start.2 = (f32[5,4096]{1,0:T(8,128)S(1)}, f32[5,4096]{1,0:T(8,128)}, u32[]{:S(2)}) copy-start(f32[5,4096]{1,0:T(8,128)} %sources_ref.1) | copy-start | bytes 245764
  30.4 3.0 %copy-start.3 = (s32[8192]{0:T(1024)S(1)}, s32[8192]{0:T(1024)}, u32[]{:S(2)}) copy-start(s32[8192]{0:T(1024)} %param.13) | copy-start | bytes 98308
  30.4 3.0 %copy-start.5 = (f32[8192]{0:T(1024)S(1)}, f32[8192]{0:T(1024)}, u32[]{:S(2)}) copy-start(f32[8192]{0:T(1024)} %param.9) | copy-start | bytes 98308
  37.6 1.2 %collective-permute-start.6 = (f32[32,128]{1,0:T(8,128)S(1)}, f32[32,128]{1,0:T(8,128)S(1)}, u32[]{:S(2)}, u32[]{:S(2)}) collective-permute-start(f32[32,128]{1,0:T(8,128)S(1)} %get-tuple-element.48.mine_ref), channel_id=1, source_target_pairs={{0,4},{4,0},{8,12},{12,8},{16,20},{20,16},{24,28},{28,24},{1,5},{5... | collective-permute-start | bytes 49160 | tf_op jit(solution)/shard_map/send/ppermute | solution.py:427
  38.9 6.0 %collective-permute-start.9 = (f32[18,8,128]{2,1,0:T(8,128)S(1)}, f32[18,8,128]{2,1,0:T(8,128)S(1)}, u32[]{:S(2)}, u32[]{:S(2)}) collective-permute-start(f32[18,8,128]{2,1,0:T(8,128)S(1)} %send.1.refs_0_), channel_id=1, source_target_pairs={{0,24},{4,28},{8,16},{12,20},{16,8},{20,12},{24,0},{28,4},{1,25},{... | collective-permute-start | bytes 221192 | tf_op jit(solution)/shard_map/ppermute | solution.py:507
  39.5 5.6 %collective-permute-start.8 = (f32[18,8,128]{2,1,0:T(8,128)S(1)}, f32[18,8,128]{2,1,0:T(8,128)S(1)}, u32[]{:S(2)}, u32[]{:S(2)}) collective-permute-start(f32[18,8,128]{2,1,0:T(8,128)S(1)} %send.1.refs_0_), channel_id=1, source_target_pairs={{0,16},{4,20},{8,24},{12,28},{16,0},{20,4},{24,8},{28,12},{1,17},{... | collective-permute-start | bytes 221192 | tf_op jit(solution)/shard_map/ppermute | solution.py:507
  40.9 4.4 %collective-permute-start.7 = (f32[18,8,128]{2,1,0:T(8,128)S(1)}, f32[18,8,128]{2,1,0:T(8,128)S(1)}, u32[]{:S(2)}, u32[]{:S(2)}) collective-permute-start(f32[18,8,128]{2,1,0:T(8,128)S(1)} %send.1.refs_0_), channel_id=1, source_target_pairs={{0,8},{4,12},{8,0},{12,4},{16,24},{20,28},{24,16},{28,20},{1,9},{5... | collective-permute-start | bytes 221192 | tf_op jit(solution)/shard_map/ppermute | solution.py:507
  45.3 1.3 %collective-permute-start.10 = (f32[10,8,128]{2,1,0:T(8,128)S(1)}, f32[10,8,128]{2,1,0:T(8,128)S(1)}, u32[]{:S(2)}, u32[]{:S(2)}) collective-permute-start(f32[10,8,128]{2,1,0:T(8,128)S(1)} %get-tuple-element.50), channel_id=1, source_target_pairs={{0,4},{4,0},{8,12},{12,8},{16,20},{20,16},{24,28},{28,24},{1,5},{5... | collective-permute-start | bytes 122888 | tf_op jit(solution)/shard_map/ppermute | solution.py:427
  45.4 1.2 %collective-permute-start.11 = (f32[10,8,128]{2,1,0:T(8,128)S(1)}, f32[10,8,128]{2,1,0:T(8,128)S(1)}, u32[]{:S(2)}, u32[]{:S(2)}) collective-permute-start(f32[10,8,128]{2,1,0:T(8,128)S(1)} %get-tuple-element.51), channel_id=1, source_target_pairs={{4,1},{5,2},{6,3},{12,9},{13,10},{14,11},{20,17},{21,18},{22,19},{... | collective-permute-start | bytes 122888 | tf_op jit(solution)/shard_map/ppermute | solution.py:518
  46.6 6.6 %copy-start.6 = (f32[128,32]{0,1:T(8,128)S(1)}, f32[128,32]{0,1:T(8,128)}, u32[]{:S(2)}) copy-start(f32[128,32]{0,1:T(8,128)} %param.16) | copy-start | bytes 49156
  47.7 5.5 %collective-permute-start.12 = (f32[32,128]{1,0:T(8,128)S(1)}, f32[32,128]{1,0:T(8,128)S(1)}, u32[]{:S(2)}, u32[]{:S(2)}) collective-permute-start(f32[32,128]{1,0:T(8,128)S(1)} %sweeps.1.mine_ref), channel_id=1, source_target_pairs={{0,4},{4,0},{8,12},{12,8},{16,20},{20,16},{24,28},{28,24},{1,5},{5... | collective-permute-start | bytes 49160 | tf_op jit(solution)/shard_map/finish/ppermute | solution.py:427

commit v4 on v3

--- a/solution.py
+++ b/solution.py
@@ -18,13 +18,18 @@
 LANES = 128
 CORES = 2
 HALF = LANES // CORES
-SPLITS = 3
+SPLITS = 2
+LOOKUP_SPLITS = 3
 ROWS = 8
 F32 = jnp.float32
 BF16 = jnp.bfloat16
 NT = (((1,), (1,)), ((), ()))
 FLOPS_MICRO = 1e9
 VMEM_LIMIT = 48 * 1024 * 1024
+
+
+def masks(count):
+    return [0] + list(range(count - 1, 0, -1))
 
 
 def vmem():
@@ -74,18 +79,32 @@
     return (row & (half - 1)) // LANES
 
 
-def moments_kernel(hi_count, me_ref, src_hbm, w_hbm, r_hbm, sp_hbm, tie_hbm, *refs):
-    peers = len(refs) - 10
-    outs, (lhs, rhs, acc, blocks, src_ref, w_ref, r_ref, sp_ref, tie_ref, sems) = refs[:peers], refs[peers:]
-    pairs = ((src_hbm, src_ref), (w_hbm, w_ref), (r_hbm, r_ref), (sp_hbm, sp_ref), (tie_hbm, tie_ref))
+def sums_kernel(hi_count, me_ref, sky_ref, win_ref, src_hbm, w_hbm, r_hbm, sp_hbm, att_hbm, tie_hbm, *refs):
+    peers = len(refs) - 14
+    outs, (keep_ref, give_ref, normals, lhs, rhs, acc, blocks) = refs[:peers], refs[peers : peers + 7]
+    src_ref, w_ref, r_ref, sp_ref, att_ref, tie_ref, sems = refs[peers + 7 :]
+    pairs = (
+        (w_hbm, w_ref),
+        (att_hbm, att_ref),
+        (src_hbm, src_ref),
+        (r_hbm, r_ref),
+        (sp_hbm, sp_ref),
+        (tie_hbm, tie_ref),
+    )
     copies = [pltpu.make_async_copy(a, b, sems.at[i]) for i, (a, b) in enumerate(pairs)]
     for copy in copies:
         copy.start()
+    normals[...] = jnp.zeros_like(normals)
+    for copy in copies[:2]:
+        copy.wait()
+    window_normals(win_ref, w_ref, att_ref, normals)
+    core = lax.rem(sky_ref[0], CORES)
+    keep_ref[...] = normals[pl.ds(core * HALF, HALF)]
+    give_ref[...] = normals[pl.ds((1 - core) * HALF, HALF)]
+    for copy in copies[2:]:
+        copy.wait()
     half = hi_count * LANES
     low_count = rhs.shape[0]
-    for copy in copies:
-        copy.wait()
-
     tiles = src_ref.shape[0]
     for base in range(0, tiles, ROWS):
         part = slice(base, base + ROWS)
@@ -121,22 +140,20 @@
     for j in range(peers):
         blocks[j, MOMENTS] = jnp.broadcast_to(tie_ref[...], (rows, LANES))
     me = me_ref[0]
-    for k in range(peers):
-        outs[k][...] = blocks[me ^ k]
-
-
-def normals_kernel(chips, win_ref, w_ref, att_ref, out_ref):
-    windows = out_ref.shape[0]
-    own = windows // chips // CORES
+    for out, mask in zip(outs, masks(peers)):
+        out[...] = blocks[me ^ mask]
+
+
+def window_normals(win_ref, w_ref, att_ref, sums):
+    windows = sums.shape[0]
     knots = att_ref.shape[0]
     copies = LANES // knots
-    out_ref[...] = jnp.zeros_like(out_ref)
     blank = jnp.zeros((knots, TILE), BF16)
     lane = iota((8, LANES), 1)
 
-    def pair(u, carry):
-        att = att_ref[:, pl.ds(pl.multiple_of(u * 2 * TILE, 2 * TILE), 2 * TILE)]
-        w = jnp.concatenate([w_ref[pl.ds(2 * u, 1), :], w_ref[pl.ds(2 * u + 1, 1), :]], axis=1)
+    for u in range(w_ref.shape[0] // 2):
+        att = att_ref[:, 2 * u * TILE : 2 * (u + 1) * TILE]
+        w = jnp.concatenate([w_ref[2 * u : 2 * u + 1, :], w_ref[2 * u + 1 : 2 * u + 2, :]], axis=1)
         scaled = (w * att.astype(F32)).astype(BF16)
         left = jnp.concatenate([scaled[:, :TILE], blank], axis=1)
         right = jnp.concatenate([blank, scaled[:, TILE:]], axis=1)
@@ -151,13 +168,16 @@
             for g in range(1, copies):
                 start = h * knots + 8 * g
                 value = jnp.where(lane < g * knots, value, normal[start : start + 8])
-            slot = lax.rem(win_ref[2 * u + h], windows)
-            block = slot // own
-            device = lax.rem(block, chips) * CORES + block // chips
-            out_ref[device * own + lax.rem(slot, own)] += value
-        return carry
-
-    lax.fori_loop(0, w_ref.shape[0] // 2, pair, 0, unroll=True)
+            sums[lax.rem(win_ref[2 * u + h], windows)] += value
+
+
+def halves_kernel(sky_ref, keep_ref, got_ref, *refs):
+    outs, total = refs[:-1], refs[-1]
+    chip = sky_ref[0] // CORES
+    own = outs[0].shape[0]
+    total[...] = keep_ref[...] + got_ref[...]
+    for out_ref, mask in zip(outs, masks(len(outs))):
+        out_ref[...] = total[pl.ds((chip ^ mask) * own, own)]
 
 
 def solve_kernel(me_ref, sky_ref, *refs):
@@ -194,8 +214,8 @@
         result[i] = current * inverse[i]
         change_ref[i] = result[i]
     me, core = me_ref[0], lax.rem(sky_ref[0], CORES)
-    for k in range(peers):
-        rows_scr[me ^ k] = jnp.broadcast_to(blocks[k][MOMENTS, 0:1, :], (8, LANES))
+    for block, mask in zip(blocks, masks(peers)):
+        rows_scr[me ^ mask] = jnp.broadcast_to(block[MOMENTS, 0:1, :], (8, LANES))
     first, last = me == 0, me == peers - 1
     own = rows_scr[me]
     before = jnp.where(first, 0.0, rows_scr[jnp.maximum(me - 1, 0)])
@@ -216,12 +236,13 @@
     ties_ref[2] = placed(before, own, after)
 
 
-def invert_kernel(sky_ref, part_ref, ties_ref, out_ref, flat, cells):
-    devices, own, _, _ = part_ref.shape
+def invert_kernel(sky_ref, ties_ref, *refs):
+    parts, (out_ref, flat, cells) = refs[:-3], refs[-3:]
+    own = out_ref.shape[0]
     knots = math.isqrt(out_ref.shape[1] * LANES)
-    total = part_ref[0]
-    for s in range(1, devices):
-        total = total + part_ref[s]
+    total = parts[0][...]
+    for part in parts[1:]:
+        total = total + part[...]
     flat[...] = jnp.zeros_like(flat)
     flat[0 : own * 8, :] = total.reshape(own * 8, LANES)
     groups = LANES // knots
@@ -262,22 +283,26 @@
     out_ref[...] = flat[0 : own * 8, :].reshape(own, 8, LANES)
 
 
-def rhs_kernel(hi_count, me_ref, win_ref, src_ref, w_ref, r_ref, sp_ref, att_ref, sources_ref, *refs):
-    peers = len(refs) - 7
+def low_kernel(half, src_ref, out_ref):
+    for i in range(src_ref.shape[0]):
+        out_ref[:, i * TILE : (i + 1) * TILE] = low_one_hot(src_ref[i : i + 1, :], half, out_ref.shape[0])
+
+
+def rhs_kernel(hi_count, me_ref, win_ref, low_ref, src_ref, w_ref, r_ref, sp_ref, att_ref, sources_ref, *refs):
+    peers = len(refs) - 6
     blocks = refs[:peers]
-    new_ref, out_ref, changes, table, rhs, chosen, weighted = refs[peers:]
+    new_ref, out_ref, changes, table, chosen, weighted = refs[peers:]
     half = hi_count * LANES
-    low_count = rhs.shape[0]
     windows = LANES
     me = me_ref[0]
-    for k in range(peers):
-        changes[me ^ k] = blocks[k][...]
+    for block, mask in zip(blocks, masks(peers)):
+        changes[me ^ mask] = block[...]
     rows = blocks[0].shape[1]
     for j in range(peers):
         q, first = divmod(j * rows, hi_count)
         for p in range(PARAMS):
             value = changes[j, p]
-            for s, piece in enumerate(split_bf16(value, SPLITS)):
+            for s, piece in enumerate(split_bf16(value, LOOKUP_SPLITS)):
                 start = (s * PARAMS + p) * hi_count + first
                 table[start : start + rows, q * LANES : (q + 1) * LANES] = piece.astype(F32)
         for i in range(rows):
@@ -287,24 +312,24 @@
     lookup = table[...].astype(BF16)
 
     tiles = src_ref.shape[0]
-    for i in range(tiles):
-        rhs[:, i * TILE : (i + 1) * TILE] = low_one_hot(src_ref[i : i + 1, :], half, low_count)
-    chosen[...] = jnp.dot(lookup, rhs[...], preferred_element_type=F32)
+    window_ids = iota((windows, LANES), 0).astype(F32).astype(BF16)
+    chosen[...] = jnp.dot(lookup, low_ref[...], preferred_element_type=F32)
     for i in range(tiles):
         lanes = slice(i * TILE, (i + 1) * TILE)
         columns = sp_ref[:, lanes].astype(F32)
         model = jnp.zeros((hi_count, LANES), F32)
         for p in range(PARAMS):
             value = chosen[p * hi_count : (p + 1) * hi_count, lanes]
-            for s in range(1, SPLITS):
+            for s in range(1, LOOKUP_SPLITS):
                 start = (s * PARAMS + p) * hi_count
                 value = value + chosen[start : start + hi_count, lanes]
             model = model + value * columns[p : p + 1]
         here = iota((hi_count, LANES), 0) == high_digit(src_ref[i : i + 1, :], half)
         model = jnp.sum(jnp.where(here, model, 0.0), axis=0, keepdims=True)
         change = w_ref[i : i + 1, :] * (r_ref[i : i + 1, :] - model)
-        slot = lax.rem(win_ref[i], windows)
-        weighted[:, lanes] = jnp.where(iota((windows, LANES), 0) == slot, change, 0.0).astype(BF16)
+        slot = lax.rem(win_ref[i], windows).astype(F32).astype(BF16)
+        change = jnp.broadcast_to(change, (windows, LANES)).astype(BF16)
+        weighted[:, lanes] = jnp.where(window_ids == slot, change, jnp.zeros((), BF16))
     total = lax.dot_general(att_ref[...], weighted[...], NT, preferred_element_type=F32)
     out_ref[...] = total
 
@@ -337,8 +362,8 @@
     sides = parts[0][own:]
     for part in parts[1:]:
         sides = sides + part[own:]
-    for k in range(chips):
-        main_ref[pl.ds((chip ^ k) * own, own)] = parts[k][0:own]
+    for part, mask in zip(parts, masks(chips)):
+        main_ref[pl.ds((chip ^ mask) * own, own)] = part[0:own]
     main_ref[HALF:] = sides
     inner_ref[0:8] = main_ref[pl.ds((1 - core) * (HALF - 8), 8)]
     outer_ref[0:8] = main_ref[pl.ds(core * (HALF - 8), 8)]
@@ -418,21 +443,29 @@
     cell_rows = knots * knots // LANES
 
     def swapped(blocks):
-        out = [blocks[0]] + [None] * (peers - 1)
-        for k in sorted(range(1, peers), key=lambda k: (k < peers // 2, k)):
-            out[k] = lax.ppermute(blocks[k], "tm", [(i, i ^ k) for i in range(peers)])
-        return out
+        return [blocks[0]] + [
+            lax.ppermute(block, "tm", [(i, i ^ mask) for i in range(peers)])
+            for block, mask in zip(blocks[1:], masks(peers)[1:])
+        ]
 
     def other_core(x):
         return lax.ppermute(x, "sky", [(i, i ^ 1) for i in range(devices)])
 
+    def other_chips(blocks):
+        return [blocks[0]] + [
+            lax.ppermute(block, "sky", [(i, i ^ (CORES * mask)) for i in range(devices)])
+            for block, mask in zip(blocks[1:], masks(chips)[1:])
+        ]
+
     block = jax.ShapeDtypeStruct((MOMENTS + 1, rows, LANES), F32)
-    with jax.named_scope("moments"):
-        blocks = call(
-            functools.partial(moments_kernel, hi_count),
-            [block] * peers,
-            [smem()] + [pl.BlockSpec(memory_space=pl.ANY)] * 5,
+    half = jax.ShapeDtypeStruct((HALF, cell_rows, LANES), F32)
+    with jax.named_scope("sums"):
+        *blocks, keep, give = call(
+            functools.partial(sums_kernel, hi_count),
+            [block] * peers + [half] * 2,
+            [smem()] * 3 + [pl.BlockSpec(memory_space=pl.ANY)] * 6,
             [
+                pltpu.VMEM((windows, cell_rows, LANES), F32),
                 pltpu.VMEM((SPLITS * MOMENTS * hi_count, observations), BF16),
                 pltpu.VMEM((low_count, observations), BF16),
                 pltpu.VMEM((SPLITS * MOMENTS * hi_count, low_count), F32),
@@ -441,23 +474,31 @@
                 pltpu.VMEM(w.shape, F32),
                 pltpu.VMEM(r.shape, F32),
                 pltpu.VMEM(source_partials.shape, BF16),
+                pltpu.VMEM(attitude_partials.shape, BF16),
                 pltpu.VMEM((1, windows), F32),
-                pltpu.SemaphoreType.DMA((5,)),
+                pltpu.SemaphoreType.DMA((6,)),
             ],
-            micros=7.5,
+            micros=9,
             limit=60 * 1024 * 1024,
-        )(me, src, w, r, source_partials, coupling.reshape(1, windows))
-    blocks, tile_window = lax.optimization_barrier((blocks, tile_window))
+        )(me, sky, tile_window, src, w, r, source_partials, attitude_partials, coupling.reshape(1, windows))
+    blocks, after_sums = lax.optimization_barrier((blocks, src))
     blocks = swapped(blocks)
-    with jax.named_scope("normals"):
-        normals = call(
-            functools.partial(normals_kernel, chips),
-            jax.ShapeDtypeStruct((windows, cell_rows, LANES), F32),
+    with jax.named_scope("halves"):
+        parts = call(
+            halves_kernel,
+            [jax.ShapeDtypeStruct((own, cell_rows, LANES), F32)] * chips,
             [smem(), vmem(), vmem()],
-            micros=3,
-        )(tile_window, w, attitude_partials)
-    parts = lax.all_to_all(normals.reshape(devices, own, cell_rows, LANES), "sky", 0, 0, tiled=True)
-    _, blocks = lax.optimization_barrier((normals, blocks))
+            [pltpu.VMEM((HALF, cell_rows, LANES), F32)],
+        )(sky, keep, other_core(give))
+    with jax.named_scope("one_hot"):
+        low = call(
+            functools.partial(low_kernel, hi_count * LANES),
+            jax.ShapeDtypeStruct((low_count, observations), BF16),
+            [vmem()],
+            micros=1,
+        )(after_sums)
+    _, low, blocks = lax.optimization_barrier((parts, low, blocks))
+    parts = other_chips(parts)
     with jax.named_scope("solve"):
         change, ties = call(
             solve_kernel,
@@ -474,10 +515,10 @@
         inverse = call(
             invert_kernel,
             jax.ShapeDtypeStruct((own, cell_rows, LANES), F32),
-            [smem(), vmem(), vmem()],
+            [smem()] + [vmem()] * (1 + chips),
             [pltpu.VMEM((cell_rows * LANES, LANES), F32), pltpu.VMEM((knots * knots, LANES), F32)],
             micros=3,
-        )(sky, parts, ties)
+        )(sky, ties, *parts)
     inverse, changes = lax.optimization_barrier((inverse, changes))
     with jax.named_scope("right_sides"):
         new_sources, part = call(
@@ -486,16 +527,15 @@
                 jax.ShapeDtypeStruct(sources.shape, F32),
                 jax.ShapeDtypeStruct((knots, windows), F32),
             ],
-            [smem(), smem()] + [vmem()] * (6 + peers),
+            [smem(), smem()] + [vmem()] * (7 + peers),
             [
                 pltpu.VMEM((peers, PARAMS, rows, LANES), F32),
-                pltpu.VMEM((SPLITS * PARAMS * hi_count, low_count), F32),
-                pltpu.VMEM((low_count, observations), BF16),
-                pltpu.VMEM((SPLITS * PARAMS * hi_count, observations), F32),
+                pltpu.VMEM((LOOKUP_SPLITS * PARAMS * hi_count, low_count), F32),
+                pltpu.VMEM((LOOKUP_SPLITS * PARAMS * hi_count, observations), F32),
                 pltpu.VMEM((windows, observations), BF16),
             ],
             micros=6,
-        )(me, tile_window, src, w, r, source_partials, attitude_partials, sources, *changes)
+        )(me, tile_window, low, src, w, r, source_partials, attitude_partials, sources, *changes)
     with jax.named_scope("send"):
         sides = knots // 2 // 8
         sent = call(
@@ -503,9 +543,7 @@
             jax.ShapeDtypeStruct((own + sides, 8, LANES), F32),
             [smem()] + [vmem()] * 3,
         )(sky, inverse, part, other_core(part))
-    got = [sent] + [
-        lax.ppermute(sent, "sky", [(i, i ^ (CORES * k)) for i in range(devices)]) for k in range(1, chips)
-    ]
+    got = other_chips([sent] * chips)
     with jax.named_scope("rims"):
         rim = jax.ShapeDtypeStruct((8 + sides, 8, LANES), F32)
         inner, outer, main = call(

time: 54.1 us -> 50.6 us (0.935)
  waiting for transfers between devices: 10.6 us -> 8.9 us
  Pallas kernels: 19.4 us -> 17.9 us
    all_to_all x1 -> x0, waiting for transfers between devices: 4.47 us -> none  [on_device(): lax.all_to_all(normals.reshape(devices, own, cell_rows, LANES), 'sky', 0,...]
    all_to_all x1 -> x0, starting transfers between devices: 4.06 us -> none  [on_device(): lax.all_to_all(normals.reshape(devices, own, cell_rows, LANES), 'sky', 0,...]
    ppermute x9 -> x12, starting transfers between devices: 13.6 us -> 16.8 us  [the longest x6 9.75 us: swapped(): lax.ppermute(block, 'tm', [(i, i ^ mask) for i in range(peers)])]
    ppermute x9 -> x12, waiting for transfers between devices: 3.6 us -> 6.34 us  [the longest x6 3.82 us: other_chips(): lax.ppermute(block, 'sky', [(i, i ^ CORES * mask) for i in range(devices)])]
    pallas_call x1, Pallas kernels: 4.21 us -> 3.2 us  [on_device(): call(functools.partial(rhs_kernel, hi_count), [jax.ShapeDtypeStruct(sourc...]
    ppermute x3 -> x4, starting transfers between devices: 4.73 us -> 5.25 us  [other_core(): return lax.ppermute(x, 'sky', [(i, i ^ 1) for i in range(devices)])]
    pallas_call x2 -> x3, Pallas kernels: 10.2 us -> 9.7 us  [the longest x1 8.43 us: on_device(): call(functools.partial(sums_kernel, hi_count), [block] * peers + [half] *...]
    ppermute x3 -> x4, waiting for transfers between devices: 2.55 us -> 2.56 us  [other_core(): return lax.ppermute(x, 'sky', [(i, i ^ 1) for i in range(devices)])]
  transfers between devices with their start and end apart: 14 -> 17, of which waited for: 8 -> 7; matrix products, arithmetic and copies ran while one was open for 0% -> 0% of each run, Pallas kernels for 10% -> 9%
where the time goes in v4:
time: 50.6 us; the launch traced here: 50.4 us
  starting transfers between devices  22.7 us (45%)
  Pallas kernels  17.9 us (35%)
  waiting for transfers between devices  8.9 us (18%)
  between operations  0.86 us (2%)
    ppermute x6, starting transfers between devices, swapped(): lax.ppermute(block, 'tm', [(i, i ^ mask) for i in range(peers)])  9.75 us
    pallas_call x1, Pallas kernels, on_device(): call(functools.partial(sums_kernel, hi_count), [block] * peers + [half] *...  8.43 us
    ppermute x6, starting transfers between devices, other_chips(): lax.ppermute(block, 'sky', [(i, i ^ CORES * mask) for i in range(devices)])  7.04 us
    ppermute x4, starting transfers between devices, other_core(): return lax.ppermute(x, 'sky', [(i, i ^ 1) for i in range(devices)])  5.25 us
    ppermute x6, waiting for transfers between devices, other_chips(): lax.ppermute(block, 'sky', [(i, i ^ CORES * mask) for i in range(devices)])  3.82 us
    pallas_call x1, Pallas kernels, on_device(): call(functools.partial(rhs_kernel, hi_count), [jax.ShapeDtypeStruct(sourc...  3.2 us
    pallas_call x1, Pallas kernels, on_device(): call(invert_kernel, jax.ShapeDtypeStruct((own, cell_rows, LANES), F32), [...  2.89 us
    ppermute x4, waiting for transfers between devices, other_core(): return lax.ppermute(x, 'sky', [(i, i ^ 1) for i in range(devices)])  2.56 us
  transfers between devices with their start and end apart: 17, of which 7 were waited for; matrix products, arithmetic and copies ran while one was open for 0% of the time, Pallas kernels for 9%

profile of v4, /device:TPU:0, one launch (start us, length us, event | category | flops | bytes accessed | tf_op | source)
XLA Modules:
  0.0 50.4 jit_solution(9233023607522853986)
XLA Ops:
  0.6 0.0 copy-start.1
  0.6 8.4 %sums.1 = (f32[21,8,128]{2,1,0:T(8,128)}, f32[21,8,128]{2,1,0:T(8,128)}, f32[21,8,128]{2,1,0:T(8,128)}, f32[21,8,128]{2,1,0:T(8,128)}, f32[64,8,128]{2,1,0:T(8,128)}, /*index=5*/f32[64,8,128]{2,1,0:T(8,128)}) custom-call(s32[1]{0:T(128)} %bitcast.me_ref, s32[1]{0:T(128)} %bitcast.1.sky_ref, s32[64]{0:T(128)} %win_ref.3, s32[64,128]{1,0:T(8,128)} %bitcast.8, ...), custom_call_target="tpu_custom_call" | custom-call | flops 8999999488 | tf_op jit(solution)/shard_map/sums/pallas_call | solution.py:463
  9.1 0.0 copy-start
  9.1 0.0 copy-start.9
  9.1 0.5 %collective-permute-start = (f32[64,8,128]{2,1,0:T(8,128)}, f32[64,8,128]{2,1,0:T(8,128)S(1)}, u32[]{:S(2)}, u32[]{:S(2)}) collective-permute-start(f32[64,8,128]{2,1,0:T(8,128)} %get-tuple-element.35), channel_id=1, source_target_pairs={{0,4},{4,0},{8,12},{12,8},{16,20},{20,16},{24,28},{28,24},{1,5},{5... | collective-permute-start | bytes 786440 | tf_op jit(solution)/shard_map/halves/ppermute | solution.py:452
  9.6 4.7 %collective-permute-start.1 = (f32[21,8,128]{2,1,0:T(8,128)}, f32[21,8,128]{2,1,0:T(8,128)S(1)}, u32[]{:S(2)}, u32[]{:S(2)}) collective-permute-start(f32[21,8,128]{2,1,0:T(8,128)} %get-tuple-element.46), channel_id=1, source_target_pairs={{0,3},{1,2},{2,1},{3,0},{4,7},{5,6},{6,5},{7,4},{8,11},{9,10},{10,... | collective-permute-start | bytes 258056 | tf_op jit(solution)/shard_map/ppermute | solution.py:447
  14.3 0.0 collective-permute-start.2
  14.3 0.7 %collective-permute-start.3 = (f32[21,8,128]{2,1,0:T(8,128)}, f32[21,8,128]{2,1,0:T(8,128)S(1)}, u32[]{:S(2)}, u32[]{:S(2)}) collective-permute-start(f32[21,8,128]{2,1,0:T(8,128)} %get-tuple-element.48), channel_id=1, source_target_pairs={{0,1},{1,0},{2,3},{3,2},{4,5},{5,4},{6,7},{7,6},{8,9},{9,8},{10,11... | collective-permute-start | bytes 258056 | tf_op jit(solution)/shard_map/ppermute | solution.py:447
  15.0 0.0 copy-done.1
  15.0 1.2 %one_hot.1.low_ref = bf16[256,8192]{1,0:T(8,128)(2,1)S(1)} custom-call(s32[64,128]{1,0:T(8,128)S(1)} %bitcast.9), custom_call_target="tpu_custom_call" | custom-call | flops 1000000000 | tf_op jit(solution)/shard_map/one_hot/pallas_call | solution.py:494
  16.2 0.0 collective-permute-done.got_ref
  16.2 0.0 copy-done
  16.2 0.1 halves.1
  16.3 2.6 %collective-permute-start.4 = (f32[16,8,128]{2,1,0:T(8,128)S(1)}, f32[16,8,128]{2,1,0:T(8,128)S(1)}, u32[]{:S(2)}, u32[]{:S(2)}) collective-permute-start(f32[16,8,128]{2,1,0:T(8,128)S(1)} %get-tuple-element.37), channel_id=1, source_target_pairs={{0,24},{4,28},{8,16},{12,20},{16,8},{20,12},{24,0},{28,4},{1,25},{... | collective-permute-start | bytes 196616 | tf_op jit(solution)/shard_map/ppermute | solution.py:456
  18.9 0.5 %collective-permute-start.5 = (f32[16,8,128]{2,1,0:T(8,128)S(1)}, f32[16,8,128]{2,1,0:T(8,128)S(1)}, u32[]{:S(2)}, u32[]{:S(2)}) collective-permute-start(f32[16,8,128]{2,1,0:T(8,128)S(1)} %get-tuple-element.38), channel_id=1, source_target_pairs={{0,16},{4,20},{8,24},{12,28},{16,0},{20,4},{24,8},{28,12},{1,17},{... | collective-permute-start | bytes 196616 | tf_op jit(solution)/shard_map/ppermute | solution.py:456
  19.4 0.0 collective-permute-done.1.refs_1_
  19.4 0.4 collective-permute-start.6
  19.8 2.5 %collective-permute-done.2.refs_2_ = f32[21,8,128]{2,1,0:T(8,128)S(1)} collective-permute-done((f32[21,8,128]{2,1,0:T(8,128)}, f32[21,8,128]{2,1,0:T(8,128)S(1)}, u32[]{:S(2)}, u32[]{:S(2)}) %collective-permute-start.2) | collective-permute-done | bytes 86048 | tf_op jit(solution)/shard_map/ppermute | solution.py:447
  22.3 0.0 collective-permute-done.3.refs_3_
  22.3 0.0 copy-done.9
  22.3 0.2 solve.1
  22.5 2.5 %collective-permute-start.7 = (f32[5,8,128]{2,1,0:T(8,128)S(1)}, f32[5,8,128]{2,1,0:T(8,128)S(1)}, u32[]{:S(2)}, u32[]{:S(2)}) collective-permute-start(f32[5,8,128]{2,1,0:T(8,128)S(1)} %get-tuple-element.56.refs_0_), channel_id=1, source_target_pairs={{0,3},{1,2},{2,1},{3,0},{4,7},{5,6},{6,5},{7,4},{8,11},{9,10},{10,... | collective-permute-start | bytes 61448 | tf_op jit(solution)/shard_map/ppermute | solution.py:447
  25.0 0.0 collective-permute-start.8
  25.0 0.0 collective-permute-done.4.refs_1_
  25.0 1.9 %collective-permute-start.9 = (f32[5,8,128]{2,1,0:T(8,128)S(1)}, f32[5,8,128]{2,1,0:T(8,128)S(1)}, u32[]{:S(2)}, u32[]{:S(2)}) collective-permute-start(f32[5,8,128]{2,1,0:T(8,128)S(1)} %get-tuple-element.56.refs_0_), channel_id=1, source_target_pairs={{0,1},{1,0},{2,3},{3,2},{4,5},{5,4},{6,7},{7,6},{8,9},{9,8},{10,11... | collective-permute-start | bytes 61448 | tf_op jit(solution)/shard_map/ppermute | solution.py:447
  26.9 0.0 collective-permute-done.5.refs_2_
  26.9 0.0 collective-permute-done.6.refs_3_
  26.9 0.0 copy-start.2
  26.9 0.0 copy-start.3
  26.9 0.0 copy-start.4
  26.9 0.0 copy-start.5
  27.0 0.0 copy-start.6
  27.0 0.0 copy-start.8
  27.0 2.9 %invert.1.inv_ref = f32[16,8,128]{2,1,0:T(8,128)S(1)} custom-call(s32[1]{0:T(128)} %bitcast.1.sky_ref, f32[3,8,128]{2,1,0:T(8,128)S(1)} %get-tuple-element.54.ties_ref, f32[16,8,128]{2,1,0:T(8,128)S(1)} %get-tuple-element.36.refs_0_, f32[16,8,128]{2,1,0:T(8,128)S(1)} %collective-permute-done.4.refs_1_, f32[16,8,128]{2,1,0:T(8,128)S(1)} %collective-permute-done.5.refs_2_, ...), custom_call_target="tpu_custom_call" | custom-call | flops 3000000000 | tf_op jit(solution)/shard_map/invert/pallas_call | solution.py:515
  29.9 0.0 collective-permute-done.7.refs_1_
  29.9 0.0 collective-permute-done.8.refs_2_
  29.9 0.0 collective-permute-done.9.refs_3_
  29.9 0.0 copy-done.2
  29.9 0.0 copy-done.3
  29.9 0.0 copy-done.4
  29.9 0.0 copy-done.5
  30.0 0.0 copy-done.6
  30.0 0.0 copy-done.8
  30.0 3.2 %right_sides.1 = (f32[5,4096]{1,0:T(8,128)}, f32[32,128]{1,0:T(8,128)S(1)}) custom-call(s32[1]{0:T(128)} %bitcast.me_ref, s32[64]{0:T(128)S(1)} %copy-done.8, bf16[256,8192]{1,0:T(8,128)(2,1)S(1)} %one_hot.1.low_ref, s32[64,128]{1,0:T(8,128)S(1)} %bitcast.10, f32[64,128]{1,0:T(8,128)S(1)} %bitcast.12, f32[64,128]{1,0:T(8,128)S(1)} %bitcast.14, ...), custom_call_target="tpu_custom_call" | custom-call | flops 6000000000 | tf_op jit(solution)/shard_map/right_sides/pallas_call | solution.py:524
  33.2 0.0 copy-start.7
  33.2 0.0 collective-permute-start.10
  33.2 1.2 %collective-permute-done.10.theirs_ref = f32[32,128]{1,0:T(8,128)S(1)} collective-permute-done((f32[32,128]{1,0:T(8,128)S(1)}, f32[32,128]{1,0:T(8,128)S(1)}, u32[]{:S(2)}, u32[]{:S(2)}) %collective-permute-start.10) | collective-permute-done | bytes 16416 | tf_op jit(solution)/shard_map/send/ppermute | solution.py:452
  34.4 0.1 send.1.refs_0_
  34.5 2.4 %collective-permute-start.11 = (f32[18,8,128]{2,1,0:T(8,128)S(1)}, f32[18,8,128]{2,1,0:T(8,128)S(1)}, u32[]{:S(2)}, u32[]{:S(2)}) collective-permute-start(f32[18,8,128]{2,1,0:T(8,128)S(1)} %send.1.refs_0_), channel_id=1, source_target_pairs={{0,24},{4,28},{8,16},{12,20},{16,8},{20,12},{24,0},{28,4},{1,25},{... | collective-permute-start | bytes 221192 | tf_op jit(solution)/shard_map/ppermute | solution.py:456
  36.9 0.5 %collective-permute-start.12 = (f32[18,8,128]{2,1,0:T(8,128)S(1)}, f32[18,8,128]{2,1,0:T(8,128)S(1)}, u32[]{:S(2)}, u32[]{:S(2)}) collective-permute-start(f32[18,8,128]{2,1,0:T(8,128)S(1)} %send.1.refs_0_), channel_id=1, source_target_pairs={{0,16},{4,20},{8,24},{12,28},{16,0},{20,4},{24,8},{28,12},{1,17},{... | collective-permute-start | bytes 221192 | tf_op jit(solution)/shard_map/ppermute | solution.py:456
  37.5 0.5 %collective-permute-start.13 = (f32[18,8,128]{2,1,0:T(8,128)S(1)}, f32[18,8,128]{2,1,0:T(8,128)S(1)}, u32[]{:S(2)}, u32[]{:S(2)}) collective-permute-start(f32[18,8,128]{2,1,0:T(8,128)S(1)} %send.1.refs_0_), channel_id=1, source_target_pairs={{0,8},{4,12},{8,0},{12,4},{16,24},{20,28},{24,16},{28,20},{1,9},{5... | collective-permute-start | bytes 221192 | tf_op jit(solution)/shard_map/ppermute | solution.py:456
  38.0 1.8 %collective-permute-done.11.refs_1_ = f32[18,8,128]{2,1,0:T(8,128)S(1)} collective-permute-done((f32[18,8,128]{2,1,0:T(8,128)S(1)}, f32[18,8,128]{2,1,0:T(8,128)S(1)}, u32[]{:S(2)}, u32[]{:S(2)}) %collective-permute-start.11) | collective-permute-done | bytes 73760 | tf_op jit(solution)/shard_map/ppermute | solution.py:456
  39.8 1.5 %collective-permute-done.12.refs_2_ = f32[18,8,128]{2,1,0:T(8,128)S(1)} collective-permute-done((f32[18,8,128]{2,1,0:T(8,128)S(1)}, f32[18,8,128]{2,1,0:T(8,128)S(1)}, u32[]{:S(2)}, u32[]{:S(2)}) %collective-permute-start.12) | collective-permute-done | bytes 73760 | tf_op jit(solution)/shard_map/ppermute | solution.py:456
  41.3 0.5 collective-permute-done.13.refs_3_
  41.8 0.1 collective-permute-start.14
  41.9 0.7 %collective-permute-start.15 = (f32[10,8,128]{2,1,0:T(8,128)S(1)}, f32[10,8,128]{2,1,0:T(8,128)S(1)}, u32[]{:S(2)}, u32[]{:S(2)}) collective-permute-start(f32[10,8,128]{2,1,0:T(8,128)S(1)} %get-tuple-element.65), channel_id=1, source_target_pairs={{4,1},{5,2},{6,3},{12,9},{13,10},{14,11},{20,17},{21,18},{22,19},{... | collective-permute-start | bytes 122888 | tf_op jit(solution)/shard_map/ppermute | solution.py:556
  42.6 0.5 %collective-permute-done.14.inner_ref = f32[10,8,128]{2,1,0:T(8,128)S(1)} collective-permute-done((f32[10,8,128]{2,1,0:T(8,128)S(1)}, f32[10,8,128]{2,1,0:T(8,128)S(1)}, u32[]{:S(2)}, u32[]{:S(2)}) %collective-permute-start.14) | collective-permute-done | bytes 40992 | tf_op jit(solution)/shard_map/ppermute | solution.py:452
  43.1 0.0 collective-permute-done.15.outer_ref
  43.1 1.1 %sweeps.1.mine_ref = f32[32,128]{1,0:T(8,128)S(1)} custom-call(s32[1]{0:T(128)} %bitcast.1.sky_ref, f32[66,8,128]{2,1,0:T(8,128)S(1)} %get-tuple-element.63.main_ref, f32[10,8,128]{2,1,0:T(8,128)S(1)} %collective-permute-done.14.inner_ref, f32[10,8,128]{2,1,0:T(8,128)S(1)} %collective-permute-done.15.outer_ref, f32[3,8,128]{2,1,0:T(8,128)S(1)} %get-tuple-element.54.ties_ref), custom_call_target="tpu_custom_call" | custom-call | flops 1000000000 | tf_op jit(solution)/shard_map/sweeps/pallas_call | solution.py:559
  44.2 4.7 %collective-permute-start.16 = (f32[32,128]{1,0:T(8,128)S(1)}, f32[32,128]{1,0:T(8,128)S(1)}, u32[]{:S(2)}, u32[]{:S(2)}) collective-permute-start(f32[32,128]{1,0:T(8,128)S(1)} %sweeps.1.mine_ref), channel_id=1, source_target_pairs={{0,4},{4,0},{8,12},{12,8},{16,20},{20,16},{24,28},{28,24},{1,5},{5... | collective-permute-start | bytes 49160 | tf_op jit(solution)/shard_map/finish/ppermute | solution.py:452
  48.9 0.8 %collective-permute-done.16.theirs_ref = f32[32,128]{1,0:T(8,128)S(1)} collective-permute-done((f32[32,128]{1,0:T(8,128)S(1)}, f32[32,128]{1,0:T(8,128)S(1)}, u32[]{:S(2)}, u32[]{:S(2)}) %collective-permute-start.16) | collective-permute-done | bytes 16416 | tf_op jit(solution)/shard_map/finish/ppermute | solution.py:452
  49.7 0.0 copy-done.7
  49.7 0.7 %finish.1 = f32[32,128]{1,0:T(8,128)} custom-call(s32[1]{0:T(128)} %bitcast.1.sky_ref, f32[32,128]{1,0:T(8,128)S(1)} %sweeps.1.mine_ref, f32[32,128]{1,0:T(8,128)S(1)} %collective-permute-done.16.theirs_ref, f32[32,128]{1,0:T(8,128)S(1)} %bitcast.15), custom_call_target="tpu_custom_call" | custom-call | flops 100000000 | tf_op jit(solution)/shard_map/finish/pallas_call | solution.py:571
  (1 shorter events, 0.0 us)
Async XLA Ops:
  0.6 14.3 %copy-start.1 = (s32[8192]{0:T(1024)S(1)}, s32[8192]{0:T(1024)}, u32[]{:S(2)}) copy-start(s32[8192]{0:T(1024)} %param.13) | copy-start | bytes 98308
  9.1 7.1 %copy-start = (f32[64,8,128]{2,1,0:T(8,128)S(1)}, f32[64,8,128]{2,1,0:T(8,128)}, u32[]{:S(2)}) copy-start(f32[64,8,128]{2,1,0:T(8,128)} %get-tuple-element.34.keep_ref) | copy-start | bytes 786436
  9.1 13.2 %copy-start.9 = (f32[21,8,128]{2,1,0:T(8,128)S(1)}, f32[21,8,128]{2,1,0:T(8,128)}, u32[]{:S(2)}) copy-start(f32[21,8,128]{2,1,0:T(8,128)} %get-tuple-element.50.refs_0_) | copy-start | bytes 258052
  9.1 7.1 %collective-permute-start = (f32[64,8,128]{2,1,0:T(8,128)}, f32[64,8,128]{2,1,0:T(8,128)S(1)}, u32[]{:S(2)}, u32[]{:S(2)}) collective-permute-start(f32[64,8,128]{2,1,0:T(8,128)} %get-tuple-element.35), channel_id=1, source_target_pairs={{0,4},{4,0},{8,12},{12,8},{16,20},{20,16},{24,28},{28,24},{1,5},{5... | collective-permute-start | bytes 786440 | tf_op jit(solution)/shard_map/halves/ppermute | solution.py:452
  9.6 9.8 %collective-permute-start.1 = (f32[21,8,128]{2,1,0:T(8,128)}, f32[21,8,128]{2,1,0:T(8,128)S(1)}, u32[]{:S(2)}, u32[]{:S(2)}) collective-permute-start(f32[21,8,128]{2,1,0:T(8,128)} %get-tuple-element.46), channel_id=1, source_target_pairs={{0,3},{1,2},{2,1},{3,0},{4,7},{5,6},{6,5},{7,4},{8,11},{9,10},{10,... | collective-permute-start | bytes 258056 | tf_op jit(solution)/shard_map/ppermute | solution.py:447
  14.3 8.0 %collective-permute-start.2 = (f32[21,8,128]{2,1,0:T(8,128)}, f32[21,8,128]{2,1,0:T(8,128)S(1)}, u32[]{:S(2)}, u32[]{:S(2)}) collective-permute-start(f32[21,8,128]{2,1,0:T(8,128)} %get-tuple-element.47), channel_id=1, source_target_pairs={{0,2},{1,3},{2,0},{3,1},{4,6},{5,7},{6,4},{7,5},{8,10},{9,11},{10,... | collective-permute-start | bytes 258056 | tf_op jit(solution)/shard_map/ppermute | solution.py:447
  14.3 8.0 %collective-permute-start.3 = (f32[21,8,128]{2,1,0:T(8,128)}, f32[21,8,128]{2,1,0:T(8,128)S(1)}, u32[]{:S(2)}, u32[]{:S(2)}) collective-permute-start(f32[21,8,128]{2,1,0:T(8,128)} %get-tuple-element.48), channel_id=1, source_target_pairs={{0,1},{1,0},{2,3},{3,2},{4,5},{5,4},{6,7},{7,6},{8,9},{9,8},{10,11... | collective-permute-start | bytes 258056 | tf_op jit(solution)/shard_map/ppermute | solution.py:447
  16.3 8.7 %collective-permute-start.4 = (f32[16,8,128]{2,1,0:T(8,128)S(1)}, f32[16,8,128]{2,1,0:T(8,128)S(1)}, u32[]{:S(2)}, u32[]{:S(2)}) collective-permute-start(f32[16,8,128]{2,1,0:T(8,128)S(1)} %get-tuple-element.37), channel_id=1, source_target_pairs={{0,24},{4,28},{8,16},{12,20},{16,8},{20,12},{24,0},{28,4},{1,25},{... | collective-permute-start | bytes 196616 | tf_op jit(solution)/shard_map/ppermute | solution.py:456
  18.9 8.0 %collective-permute-start.5 = (f32[16,8,128]{2,1,0:T(8,128)S(1)}, f32[16,8,128]{2,1,0:T(8,128)S(1)}, u32[]{:S(2)}, u32[]{:S(2)}) collective-permute-start(f32[16,8,128]{2,1,0:T(8,128)S(1)} %get-tuple-element.38), channel_id=1, source_target_pairs={{0,16},{4,20},{8,24},{12,28},{16,0},{20,4},{24,8},{28,12},{1,17},{... | collective-permute-start | bytes 196616 | tf_op jit(solution)/shard_map/ppermute | solution.py:456
  19.4 7.5 %collective-permute-start.6 = (f32[16,8,128]{2,1,0:T(8,128)S(1)}, f32[16,8,128]{2,1,0:T(8,128)S(1)}, u32[]{:S(2)}, u32[]{:S(2)}) collective-permute-start(f32[16,8,128]{2,1,0:T(8,128)S(1)} %get-tuple-element.39), channel_id=1, source_target_pairs={{0,8},{4,12},{8,0},{12,4},{16,24},{20,28},{24,16},{28,20},{1,9},{5... | collective-permute-start | bytes 196616 | tf_op jit(solution)/shard_map/ppermute | solution.py:456
  22.5 7.4 %collective-permute-start.7 = (f32[5,8,128]{2,1,0:T(8,128)S(1)}, f32[5,8,128]{2,1,0:T(8,128)S(1)}, u32[]{:S(2)}, u32[]{:S(2)}) collective-permute-start(f32[5,8,128]{2,1,0:T(8,128)S(1)} %get-tuple-element.56.refs_0_), channel_id=1, source_target_pairs={{0,3},{1,2},{2,1},{3,0},{4,7},{5,6},{6,5},{7,4},{8,11},{9,10},{10,... | collective-permute-start | bytes 61448 | tf_op jit(solution)/shard_map/ppermute | solution.py:447
  25.0 4.9 %collective-permute-start.8 = (f32[5,8,128]{2,1,0:T(8,128)S(1)}, f32[5,8,128]{2,1,0:T(8,128)S(1)}, u32[]{:S(2)}, u32[]{:S(2)}) collective-permute-start(f32[5,8,128]{2,1,0:T(8,128)S(1)} %get-tuple-element.56.refs_0_), channel_id=1, source_target_pairs={{0,2},{1,3},{2,0},{3,1},{4,6},{5,7},{6,4},{7,5},{8,10},{9,11},{10,... | collective-permute-start | bytes 61448 | tf_op jit(solution)/shard_map/ppermute | solution.py:447
  25.0 4.9 %collective-permute-start.9 = (f32[5,8,128]{2,1,0:T(8,128)S(1)}, f32[5,8,128]{2,1,0:T(8,128)S(1)}, u32[]{:S(2)}, u32[]{:S(2)}) collective-permute-start(f32[5,8,128]{2,1,0:T(8,128)S(1)} %get-tuple-element.56.refs_0_), channel_id=1, source_target_pairs={{0,1},{1,0},{2,3},{3,2},{4,5},{5,4},{6,7},{7,6},{8,9},{9,8},{10,11... | collective-permute-start | bytes 61448 | tf_op jit(solution)/shard_map/ppermute | solution.py:447
  26.9 3.0 %copy-start.2 = (bf16[32,8192]{1,0:T(8,128)(2,1)S(1)}, bf16[32,8192]{1,0:T(8,128)(2,1)}, u32[]{:S(2)}) copy-start(bf16[32,8192]{1,0:T(8,128)(2,1)} %att_ref.1) | copy-start | bytes 1572868
  26.9 3.0 %copy-start.3 = (bf16[5,8192]{1,0:T(8,128)(2,1)S(1)}, bf16[5,8192]{1,0:T(8,128)(2,1)}, u32[]{:S(2)}) copy-start(bf16[5,8192]{1,0:T(8,128)(2,1)} %sp_ref.1) | copy-start | bytes 245764
  26.9 3.0 %copy-start.4 = (f32[5,4096]{1,0:T(8,128)S(1)}, f32[5,4096]{1,0:T(8,128)}, u32[]{:S(2)}) copy-start(f32[5,4096]{1,0:T(8,128)} %sources_ref.1) | copy-start | bytes 245764
  26.9 3.0 %copy-start.5 = (f32[8192]{0:T(1024)S(1)}, f32[8192]{0:T(1024)}, u32[]{:S(2)}) copy-start(f32[8192]{0:T(1024)} %param.10) | copy-start | bytes 98308
  27.0 3.0 %copy-start.6 = (f32[8192]{0:T(1024)S(1)}, f32[8192]{0:T(1024)}, u32[]{:S(2)}) copy-start(f32[8192]{0:T(1024)} %param.9) | copy-start | bytes 98308
  27.0 3.0 %copy-start.8 = (s32[64]{0:T(128)S(1)}, s32[64]{0:T(128)}, u32[]{:S(2)}) copy-start(s32[64]{0:T(128)} %win_ref.3) | copy-start | bytes 772
  33.2 16.5 %copy-start.7 = (f32[128,32]{0,1:T(8,128)S(1)}, f32[128,32]{0,1:T(8,128)}, u32[]{:S(2)}) copy-start(f32[128,32]{0,1:T(8,128)} %param.16) | copy-start | bytes 49156
  33.2 1.2 %collective-permute-start.10 = (f32[32,128]{1,0:T(8,128)S(1)}, f32[32,128]{1,0:T(8,128)S(1)}, u32[]{:S(2)}, u32[]{:S(2)}) collective-permute-start(f32[32,128]{1,0:T(8,128)S(1)} %get-tuple-element.62.mine_ref), channel_id=1, source_target_pairs={{0,4},{4,0},{8,12},{12,8},{16,20},{20,16},{24,28},{28,24},{1,5},{5... | collective-permute-start | bytes 49160 | tf_op jit(solution)/shard_map/send/ppermute | solution.py:452
  34.5 5.3 %collective-permute-start.11 = (f32[18,8,128]{2,1,0:T(8,128)S(1)}, f32[18,8,128]{2,1,0:T(8,128)S(1)}, u32[]{:S(2)}, u32[]{:S(2)}) collective-permute-start(f32[18,8,128]{2,1,0:T(8,128)S(1)} %send.1.refs_0_), channel_id=1, source_target_pairs={{0,24},{4,28},{8,16},{12,20},{16,8},{20,12},{24,0},{28,4},{1,25},{... | collective-permute-start | bytes 221192 | tf_op jit(solution)/shard_map/ppermute | solution.py:456
  36.9 4.4 %collective-permute-start.12 = (f32[18,8,128]{2,1,0:T(8,128)S(1)}, f32[18,8,128]{2,1,0:T(8,128)S(1)}, u32[]{:S(2)}, u32[]{:S(2)}) collective-permute-start(f32[18,8,128]{2,1,0:T(8,128)S(1)} %send.1.refs_0_), channel_id=1, source_target_pairs={{0,16},{4,20},{8,24},{12,28},{16,0},{20,4},{24,8},{28,12},{1,17},{... | collective-permute-start | bytes 221192 | tf_op jit(solution)/shard_map/ppermute | solution.py:456
  37.5 4.4 %collective-permute-start.13 = (f32[18,8,128]{2,1,0:T(8,128)S(1)}, f32[18,8,128]{2,1,0:T(8,128)S(1)}, u32[]{:S(2)}, u32[]{:S(2)}) collective-permute-start(f32[18,8,128]{2,1,0:T(8,128)S(1)} %send.1.refs_0_), channel_id=1, source_target_pairs={{0,8},{4,12},{8,0},{12,4},{16,24},{20,28},{24,16},{28,20},{1,9},{5... | collective-permute-start | bytes 221192 | tf_op jit(solution)/shard_map/ppermute | solution.py:456
  41.8 1.3 %collective-permute-start.14 = (f32[10,8,128]{2,1,0:T(8,128)S(1)}, f32[10,8,128]{2,1,0:T(8,128)S(1)}, u32[]{:S(2)}, u32[]{:S(2)}) collective-permute-start(f32[10,8,128]{2,1,0:T(8,128)S(1)} %get-tuple-element.64), channel_id=1, source_target_pairs={{0,4},{4,0},{8,12},{12,8},{16,20},{20,16},{24,28},{28,24},{1,5},{5... | collective-permute-start | bytes 122888 | tf_op jit(solution)/shard_map/ppermute | solution.py:452
  41.9 1.2 %collective-permute-start.15 = (f32[10,8,128]{2,1,0:T(8,128)S(1)}, f32[10,8,128]{2,1,0:T(8,128)S(1)}, u32[]{:S(2)}, u32[]{:S(2)}) collective-permute-start(f32[10,8,128]{2,1,0:T(8,128)S(1)} %get-tuple-element.65), channel_id=1, source_target_pairs={{4,1},{5,2},{6,3},{12,9},{13,10},{14,11},{20,17},{21,18},{22,19},{... | collective-permute-start | bytes 122888 | tf_op jit(solution)/shard_map/ppermute | solution.py:556
  44.2 5.5 %collective-permute-start.16 = (f32[32,128]{1,0:T(8,128)S(1)}, f32[32,128]{1,0:T(8,128)S(1)}, u32[]{:S(2)}, u32[]{:S(2)}) collective-permute-start(f32[32,128]{1,0:T(8,128)S(1)} %sweeps.1.mine_ref), channel_id=1, source_target_pairs={{0,4},{4,0},{8,12},{12,8},{16,20},{20,16},{24,28},{28,24},{1,5},{5... | collective-permute-start | bytes 49160 | tf_op jit(solution)/shard_map/finish/ppermute | solution.py:452

commit v5 on v4

--- a/solution.py
+++ b/solution.py
@@ -19,7 +19,6 @@
 CORES = 2
 HALF = LANES // CORES
 SPLITS = 2
-LOOKUP_SPLITS = 3
 ROWS = 8
 F32 = jnp.float32
 BF16 = jnp.bfloat16
@@ -288,10 +287,10 @@
         out_ref[:, i * TILE : (i + 1) * TILE] = low_one_hot(src_ref[i : i + 1, :], half, out_ref.shape[0])
 
 
-def rhs_kernel(hi_count, me_ref, win_ref, low_ref, src_ref, w_ref, r_ref, sp_ref, att_ref, sources_ref, *refs):
-    peers = len(refs) - 6
+def rhs_kernel(hi_count, me_ref, win_ref, low_ref, src_ref, w_ref, r_ref, sp_ref, att_ref, *refs):
+    peers = len(refs) - 5
     blocks = refs[:peers]
-    new_ref, out_ref, changes, table, chosen, weighted = refs[peers:]
+    out_ref, changes, table, chosen, weighted = refs[peers:]
     half = hi_count * LANES
     windows = LANES
     me = me_ref[0]
@@ -302,13 +301,9 @@
         q, first = divmod(j * rows, hi_count)
         for p in range(PARAMS):
             value = changes[j, p]
-            for s, piece in enumerate(split_bf16(value, LOOKUP_SPLITS)):
+            for s, piece in enumerate(split_bf16(value, SPLITS)):
                 start = (s * PARAMS + p) * hi_count + first
                 table[start : start + rows, q * LANES : (q + 1) * LANES] = piece.astype(F32)
-        for i in range(rows):
-            lanes = slice((j * rows + i) * LANES, (j * rows + i + 1) * LANES)
-            step = jnp.concatenate([changes[j, p, i : i + 1, :] for p in range(PARAMS)], axis=0)
-            new_ref[:, lanes] = sources_ref[:, lanes] + step
     lookup = table[...].astype(BF16)
 
     tiles = src_ref.shape[0]
@@ -320,7 +315,7 @@
         model = jnp.zeros((hi_count, LANES), F32)
         for p in range(PARAMS):
             value = chosen[p * hi_count : (p + 1) * hi_count, lanes]
-            for s in range(1, LOOKUP_SPLITS):
+            for s in range(1, SPLITS):
                 start = (s * PARAMS + p) * hi_count
                 value = value + chosen[start : start + hi_count, lanes]
             model = model + value * columns[p : p + 1]
@@ -332,6 +327,18 @@
         weighted[:, lanes] = jnp.where(window_ids == slot, change, jnp.zeros((), BF16))
     total = lax.dot_general(att_ref[...], weighted[...], NT, preferred_element_type=F32)
     out_ref[...] = total
+
+
+def update_kernel(me_ref, sources_ref, *refs):
+    blocks, (new_ref, changes) = refs[:-2], refs[-2:]
+    for block, mask in zip(blocks, masks(len(blocks))):
+        changes[me_ref[0] ^ mask] = block[...]
+    rows = blocks[0].shape[1]
+    for j in range(len(blocks)):
+        for i in range(rows):
+            lanes = slice((j * rows + i) * LANES, (j * rows + i + 1) * LANES)
+            step = jnp.concatenate([changes[j, p, i : i + 1, :] for p in range(PARAMS)], axis=0)
+            new_ref[:, lanes] = sources_ref[:, lanes] + step
 
 
 def send_kernel(sky_ref, inv_ref, mine_ref, theirs_ref, out_ref):
@@ -371,7 +378,7 @@
     outer_ref[8:] = sides
 
 
-def sweeps_kernel(sky_ref, main_ref, inner_ref, outer_ref, ties_ref, out_ref, flat, cells, vector):
+def sweeps_kernel(sky_ref, main_ref, outer_ref, inner_ref, ties_ref, out_ref, flat, cells, vector):
     knots = out_ref.shape[0]
     groups = LANES // knots
     core = lax.rem(sky_ref[0], CORES)
@@ -434,7 +441,8 @@
     hi_count = source_count // (2 * LANES)
     low_count = 2 * LANES
     me = lax.axis_index("tm").astype(jnp.int32).reshape(1)
-    sky = lax.axis_index("sky").astype(jnp.int32).reshape(1)
+    place = lax.axis_index("sky") ^ (lax.axis_index("tm") & 1)
+    sky = place.astype(jnp.int32).reshape(1)
     src = source_index.reshape(tiles, TILE)
     w = weights.reshape(tiles, TILE)
     r = residuals.reshape(tiles, TILE)
@@ -521,21 +529,26 @@
         )(sky, ties, *parts)
     inverse, changes = lax.optimization_barrier((inverse, changes))
     with jax.named_scope("right_sides"):
-        new_sources, part = call(
+        part = call(
             functools.partial(rhs_kernel, hi_count),
-            [
-                jax.ShapeDtypeStruct(sources.shape, F32),
-                jax.ShapeDtypeStruct((knots, windows), F32),
-            ],
-            [smem(), smem()] + [vmem()] * (7 + peers),
+            jax.ShapeDtypeStruct((knots, windows), F32),
+            [smem(), smem()] + [vmem()] * (6 + peers),
             [
                 pltpu.VMEM((peers, PARAMS, rows, LANES), F32),
-                pltpu.VMEM((LOOKUP_SPLITS * PARAMS * hi_count, low_count), F32),
-                pltpu.VMEM((LOOKUP_SPLITS * PARAMS * hi_count, observations), F32),
+                pltpu.VMEM((SPLITS * PARAMS * hi_count, low_count), F32),
+                pltpu.VMEM((SPLITS * PARAMS * hi_count, observations), F32),
                 pltpu.VMEM((windows, observations), BF16),
             ],
             micros=6,
-        )(me, tile_window, low, src, w, r, source_partials, attitude_partials, sources, *changes)
+        )(me, tile_window, low, src, w, r, source_partials, attitude_partials, *changes)
+    with jax.named_scope("update"):
+        changes, part = lax.optimization_barrier((changes, part))
+        new_sources = call(
+            update_kernel,
+            jax.ShapeDtypeStruct(sources.shape, F32),
+            [smem()] + [vmem()] * (1 + peers),
+            [pltpu.VMEM((peers, PARAMS, rows, LANES), F32)],
+        )(me, sources, *changes)
     with jax.named_scope("send"):
         sides = knots // 2 // 8
         sent = call(
@@ -551,8 +564,8 @@
             [rim, rim, jax.ShapeDtypeStruct((HALF + sides, 8, LANES), F32)],
             [smem()] + [vmem()] * chips,
         )(sky, *got)
-    upper = [(chip * CORES + 1) * peers + t for chip in range(chips) for t in range(peers - 1)]
-    lower = [chip * CORES * peers + t + 1 for chip in range(chips) for t in range(peers - 1)]
+    upper = [(chip * CORES + (1 ^ (t & 1))) * peers + t for chip in range(chips) for t in range(peers - 1)]
+    lower = [i + 1 for i in upper]
     outer = lax.ppermute(outer, ("sky", "tm"), list(zip(upper + lower, lower + upper)))
     inner = other_core(inner)
     with jax.named_scope("sweeps"):
@@ -566,7 +579,7 @@
                 pltpu.VMEM((knots, LANES), F32),
             ],
             micros=1,
-        )(sky, main, inner, outer, ties)
+        )(sky, main, outer, inner, ties)
     with jax.named_scope("finish"):
         new_attitude = call(
             finish_kernel,

time: 50.6 us -> 48.2 us (0.953); the launches traced: 50.4 us -> 47.3 us
  starting transfers between devices: 22.7 us -> 20.2 us
    ppermute x4, starting transfers between devices: 5.25 us -> 2.77 us  [other_core(): return lax.ppermute(x, 'sky', [(i, i ^ 1) for i in range(devices)])]
    pallas_call x1 -> x2, Pallas kernels: 3.2 us -> 3.01 us  [the longest x1 2.29 us: on_device(): call(functools.partial(rhs_kernel, hi_count), jax.ShapeDtypeStruct((knots...]
  transfers between devices with their start and end apart: 17 -> 17, of which waited for: 7 -> 7; matrix products, arithmetic and copies ran while one was open for 0% -> 0% of each run, Pallas kernels for 9% -> 11%
where the time goes in v5:
time: 48.2 us; the launch traced here: 47.3 us
  starting transfers between devices  20.2 us (42%)
  Pallas kernels  17.7 us (37%)
  waiting for transfers between devices  8.5 us (18%)
  between operations  0.86 us (2%)
    ppermute x6, starting transfers between devices, swapped(): lax.ppermute(block, 'tm', [(i, i ^ mask) for i in range(peers)])  9.75 us
    pallas_call x1, Pallas kernels, on_device(): call(functools.partial(sums_kernel, hi_count), [block] * peers + [half] *...  8.42 us
    ppermute x6, starting transfers between devices, other_chips(): lax.ppermute(block, 'sky', [(i, i ^ CORES * mask) for i in range(devices)])  7.04 us
    ppermute x6, waiting for transfers between devices, other_chips(): lax.ppermute(block, 'sky', [(i, i ^ CORES * mask) for i in range(devices)])  3.82 us
    pallas_call x1, Pallas kernels, on_device(): call(invert_kernel, jax.ShapeDtypeStruct((own, cell_rows, LANES), F32), [...  2.89 us
    ppermute x4, starting transfers between devices, other_core(): return lax.ppermute(x, 'sky', [(i, i ^ 1) for i in range(devices)])  2.77 us
    ppermute x6, waiting for transfers between devices, swapped(): lax.ppermute(block, 'tm', [(i, i ^ mask) for i in range(peers)])  2.52 us
    pallas_call x1, Pallas kernels, on_device(): call(functools.partial(rhs_kernel, hi_count), jax.ShapeDtypeStruct((knots...  2.29 us
  transfers between devices with their start and end apart: 17, of which 7 were waited for; matrix products, arithmetic and copies ran while one was open for 0% of the time, Pallas kernels for 11%

profile of v5, /device:TPU:0, one launch (start us, length us, event | category | flops | bytes accessed | tf_op | source)
XLA Modules:
  0.0 47.3 jit_solution(18068352215913292035)
XLA Ops:
  0.6 0.0 copy-start.1
  0.6 8.4 %sums.1 = (f32[21,8,128]{2,1,0:T(8,128)}, f32[21,8,128]{2,1,0:T(8,128)}, f32[21,8,128]{2,1,0:T(8,128)}, f32[21,8,128]{2,1,0:T(8,128)}, f32[64,8,128]{2,1,0:T(8,128)}, /*index=5*/f32[64,8,128]{2,1,0:T(8,128)}) custom-call(s32[1]{0:T(128)} %bitcast.me_ref, s32[1]{0:T(128)} %bitcast.1.sky_ref, s32[64]{0:T(128)} %win_ref.3, s32[64,128]{1,0:T(8,128)} %bitcast.8, ...), custom_call_target="tpu_custom_call" | custom-call | flops 8999999488 | tf_op jit(solution)/shard_map/sums/pallas_call | solution.py:471
  9.1 0.0 copy-start
  9.1 0.0 copy-start.9
  9.1 0.5 %collective-permute-start = (f32[64,8,128]{2,1,0:T(8,128)}, f32[64,8,128]{2,1,0:T(8,128)S(1)}, u32[]{:S(2)}, u32[]{:S(2)}) collective-permute-start(f32[64,8,128]{2,1,0:T(8,128)} %get-tuple-element.38), channel_id=1, source_target_pairs={{0,4},{4,0},{8,12},{12,8},{16,20},{20,16},{24,28},{28,24},{1,5},{5... | collective-permute-start | bytes 786440 | tf_op jit(solution)/shard_map/halves/ppermute | solution.py:460
  9.6 4.7 %collective-permute-start.1 = (f32[21,8,128]{2,1,0:T(8,128)}, f32[21,8,128]{2,1,0:T(8,128)S(1)}, u32[]{:S(2)}, u32[]{:S(2)}) collective-permute-start(f32[21,8,128]{2,1,0:T(8,128)} %get-tuple-element.49), channel_id=1, source_target_pairs={{0,3},{1,2},{2,1},{3,0},{4,7},{5,6},{6,5},{7,4},{8,11},{9,10},{10,... | collective-permute-start | bytes 258056 | tf_op jit(solution)/shard_map/ppermute | solution.py:455
  14.3 0.0 collective-permute-start.2
  14.3 0.7 %collective-permute-start.3 = (f32[21,8,128]{2,1,0:T(8,128)}, f32[21,8,128]{2,1,0:T(8,128)S(1)}, u32[]{:S(2)}, u32[]{:S(2)}) collective-permute-start(f32[21,8,128]{2,1,0:T(8,128)} %get-tuple-element.51), channel_id=1, source_target_pairs={{0,1},{1,0},{2,3},{3,2},{4,5},{5,4},{6,7},{7,6},{8,9},{9,8},{10,11... | collective-permute-start | bytes 258056 | tf_op jit(solution)/shard_map/ppermute | solution.py:455
  14.9 0.0 copy-done.1
  15.0 1.2 %one_hot.1.low_ref = bf16[256,8192]{1,0:T(8,128)(2,1)S(1)} custom-call(s32[64,128]{1,0:T(8,128)S(1)} %bitcast.9), custom_call_target="tpu_custom_call" | custom-call | flops 1000000000 | tf_op jit(solution)/shard_map/one_hot/pallas_call | solution.py:502
  16.2 0.0 collective-permute-done.got_ref
  16.2 0.0 copy-done
  16.2 0.1 halves.1
  16.3 2.6 %collective-permute-start.4 = (f32[16,8,128]{2,1,0:T(8,128)S(1)}, f32[16,8,128]{2,1,0:T(8,128)S(1)}, u32[]{:S(2)}, u32[]{:S(2)}) collective-permute-start(f32[16,8,128]{2,1,0:T(8,128)S(1)} %get-tuple-element.40), channel_id=1, source_target_pairs={{0,24},{4,28},{8,16},{12,20},{16,8},{20,12},{24,0},{28,4},{1,25},{... | collective-permute-start | bytes 196616 | tf_op jit(solution)/shard_map/ppermute | solution.py:464
  18.9 0.5 %collective-permute-start.5 = (f32[16,8,128]{2,1,0:T(8,128)S(1)}, f32[16,8,128]{2,1,0:T(8,128)S(1)}, u32[]{:S(2)}, u32[]{:S(2)}) collective-permute-start(f32[16,8,128]{2,1,0:T(8,128)S(1)} %get-tuple-element.41), channel_id=1, source_target_pairs={{0,16},{4,20},{8,24},{12,28},{16,0},{20,4},{24,8},{28,12},{1,17},{... | collective-permute-start | bytes 196616 | tf_op jit(solution)/shard_map/ppermute | solution.py:464
  19.4 0.0 collective-permute-done.1.refs_1_
  19.4 0.4 collective-permute-start.6
  19.8 2.5 %collective-permute-done.2.refs_2_ = f32[21,8,128]{2,1,0:T(8,128)S(1)} collective-permute-done((f32[21,8,128]{2,1,0:T(8,128)}, f32[21,8,128]{2,1,0:T(8,128)S(1)}, u32[]{:S(2)}, u32[]{:S(2)}) %collective-permute-start.2) | collective-permute-done | bytes 86048 | tf_op jit(solution)/shard_map/ppermute | solution.py:455
  22.3 0.0 collective-permute-done.3.refs_3_
  22.3 0.0 copy-done.9
  22.3 0.2 solve.1
  22.5 2.5 %collective-permute-start.7 = (f32[5,8,128]{2,1,0:T(8,128)S(1)}, f32[5,8,128]{2,1,0:T(8,128)S(1)}, u32[]{:S(2)}, u32[]{:S(2)}) collective-permute-start(f32[5,8,128]{2,1,0:T(8,128)S(1)} %get-tuple-element.63.refs_0_), channel_id=1, source_target_pairs={{0,3},{1,2},{2,1},{3,0},{4,7},{5,6},{6,5},{7,4},{8,11},{9,10},{10,... | collective-permute-start | bytes 61448 | tf_op jit(solution)/shard_map/ppermute | solution.py:455
  25.0 0.0 collective-permute-start.8
  25.0 0.0 collective-permute-done.4.refs_1_
  25.0 1.9 %collective-permute-start.9 = (f32[5,8,128]{2,1,0:T(8,128)S(1)}, f32[5,8,128]{2,1,0:T(8,128)S(1)}, u32[]{:S(2)}, u32[]{:S(2)}) collective-permute-start(f32[5,8,128]{2,1,0:T(8,128)S(1)} %get-tuple-element.63.refs_0_), channel_id=1, source_target_pairs={{0,1},{1,0},{2,3},{3,2},{4,5},{5,4},{6,7},{7,6},{8,9},{9,8},{10,11... | collective-permute-start | bytes 61448 | tf_op jit(solution)/shard_map/ppermute | solution.py:455
  26.9 0.0 collective-permute-done.5.refs_2_
  26.9 0.0 collective-permute-done.6.refs_3_
  26.9 0.0 copy-start.2
  26.9 0.0 copy-start.3
  26.9 0.0 copy-start.5
  26.9 0.0 copy-start.6
  27.0 0.0 copy-start.8
  27.0 2.9 %invert.1.inv_ref = f32[16,8,128]{2,1,0:T(8,128)S(1)} custom-call(s32[1]{0:T(128)} %bitcast.1.sky_ref, f32[3,8,128]{2,1,0:T(8,128)S(1)} %get-tuple-element.56.ties_ref, f32[16,8,128]{2,1,0:T(8,128)S(1)} %get-tuple-element.39.refs_0_, f32[16,8,128]{2,1,0:T(8,128)S(1)} %collective-permute-done.4.refs_1_, f32[16,8,128]{2,1,0:T(8,128)S(1)} %collective-permute-done.5.refs_2_, ...), custom_call_target="tpu_custom_call" | custom-call | flops 3000000000 | tf_op jit(solution)/shard_map/invert/pallas_call | solution.py:523
  29.9 0.0 collective-permute-done.7.refs_1_
  29.9 0.0 collective-permute-done.8.refs_2_
  29.9 0.0 collective-permute-done.9.refs_3_
  29.9 0.0 copy-done.2
  29.9 0.0 copy-done.3
  29.9 0.0 copy-done.5
  29.9 0.0 copy-done.6
  29.9 0.0 copy-done.8
  29.9 2.3 %right_sides.1.mine_ref = f32[32,128]{1,0:T(8,128)S(1)} custom-call(s32[1]{0:T(128)} %bitcast.me_ref, s32[64]{0:T(128)S(1)} %copy-done.8, bf16[256,8192]{1,0:T(8,128)(2,1)S(1)} %one_hot.1.low_ref, s32[64,128]{1,0:T(8,128)S(1)} %bitcast.10, f32[64,128]{1,0:T(8,128)S(1)} %bitcast.12, f32[64,128]{1,0:T(8,128)S(1)} %bitcast.14, bf16[5,8192]{1,0:T(8,128)(2,1)S(1)} %copy-done.3, ...), custom_call_target="tpu_custom_call" | custom-call | flops 6000000000 | tf_op jit(solution)/shard_map/right_sides/pallas_call | solution.py:532
  32.2 0.0 copy-start.4
  32.2 0.0 copy-start.7
  32.3 0.1 collective-permute-start.10
  32.3 1.2 %collective-permute-done.10.theirs_ref = f32[32,128]{1,0:T(8,128)S(1)} collective-permute-done((f32[32,128]{1,0:T(8,128)S(1)}, f32[32,128]{1,0:T(8,128)S(1)}, u32[]{:S(2)}, u32[]{:S(2)}) %collective-permute-start.10) | collective-permute-done | bytes 16416 | tf_op jit(solution)/shard_map/send/ppermute | solution.py:460
  33.5 0.1 send.1.refs_0_
  33.7 2.5 %collective-permute-start.11 = (f32[18,8,128]{2,1,0:T(8,128)S(1)}, f32[18,8,128]{2,1,0:T(8,128)S(1)}, u32[]{:S(2)}, u32[]{:S(2)}) collective-permute-start(f32[18,8,128]{2,1,0:T(8,128)S(1)} %send.1.refs_0_), channel_id=1, source_target_pairs={{0,24},{4,28},{8,16},{12,20},{16,8},{20,12},{24,0},{28,4},{1,25},{... | collective-permute-start | bytes 221192 | tf_op jit(solution)/shard_map/ppermute | solution.py:464
  36.1 0.5 %collective-permute-start.12 = (f32[18,8,128]{2,1,0:T(8,128)S(1)}, f32[18,8,128]{2,1,0:T(8,128)S(1)}, u32[]{:S(2)}, u32[]{:S(2)}) collective-permute-start(f32[18,8,128]{2,1,0:T(8,128)S(1)} %send.1.refs_0_), channel_id=1, source_target_pairs={{0,16},{4,20},{8,24},{12,28},{16,0},{20,4},{24,8},{28,12},{1,17},{... | collective-permute-start | bytes 221192 | tf_op jit(solution)/shard_map/ppermute | solution.py:464
  36.6 0.5 %collective-permute-start.13 = (f32[18,8,128]{2,1,0:T(8,128)S(1)}, f32[18,8,128]{2,1,0:T(8,128)S(1)}, u32[]{:S(2)}, u32[]{:S(2)}) collective-permute-start(f32[18,8,128]{2,1,0:T(8,128)S(1)} %send.1.refs_0_), channel_id=1, source_target_pairs={{0,8},{4,12},{8,0},{12,4},{16,24},{20,28},{24,16},{28,20},{1,9},{5... | collective-permute-start | bytes 221192 | tf_op jit(solution)/shard_map/ppermute | solution.py:464
  37.1 1.8 %collective-permute-done.11.refs_1_ = f32[18,8,128]{2,1,0:T(8,128)S(1)} collective-permute-done((f32[18,8,128]{2,1,0:T(8,128)S(1)}, f32[18,8,128]{2,1,0:T(8,128)S(1)}, u32[]{:S(2)}, u32[]{:S(2)}) %collective-permute-start.11) | collective-permute-done | bytes 73760 | tf_op jit(solution)/shard_map/ppermute | solution.py:464
  38.9 1.5 %collective-permute-done.12.refs_2_ = f32[18,8,128]{2,1,0:T(8,128)S(1)} collective-permute-done((f32[18,8,128]{2,1,0:T(8,128)S(1)}, f32[18,8,128]{2,1,0:T(8,128)S(1)}, u32[]{:S(2)}, u32[]{:S(2)}) %collective-permute-start.12) | collective-permute-done | bytes 73760 | tf_op jit(solution)/shard_map/ppermute | solution.py:464
  40.5 0.5 %collective-permute-done.13.refs_3_ = f32[18,8,128]{2,1,0:T(8,128)S(1)} collective-permute-done((f32[18,8,128]{2,1,0:T(8,128)S(1)}, f32[18,8,128]{2,1,0:T(8,128)S(1)}, u32[]{:S(2)}, u32[]{:S(2)}) %collective-permute-start.13) | collective-permute-done | bytes 73760 | tf_op jit(solution)/shard_map/ppermute | solution.py:464
  41.0 0.7 %collective-permute-start.14 = (f32[10,8,128]{2,1,0:T(8,128)S(1)}, f32[10,8,128]{2,1,0:T(8,128)S(1)}, u32[]{:S(2)}, u32[]{:S(2)}) collective-permute-start(f32[10,8,128]{2,1,0:T(8,128)S(1)} %get-tuple-element.70), channel_id=1, source_target_pairs={{4,5},{1,2},{6,7},{12,13},{9,10},{14,15},{20,21},{17,18},{22,23},{... | collective-permute-start | bytes 122888 | tf_op jit(solution)/shard_map/ppermute | solution.py:569
  41.7 0.7 %collective-permute-start.15 = (f32[10,8,128]{2,1,0:T(8,128)S(1)}, f32[10,8,128]{2,1,0:T(8,128)S(1)}, u32[]{:S(2)}, u32[]{:S(2)}) collective-permute-start(f32[10,8,128]{2,1,0:T(8,128)S(1)} %get-tuple-element.71), channel_id=1, source_target_pairs={{0,4},{4,0},{8,12},{12,8},{16,20},{20,16},{24,28},{28,24},{1,5},{5... | collective-permute-start | bytes 122888 | tf_op jit(solution)/shard_map/ppermute | solution.py:460
  42.4 0.0 collective-permute-done.14.outer_ref
  42.4 0.9 %collective-permute-done.15.inner_ref = f32[10,8,128]{2,1,0:T(8,128)S(1)} collective-permute-done((f32[10,8,128]{2,1,0:T(8,128)S(1)}, f32[10,8,128]{2,1,0:T(8,128)S(1)}, u32[]{:S(2)}, u32[]{:S(2)}) %collective-permute-start.15) | collective-permute-done | bytes 40992 | tf_op jit(solution)/shard_map/ppermute | solution.py:460
  43.3 1.1 %sweeps.1.mine_ref = f32[32,128]{1,0:T(8,128)S(1)} custom-call(s32[1]{0:T(128)} %bitcast.1.sky_ref, f32[66,8,128]{2,1,0:T(8,128)S(1)} %get-tuple-element.69.main_ref, f32[10,8,128]{2,1,0:T(8,128)S(1)} %collective-permute-done.14.outer_ref, f32[10,8,128]{2,1,0:T(8,128)S(1)} %collective-permute-done.15.inner_ref, f32[3,8,128]{2,1,0:T(8,128)S(1)} %get-tuple-element.56.ties_ref), custom_call_target="tpu_custom_call" | custom-call | flops 1000000000 | tf_op jit(solution)/shard_map/sweeps/pallas_call | solution.py:572
  44.3 1.5 %collective-permute-start.16 = (f32[32,128]{1,0:T(8,128)S(1)}, f32[32,128]{1,0:T(8,128)S(1)}, u32[]{:S(2)}, u32[]{:S(2)}) collective-permute-start(f32[32,128]{1,0:T(8,128)S(1)} %sweeps.1.mine_ref), channel_id=1, source_target_pairs={{0,4},{4,0},{8,12},{12,8},{16,20},{20,16},{24,28},{28,24},{1,5},{5... | collective-permute-start | bytes 49160 | tf_op jit(solution)/shard_map/finish/ppermute | solution.py:460
  45.8 0.0 copy-done.4
  45.8 0.7 %update.1 = f32[5,4096]{1,0:T(8,128)} custom-call(s32[1]{0:T(128)} %bitcast.me_ref, f32[5,4096]{1,0:T(8,128)S(1)} %copy-done.4, f32[5,8,128]{2,1,0:T(8,128)S(1)} %get-tuple-element.63.refs_0_, f32[5,8,128]{2,1,0:T(8,128)S(1)} %collective-permute-done.7.refs_1_, f32[5,8,128]{2,1,0:T(8,128)S(1)} %collective-permute-done.8.refs_2_, ...), custom_call_target="tpu_custom_call" | custom-call | flops 100000000 | tf_op jit(solution)/shard_map/update/pallas_call | solution.py:546
  46.5 0.1 collective-permute-done.16.theirs_ref
  46.6 0.0 copy-done.7
  46.7 0.7 %finish.1 = f32[32,128]{1,0:T(8,128)} custom-call(s32[1]{0:T(128)} %bitcast.1.sky_ref, f32[32,128]{1,0:T(8,128)S(1)} %sweeps.1.mine_ref, f32[32,128]{1,0:T(8,128)S(1)} %collective-permute-done.16.theirs_ref, f32[32,128]{1,0:T(8,128)S(1)} %bitcast.15), custom_call_target="tpu_custom_call" | custom-call | flops 100000000 | tf_op jit(solution)/shard_map/finish/pallas_call | solution.py:584
  (1 shorter events, 0.0 us)
Async XLA Ops:
  0.6 14.3 %copy-start.1 = (s32[8192]{0:T(1024)S(1)}, s32[8192]{0:T(1024)}, u32[]{:S(2)}) copy-start(s32[8192]{0:T(1024)} %param.13) | copy-start | bytes 98308
  9.1 7.1 %copy-start = (f32[64,8,128]{2,1,0:T(8,128)S(1)}, f32[64,8,128]{2,1,0:T(8,128)}, u32[]{:S(2)}) copy-start(f32[64,8,128]{2,1,0:T(8,128)} %get-tuple-element.37.keep_ref) | copy-start | bytes 786436
  9.1 13.2 %copy-start.9 = (f32[21,8,128]{2,1,0:T(8,128)S(1)}, f32[21,8,128]{2,1,0:T(8,128)}, u32[]{:S(2)}) copy-start(f32[21,8,128]{2,1,0:T(8,128)} %get-tuple-element.52.refs_0_) | copy-start | bytes 258052
  9.1 7.1 %collective-permute-start = (f32[64,8,128]{2,1,0:T(8,128)}, f32[64,8,128]{2,1,0:T(8,128)S(1)}, u32[]{:S(2)}, u32[]{:S(2)}) collective-permute-start(f32[64,8,128]{2,1,0:T(8,128)} %get-tuple-element.38), channel_id=1, source_target_pairs={{0,4},{4,0},{8,12},{12,8},{16,20},{20,16},{24,28},{28,24},{1,5},{5... | collective-permute-start | bytes 786440 | tf_op jit(solution)/shard_map/halves/ppermute | solution.py:460
  9.6 9.8 %collective-permute-start.1 = (f32[21,8,128]{2,1,0:T(8,128)}, f32[21,8,128]{2,1,0:T(8,128)S(1)}, u32[]{:S(2)}, u32[]{:S(2)}) collective-permute-start(f32[21,8,128]{2,1,0:T(8,128)} %get-tuple-element.49), channel_id=1, source_target_pairs={{0,3},{1,2},{2,1},{3,0},{4,7},{5,6},{6,5},{7,4},{8,11},{9,10},{10,... | collective-permute-start | bytes 258056 | tf_op jit(solution)/shard_map/ppermute | solution.py:455
  14.3 8.0 %collective-permute-start.2 = (f32[21,8,128]{2,1,0:T(8,128)}, f32[21,8,128]{2,1,0:T(8,128)S(1)}, u32[]{:S(2)}, u32[]{:S(2)}) collective-permute-start(f32[21,8,128]{2,1,0:T(8,128)} %get-tuple-element.50), channel_id=1, source_target_pairs={{0,2},{1,3},{2,0},{3,1},{4,6},{5,7},{6,4},{7,5},{8,10},{9,11},{10,... | collective-permute-start | bytes 258056 | tf_op jit(solution)/shard_map/ppermute | solution.py:455
  14.3 8.0 %collective-permute-start.3 = (f32[21,8,128]{2,1,0:T(8,128)}, f32[21,8,128]{2,1,0:T(8,128)S(1)}, u32[]{:S(2)}, u32[]{:S(2)}) collective-permute-start(f32[21,8,128]{2,1,0:T(8,128)} %get-tuple-element.51), channel_id=1, source_target_pairs={{0,1},{1,0},{2,3},{3,2},{4,5},{5,4},{6,7},{7,6},{8,9},{9,8},{10,11... | collective-permute-start | bytes 258056 | tf_op jit(solution)/shard_map/ppermute | solution.py:455
  16.3 8.7 %collective-permute-start.4 = (f32[16,8,128]{2,1,0:T(8,128)S(1)}, f32[16,8,128]{2,1,0:T(8,128)S(1)}, u32[]{:S(2)}, u32[]{:S(2)}) collective-permute-start(f32[16,8,128]{2,1,0:T(8,128)S(1)} %get-tuple-element.40), channel_id=1, source_target_pairs={{0,24},{4,28},{8,16},{12,20},{16,8},{20,12},{24,0},{28,4},{1,25},{... | collective-permute-start | bytes 196616 | tf_op jit(solution)/shard_map/ppermute | solution.py:464
  18.9 8.0 %collective-permute-start.5 = (f32[16,8,128]{2,1,0:T(8,128)S(1)}, f32[16,8,128]{2,1,0:T(8,128)S(1)}, u32[]{:S(2)}, u32[]{:S(2)}) collective-permute-start(f32[16,8,128]{2,1,0:T(8,128)S(1)} %get-tuple-element.41), channel_id=1, source_target_pairs={{0,16},{4,20},{8,24},{12,28},{16,0},{20,4},{24,8},{28,12},{1,17},{... | collective-permute-start | bytes 196616 | tf_op jit(solution)/shard_map/ppermute | solution.py:464
  19.4 7.5 %collective-permute-start.6 = (f32[16,8,128]{2,1,0:T(8,128)S(1)}, f32[16,8,128]{2,1,0:T(8,128)S(1)}, u32[]{:S(2)}, u32[]{:S(2)}) collective-permute-start(f32[16,8,128]{2,1,0:T(8,128)S(1)} %get-tuple-element.42), channel_id=1, source_target_pairs={{0,8},{4,12},{8,0},{12,4},{16,24},{20,28},{24,16},{28,20},{1,9},{5... | collective-permute-start | bytes 196616 | tf_op jit(solution)/shard_map/ppermute | solution.py:464
  22.5 7.4 %collective-permute-start.7 = (f32[5,8,128]{2,1,0:T(8,128)S(1)}, f32[5,8,128]{2,1,0:T(8,128)S(1)}, u32[]{:S(2)}, u32[]{:S(2)}) collective-permute-start(f32[5,8,128]{2,1,0:T(8,128)S(1)} %get-tuple-element.63.refs_0_), channel_id=1, source_target_pairs={{0,3},{1,2},{2,1},{3,0},{4,7},{5,6},{6,5},{7,4},{8,11},{9,10},{10,... | collective-permute-start | bytes 61448 | tf_op jit(solution)/shard_map/ppermute | solution.py:455
  25.0 4.9 %collective-permute-start.8 = (f32[5,8,128]{2,1,0:T(8,128)S(1)}, f32[5,8,128]{2,1,0:T(8,128)S(1)}, u32[]{:S(2)}, u32[]{:S(2)}) collective-permute-start(f32[5,8,128]{2,1,0:T(8,128)S(1)} %get-tuple-element.63.refs_0_), channel_id=1, source_target_pairs={{0,2},{1,3},{2,0},{3,1},{4,6},{5,7},{6,4},{7,5},{8,10},{9,11},{10,... | collective-permute-start | bytes 61448 | tf_op jit(solution)/shard_map/ppermute | solution.py:455
  25.0 4.9 %collective-permute-start.9 = (f32[5,8,128]{2,1,0:T(8,128)S(1)}, f32[5,8,128]{2,1,0:T(8,128)S(1)}, u32[]{:S(2)}, u32[]{:S(2)}) collective-permute-start(f32[5,8,128]{2,1,0:T(8,128)S(1)} %get-tuple-element.63.refs_0_), channel_id=1, source_target_pairs={{0,1},{1,0},{2,3},{3,2},{4,5},{5,4},{6,7},{7,6},{8,9},{9,8},{10,11... | collective-permute-start | bytes 61448 | tf_op jit(solution)/shard_map/ppermute | solution.py:455
  26.9 3.0 %copy-start.2 = (bf16[32,8192]{1,0:T(8,128)(2,1)S(1)}, bf16[32,8192]{1,0:T(8,128)(2,1)}, u32[]{:S(2)}) copy-start(bf16[32,8192]{1,0:T(8,128)(2,1)} %att_ref.1) | copy-start | bytes 1572868
  26.9 3.0 %copy-start.3 = (bf16[5,8192]{1,0:T(8,128)(2,1)S(1)}, bf16[5,8192]{1,0:T(8,128)(2,1)}, u32[]{:S(2)}) copy-start(bf16[5,8192]{1,0:T(8,128)(2,1)} %sp_ref.1) | copy-start | bytes 245764
  26.9 3.0 %copy-start.5 = (f32[8192]{0:T(1024)S(1)}, f32[8192]{0:T(1024)}, u32[]{:S(2)}) copy-start(f32[8192]{0:T(1024)} %param.10) | copy-start | bytes 98308
  26.9 3.0 %copy-start.6 = (f32[8192]{0:T(1024)S(1)}, f32[8192]{0:T(1024)}, u32[]{:S(2)}) copy-start(f32[8192]{0:T(1024)} %param.9) | copy-start | bytes 98308
  27.0 3.0 %copy-start.8 = (s32[64]{0:T(128)S(1)}, s32[64]{0:T(128)}, u32[]{:S(2)}) copy-start(s32[64]{0:T(128)} %win_ref.3) | copy-start | bytes 772
  32.2 13.6 %copy-start.4 = (f32[5,4096]{1,0:T(8,128)S(1)}, f32[5,4096]{1,0:T(8,128)}, u32[]{:S(2)}) copy-start(f32[5,4096]{1,0:T(8,128)} %sources_ref.1) | copy-start | bytes 245764
  32.2 14.4 %copy-start.7 = (f32[128,32]{0,1:T(8,128)S(1)}, f32[128,32]{0,1:T(8,128)}, u32[]{:S(2)}) copy-start(f32[128,32]{0,1:T(8,128)} %param.16) | copy-start | bytes 49156
  32.3 1.2 %collective-permute-start.10 = (f32[32,128]{1,0:T(8,128)S(1)}, f32[32,128]{1,0:T(8,128)S(1)}, u32[]{:S(2)}, u32[]{:S(2)}) collective-permute-start(f32[32,128]{1,0:T(8,128)S(1)} %right_sides.1.mine_ref), channel_id=1, source_target_pairs={{0,4},{4,0},{8,12},{12,8},{16,20},{20,16},{24,28},{28,24},{1,5},{5... | collective-permute-start | bytes 49160 | tf_op jit(solution)/shard_map/send/ppermute | solution.py:460
  33.7 5.3 %collective-permute-start.11 = (f32[18,8,128]{2,1,0:T(8,128)S(1)}, f32[18,8,128]{2,1,0:T(8,128)S(1)}, u32[]{:S(2)}, u32[]{:S(2)}) collective-permute-start(f32[18,8,128]{2,1,0:T(8,128)S(1)} %send.1.refs_0_), channel_id=1, source_target_pairs={{0,24},{4,28},{8,16},{12,20},{16,8},{20,12},{24,0},{28,4},{1,25},{... | collective-permute-start | bytes 221192 | tf_op jit(solution)/shard_map/ppermute | solution.py:464
  36.1 4.4 %collective-permute-start.12 = (f32[18,8,128]{2,1,0:T(8,128)S(1)}, f32[18,8,128]{2,1,0:T(8,128)S(1)}, u32[]{:S(2)}, u32[]{:S(2)}) collective-permute-start(f32[18,8,128]{2,1,0:T(8,128)S(1)} %send.1.refs_0_), channel_id=1, source_target_pairs={{0,16},{4,20},{8,24},{12,28},{16,0},{20,4},{24,8},{28,12},{1,17},{... | collective-permute-start | bytes 221192 | tf_op jit(solution)/shard_map/ppermute | solution.py:464
  36.6 4.4 %collective-permute-start.13 = (f32[18,8,128]{2,1,0:T(8,128)S(1)}, f32[18,8,128]{2,1,0:T(8,128)S(1)}, u32[]{:S(2)}, u32[]{:S(2)}) collective-permute-start(f32[18,8,128]{2,1,0:T(8,128)S(1)} %send.1.refs_0_), channel_id=1, source_target_pairs={{0,8},{4,12},{8,0},{12,4},{16,24},{20,28},{24,16},{28,20},{1,9},{5... | collective-permute-start | bytes 221192 | tf_op jit(solution)/shard_map/ppermute | solution.py:464
  41.0 1.4 %collective-permute-start.14 = (f32[10,8,128]{2,1,0:T(8,128)S(1)}, f32[10,8,128]{2,1,0:T(8,128)S(1)}, u32[]{:S(2)}, u32[]{:S(2)}) collective-permute-start(f32[10,8,128]{2,1,0:T(8,128)S(1)} %get-tuple-element.70), channel_id=1, source_target_pairs={{4,5},{1,2},{6,7},{12,13},{9,10},{14,15},{20,21},{17,18},{22,23},{... | collective-permute-start | bytes 122888 | tf_op jit(solution)/shard_map/ppermute | solution.py:569
  41.7 1.6 %collective-permute-start.15 = (f32[10,8,128]{2,1,0:T(8,128)S(1)}, f32[10,8,128]{2,1,0:T(8,128)S(1)}, u32[]{:S(2)}, u32[]{:S(2)}) collective-permute-start(f32[10,8,128]{2,1,0:T(8,128)S(1)} %get-tuple-element.71), channel_id=1, source_target_pairs={{0,4},{4,0},{8,12},{12,8},{16,20},{20,16},{24,28},{28,24},{1,5},{5... | collective-permute-start | bytes 122888 | tf_op jit(solution)/shard_map/ppermute | solution.py:460
  44.3 2.3 %collective-permute-start.16 = (f32[32,128]{1,0:T(8,128)S(1)}, f32[32,128]{1,0:T(8,128)S(1)}, u32[]{:S(2)}, u32[]{:S(2)}) collective-permute-start(f32[32,128]{1,0:T(8,128)S(1)} %sweeps.1.mine_ref), channel_id=1, source_target_pairs={{0,4},{4,0},{8,12},{12,8},{16,20},{20,16},{24,28},{28,24},{1,5},{5... | collective-permute-start | bytes 49160 | tf_op jit(solution)/shard_map/finish/ppermute | solution.py:460

commit v6 on v5

--- a/solution.py
+++ b/solution.py
@@ -19,6 +19,7 @@
 CORES = 2
 HALF = LANES // CORES
 SPLITS = 2
+STEP = 8
 ROWS = 8
 F32 = jnp.float32
 BF16 = jnp.bfloat16
@@ -147,27 +148,17 @@
     windows = sums.shape[0]
     knots = att_ref.shape[0]
     copies = LANES // knots
-    blank = jnp.zeros((knots, TILE), BF16)
-    lane = iota((8, LANES), 1)
-
-    for u in range(w_ref.shape[0] // 2):
-        att = att_ref[:, 2 * u * TILE : 2 * (u + 1) * TILE]
-        w = jnp.concatenate([w_ref[2 * u : 2 * u + 1, :], w_ref[2 * u + 1 : 2 * u + 2, :]], axis=1)
-        scaled = (w * att.astype(F32)).astype(BF16)
-        left = jnp.concatenate([scaled[:, :TILE], blank], axis=1)
-        right = jnp.concatenate([blank, scaled[:, TILE:]], axis=1)
+    for t in range(w_ref.shape[0]):
+        att = att_ref[:, t * TILE : (t + 1) * TILE]
+        scaled = (w_ref[t : t + 1, :] * att.astype(F32)).astype(BF16)
         normal = lax.dot_general(
-            jnp.concatenate([left, right], axis=0),
-            jnp.concatenate([att] * copies, axis=0),
+            jnp.concatenate([scaled, att], axis=1),
+            jnp.concatenate([att, scaled], axis=1),
             NT,
             preferred_element_type=F32,
         )
-        for h in range(2):
-            value = normal[h * knots : h * knots + 8]
-            for g in range(1, copies):
-                start = h * knots + 8 * g
-                value = jnp.where(lane < g * knots, value, normal[start : start + 8])
-            sums[lax.rem(win_ref[2 * u + h], windows)] += value
+        value = jnp.concatenate([normal[8 * g : 8 * (g + 1)] for g in range(copies)], axis=1)
+        sums[lax.rem(win_ref[t], windows)] += value
 
 
 def halves_kernel(sky_ref, keep_ref, got_ref, *refs):
@@ -236,49 +227,44 @@
 
 
 def invert_kernel(sky_ref, ties_ref, *refs):
-    parts, (out_ref, flat, cells) = refs[:-3], refs[-3:]
+    parts, (out_ref, flat) = refs[:-2], refs[-2:]
     own = out_ref.shape[0]
     knots = math.isqrt(out_ref.shape[1] * LANES)
+    groups = knots // 8
     total = parts[0][...]
     for part in parts[1:]:
         total = total + part[...]
-    flat[...] = jnp.zeros_like(flat)
+    if own * 8 < LANES:
+        flat[...] = jnp.zeros_like(flat)
     flat[0 : own * 8, :] = total.reshape(own * 8, LANES)
-    groups = LANES // knots
-    for r in range(8):
-        turned = flat[pl.ds(r, LANES, stride=8), :].T
-        for g in range(groups):
-            cells[(8 * g + r) * knots : (8 * g + r + 1) * knots, :] = turned[g * knots : (g + 1) * knots]
+    cells = flat[...].T
     core, chip = lax.rem(sky_ref[0], CORES), sky_ref[0] // CORES
-    shift = lax.rem(LANES - core * HALF - chip * own, LANES)
-    ties = pltpu.roll(ties_ref[0], shift, 1)
-    diagonal = jnp.concatenate([ties] * (knots // 8), axis=0)
-    inner = iota((knots, LANES), 0)
-    blocks = []
-    for k in range(knots):
-        row = 0.5 * (cells[k * knots : (k + 1) * knots, :] + cells[pl.ds(k, knots, stride=knots), :])
-        blocks.append(jnp.where(inner == k, row + diagonal, row))
-    for k in range(knots):
-        cells[k * knots : (k + 1) * knots, :] = blocks[k]
-
-    def sweep(k, carry):
-        at = pl.multiple_of(k * knots, knots)
-        row = cells[pl.ds(at, knots), :]
-        pivot = 1.0 / cells[pl.ds(at + k, 1), :]
-        here = inner == k
-        scaled = jnp.where(here, -pivot, row * pivot)
-        for i in range(knots):
-            old = jnp.where(here, 0.0, cells[i * knots : (i + 1) * knots, :])
-            cells[i * knots : (i + 1) * knots, :] = old - row[i : i + 1] * scaled
-        cells[pl.ds(at, knots), :] = scaled
-        return carry
-
-    lax.fori_loop(0, knots, sweep, 0)
-    for r in range(8):
-        turned = jnp.concatenate(
-            [cells[(8 * g + r) * knots : (8 * g + r + 1) * knots, :] for g in range(groups)], axis=0
-        ).T
-        flat[pl.ds(r, LANES, stride=8), :] = -turned
+    window = core * HALF + chip * own + iota((8, LANES), 1) // 8
+    ties = jnp.take_along_axis(ties_ref[0], jnp.minimum(window, LANES - 1), axis=1)
+    diagonal = jnp.concatenate([ties] * groups, axis=0)
+    column = iota((knots, LANES), 0)
+    lane = iota((knots, LANES), 1)
+    offset = lane & 7
+    rows = [
+        0.5 * cells[g * knots : (g + 1) * knots] + jnp.where(column == 8 * g + offset, diagonal, 0.0)
+        for g in range(groups)
+    ]
+    for start in range(0, knots, STEP):
+        mine, first = divmod(start, 8)
+        pivots = [jnp.take_along_axis(rows[mine], lane - offset + first + i, axis=1) for i in range(STEP)]
+        for i in range(STEP):
+            k = start + i
+            here = column == k
+            pivot = 1.0 / pivots[i][k : k + 1]
+            scaled = jnp.where(here, -pivot, pivots[i] * pivot)
+            rows = [jnp.where(here, 0.0, old) - old[k : k + 1] * scaled for old in rows]
+            pivots = [
+                scaled if j == i else jnp.where(here, 0.0, old) - old[k : k + 1] * scaled
+                for j, old in enumerate(pivots)
+            ]
+        for i in range(STEP):
+            rows[mine] = jnp.where(offset == first + i, pivots[i], rows[mine])
+    flat[...] = -jnp.concatenate(rows, axis=0).T
     out_ref[...] = flat[0 : own * 8, :].reshape(own, 8, LANES)
 
 
@@ -524,7 +510,7 @@
             invert_kernel,
             jax.ShapeDtypeStruct((own, cell_rows, LANES), F32),
             [smem()] + [vmem()] * (1 + chips),
-            [pltpu.VMEM((cell_rows * LANES, LANES), F32), pltpu.VMEM((knots * knots, LANES), F32)],
+            [pltpu.VMEM((LANES, LANES), F32)],
             micros=3,
         )(sky, ties, *parts)
     inverse, changes = lax.optimization_barrier((inverse, changes))

time: 48.2 us -> 47.9 us (level)
  the two profiles are of different devices: /device:TPU:0 before, /device:TPU:17 now
where the time goes in v6:
time: 47.9 us; the launch traced here: 47.7 us
  starting transfers between devices  23.5 us (49%)
  Pallas kernels  15.6 us (33%)
  waiting for transfers between devices  7.7 us (16%)
  between operations  0.83 us (2%)
    ppermute x6, starting transfers between devices, swapped(): lax.ppermute(block, 'tm', [(i, i ^ mask) for i in range(peers)])  8.42 us
    pallas_call x1, Pallas kernels, on_device(): call(functools.partial(sums_kernel, hi_count), [block] * peers + [half] *...  8.13 us
    ppermute x4, starting transfers between devices, other_core(): return lax.ppermute(x, 'sky', [(i, i ^ 1) for i in range(devices)])  7.85 us
    ppermute x6, starting transfers between devices, other_chips(): lax.ppermute(block, 'sky', [(i, i ^ CORES * mask) for i in range(devices)])  5.36 us
    ppermute x6, waiting for transfers between devices, other_chips(): lax.ppermute(block, 'sky', [(i, i ^ CORES * mask) for i in range(devices)])  3.41 us
    ppermute x6, waiting for transfers between devices, swapped(): lax.ppermute(block, 'tm', [(i, i ^ mask) for i in range(peers)])  2.47 us
    pallas_call x1, Pallas kernels, on_device(): call(functools.partial(rhs_kernel, hi_count), jax.ShapeDtypeStruct((knots...  2.29 us
    ppermute x1, starting transfers between devices, on_device(): lax.ppermute(outer, ('sky', 'tm'), list(zip(upper + lower, lower + upper)))  1.92 us
  transfers between devices with their start and end apart: 17, of which 9 were waited for; matrix products, arithmetic and copies ran while one was open for 0% of the time, Pallas kernels for 7%

profile of v6, /device:TPU:17, one launch (start us, length us, event | category | flops | bytes accessed | tf_op | source)
XLA Modules:
  0.0 47.7 jit_solution(4736174995594801403)
XLA Ops:
  0.6 0.0 copy-start.1
  0.6 8.1 %sums.1 = (f32[21,8,128]{2,1,0:T(8,128)}, f32[21,8,128]{2,1,0:T(8,128)}, f32[21,8,128]{2,1,0:T(8,128)}, f32[21,8,128]{2,1,0:T(8,128)}, f32[64,8,128]{2,1,0:T(8,128)}, /*index=5*/f32[64,8,128]{2,1,0:T(8,128)}) custom-call(s32[1]{0:T(128)} %bitcast.me_ref, s32[1]{0:T(128)} %bitcast.1.sky_ref, s32[64]{0:T(128)} %win_ref.3, s32[64,128]{1,0:T(8,128)} %bitcast.8, ...), custom_call_target="tpu_custom_call" | custom-call | flops 8999999488 | tf_op jit(solution)/shard_map/sums/pallas_call | solution.py:457
  8.8 0.0 copy-start
  8.8 0.0 copy-start.9
  8.8 0.7 %collective-permute-start = (f32[64,8,128]{2,1,0:T(8,128)}, f32[64,8,128]{2,1,0:T(8,128)S(1)}, u32[]{:S(2)}, u32[]{:S(2)}) collective-permute-start(f32[64,8,128]{2,1,0:T(8,128)} %get-tuple-element.38), channel_id=1, source_target_pairs={{0,4},{4,0},{8,12},{12,8},{16,20},{20,16},{24,28},{28,24},{1,5},{5... | collective-permute-start | bytes 786440 | tf_op jit(solution)/shard_map/halves/ppermute | solution.py:446
  9.6 0.2 collective-permute-start.1
  9.7 3.2 %collective-permute-start.2 = (f32[21,8,128]{2,1,0:T(8,128)}, f32[21,8,128]{2,1,0:T(8,128)S(1)}, u32[]{:S(2)}, u32[]{:S(2)}) collective-permute-start(f32[21,8,128]{2,1,0:T(8,128)} %get-tuple-element.50), channel_id=1, source_target_pairs={{0,2},{1,3},{2,0},{3,1},{4,6},{5,7},{6,4},{7,5},{8,10},{9,11},{10,... | collective-permute-start | bytes 258056 | tf_op jit(solution)/shard_map/ppermute | solution.py:441
  12.9 0.0 collective-permute-start.3
  13.0 0.0 copy-done.1
  13.0 1.2 %one_hot.1.low_ref = bf16[256,8192]{1,0:T(8,128)(2,1)S(1)} custom-call(s32[64,128]{1,0:T(8,128)S(1)} %bitcast.9), custom_call_target="tpu_custom_call" | custom-call | flops 1000000000 | tf_op jit(solution)/shard_map/one_hot/pallas_call | solution.py:488
  14.2 0.0 collective-permute-done.got_ref
  14.2 0.0 copy-done
  14.2 0.1 halves.1
  14.3 2.2 %collective-permute-start.4 = (f32[16,8,128]{2,1,0:T(8,128)S(1)}, f32[16,8,128]{2,1,0:T(8,128)S(1)}, u32[]{:S(2)}, u32[]{:S(2)}) collective-permute-start(f32[16,8,128]{2,1,0:T(8,128)S(1)} %get-tuple-element.40), channel_id=1, source_target_pairs={{0,24},{4,28},{8,16},{12,20},{16,8},{20,12},{24,0},{28,4},{1,25},{... | collective-permute-start | bytes 196616 | tf_op jit(solution)/shard_map/ppermute | solution.py:450
  16.5 0.2 collective-permute-start.5
  16.7 0.0 collective-permute-done.1.refs_1_
  16.7 0.3 collective-permute-start.6
  17.0 0.7 %collective-permute-done.2.refs_2_ = f32[21,8,128]{2,1,0:T(8,128)S(1)} collective-permute-done((f32[21,8,128]{2,1,0:T(8,128)}, f32[21,8,128]{2,1,0:T(8,128)S(1)}, u32[]{:S(2)}, u32[]{:S(2)}) %collective-permute-start.2) | collective-permute-done | bytes 86048 | tf_op jit(solution)/shard_map/ppermute | solution.py:441
  17.7 0.0 collective-permute-done.3.refs_3_
  17.7 0.0 copy-done.9
  17.7 0.2 solve.1
  17.8 2.2 %collective-permute-start.7 = (f32[5,8,128]{2,1,0:T(8,128)S(1)}, f32[5,8,128]{2,1,0:T(8,128)S(1)}, u32[]{:S(2)}, u32[]{:S(2)}) collective-permute-start(f32[5,8,128]{2,1,0:T(8,128)S(1)} %get-tuple-element.63.refs_0_), channel_id=1, source_target_pairs={{0,3},{1,2},{2,1},{3,0},{4,7},{5,6},{6,5},{7,4},{8,11},{9,10},{10,... | collective-permute-start | bytes 61448 | tf_op jit(solution)/shard_map/ppermute | solution.py:441
  20.0 2.9 %collective-permute-start.8 = (f32[5,8,128]{2,1,0:T(8,128)S(1)}, f32[5,8,128]{2,1,0:T(8,128)S(1)}, u32[]{:S(2)}, u32[]{:S(2)}) collective-permute-start(f32[5,8,128]{2,1,0:T(8,128)S(1)} %get-tuple-element.63.refs_0_), channel_id=1, source_target_pairs={{0,2},{1,3},{2,0},{3,1},{4,6},{5,7},{6,4},{7,5},{8,10},{9,11},{10,... | collective-permute-start | bytes 61448 | tf_op jit(solution)/shard_map/ppermute | solution.py:441
  22.9 0.0 collective-permute-done.4.refs_1_
  22.9 0.0 collective-permute-start.9
  22.9 0.0 collective-permute-done.5.refs_2_
  22.9 0.0 collective-permute-done.6.refs_3_
  22.9 0.0 copy-start.2
  22.9 0.0 copy-start.3
  22.9 0.0 copy-start.5
  22.9 0.0 copy-start.6
  22.9 0.0 copy-start.8
  22.9 1.1 %invert.1.inv_ref = f32[16,8,128]{2,1,0:T(8,128)S(1)} custom-call(s32[1]{0:T(128)} %bitcast.1.sky_ref, f32[3,8,128]{2,1,0:T(8,128)S(1)} %get-tuple-element.56.ties_ref, f32[16,8,128]{2,1,0:T(8,128)S(1)} %get-tuple-element.39.refs_0_, f32[16,8,128]{2,1,0:T(8,128)S(1)} %collective-permute-done.4.refs_1_, f32[16,8,128]{2,1,0:T(8,128)S(1)} %collective-permute-done.5.refs_2_, ...), custom_call_target="tpu_custom_call" | custom-call | flops 3000000000 | tf_op jit(solution)/shard_map/invert/pallas_call | solution.py:509
  24.0 0.0 collective-permute-done.7.refs_1_
  24.0 0.2 collective-permute-done.8.refs_2_
  24.3 1.5 %collective-permute-done.9.refs_3_ = f32[5,8,128]{2,1,0:T(8,128)S(1)} collective-permute-done((f32[5,8,128]{2,1,0:T(8,128)S(1)}, f32[5,8,128]{2,1,0:T(8,128)S(1)}, u32[]{:S(2)}, u32[]{:S(2)}) %collective-permute-start.9) | collective-permute-done | bytes 20512 | tf_op jit(solution)/shard_map/ppermute | solution.py:441
  25.8 0.0 copy-done.2
  25.8 0.0 copy-done.3
  25.8 0.0 copy-done.5
  25.8 0.0 copy-done.6
  25.8 0.0 copy-done.8
  25.8 2.3 %right_sides.1.mine_ref = f32[32,128]{1,0:T(8,128)S(1)} custom-call(s32[1]{0:T(128)} %bitcast.me_ref, s32[64]{0:T(128)S(1)} %copy-done.8, bf16[256,8192]{1,0:T(8,128)(2,1)S(1)} %one_hot.1.low_ref, s32[64,128]{1,0:T(8,128)S(1)} %bitcast.10, f32[64,128]{1,0:T(8,128)S(1)} %bitcast.12, f32[64,128]{1,0:T(8,128)S(1)} %bitcast.14, bf16[5,8192]{1,0:T(8,128)(2,1)S(1)} %copy-done.3, ...), custom_call_target="tpu_custom_call" | custom-call | flops 6000000000 | tf_op jit(solution)/shard_map/right_sides/pallas_call | solution.py:518
  28.1 0.0 copy-start.4
  28.1 0.0 copy-start.7
  28.1 2.3 %collective-permute-start.10 = (f32[32,128]{1,0:T(8,128)S(1)}, f32[32,128]{1,0:T(8,128)S(1)}, u32[]{:S(2)}, u32[]{:S(2)}) collective-permute-start(f32[32,128]{1,0:T(8,128)S(1)} %right_sides.1.mine_ref), channel_id=1, source_target_pairs={{0,4},{4,0},{8,12},{12,8},{16,20},{20,16},{24,28},{28,24},{1,5},{5... | collective-permute-start | bytes 49160 | tf_op jit(solution)/shard_map/send/ppermute | solution.py:446
  30.5 0.8 %collective-permute-done.10.theirs_ref = f32[32,128]{1,0:T(8,128)S(1)} collective-permute-done((f32[32,128]{1,0:T(8,128)S(1)}, f32[32,128]{1,0:T(8,128)S(1)}, u32[]{:S(2)}, u32[]{:S(2)}) %collective-permute-start.10) | collective-permute-done | bytes 16416 | tf_op jit(solution)/shard_map/send/ppermute | solution.py:446
  31.3 0.1 send.1.refs_0_
  31.5 2.2 %collective-permute-start.11 = (f32[18,8,128]{2,1,0:T(8,128)S(1)}, f32[18,8,128]{2,1,0:T(8,128)S(1)}, u32[]{:S(2)}, u32[]{:S(2)}) collective-permute-start(f32[18,8,128]{2,1,0:T(8,128)S(1)} %send.1.refs_0_), channel_id=1, source_target_pairs={{0,24},{4,28},{8,16},{12,20},{16,8},{20,12},{24,0},{28,4},{1,25},{... | collective-permute-start | bytes 221192 | tf_op jit(solution)/shard_map/ppermute | solution.py:450
  33.6 0.2 collective-permute-start.12
  33.9 0.2 collective-permute-start.13
  34.1 1.5 %collective-permute-done.11.refs_1_ = f32[18,8,128]{2,1,0:T(8,128)S(1)} collective-permute-done((f32[18,8,128]{2,1,0:T(8,128)S(1)}, f32[18,8,128]{2,1,0:T(8,128)S(1)}, u32[]{:S(2)}, u32[]{:S(2)}) %collective-permute-start.11) | collective-permute-done | bytes 73760 | tf_op jit(solution)/shard_map/ppermute | solution.py:450
  35.6 1.9 %collective-permute-done.12.refs_2_ = f32[18,8,128]{2,1,0:T(8,128)S(1)} collective-permute-done((f32[18,8,128]{2,1,0:T(8,128)S(1)}, f32[18,8,128]{2,1,0:T(8,128)S(1)}, u32[]{:S(2)}, u32[]{:S(2)}) %collective-permute-start.12) | collective-permute-done | bytes 73760 | tf_op jit(solution)/shard_map/ppermute | solution.py:450
  37.5 0.0 collective-permute-done.13.refs_3_
  37.5 1.9 %collective-permute-start.14 = (f32[10,8,128]{2,1,0:T(8,128)S(1)}, f32[10,8,128]{2,1,0:T(8,128)S(1)}, u32[]{:S(2)}, u32[]{:S(2)}) collective-permute-start(f32[10,8,128]{2,1,0:T(8,128)S(1)} %get-tuple-element.70), channel_id=1, source_target_pairs={{4,5},{1,2},{6,7},{12,13},{9,10},{14,15},{20,21},{17,18},{22,23},{... | collective-permute-start | bytes 122888 | tf_op jit(solution)/shard_map/ppermute | solution.py:555
  39.5 2.1 %collective-permute-start.15 = (f32[10,8,128]{2,1,0:T(8,128)S(1)}, f32[10,8,128]{2,1,0:T(8,128)S(1)}, u32[]{:S(2)}, u32[]{:S(2)}) collective-permute-start(f32[10,8,128]{2,1,0:T(8,128)S(1)} %get-tuple-element.71), channel_id=1, source_target_pairs={{0,4},{4,0},{8,12},{12,8},{16,20},{20,16},{24,28},{28,24},{1,5},{5... | collective-permute-start | bytes 122888 | tf_op jit(solution)/shard_map/ppermute | solution.py:446
  41.6 0.7 %collective-permute-done.14.outer_ref = f32[10,8,128]{2,1,0:T(8,128)S(1)} collective-permute-done((f32[10,8,128]{2,1,0:T(8,128)S(1)}, f32[10,8,128]{2,1,0:T(8,128)S(1)}, u32[]{:S(2)}, u32[]{:S(2)}) %collective-permute-start.14) | collective-permute-done | bytes 40992 | tf_op jit(solution)/shard_map/ppermute | solution.py:555
  42.3 0.2 collective-permute-done.15.inner_ref
  42.4 1.1 %sweeps.1.mine_ref = f32[32,128]{1,0:T(8,128)S(1)} custom-call(s32[1]{0:T(128)} %bitcast.1.sky_ref, f32[66,8,128]{2,1,0:T(8,128)S(1)} %get-tuple-element.69.main_ref, f32[10,8,128]{2,1,0:T(8,128)S(1)} %collective-permute-done.14.outer_ref, f32[10,8,128]{2,1,0:T(8,128)S(1)} %collective-permute-done.15.inner_ref, f32[3,8,128]{2,1,0:T(8,128)S(1)} %get-tuple-element.56.ties_ref), custom_call_target="tpu_custom_call" | custom-call | flops 1000000000 | tf_op jit(solution)/shard_map/sweeps/pallas_call | solution.py:558
  43.5 2.7 %collective-permute-start.16 = (f32[32,128]{1,0:T(8,128)S(1)}, f32[32,128]{1,0:T(8,128)S(1)}, u32[]{:S(2)}, u32[]{:S(2)}) collective-permute-start(f32[32,128]{1,0:T(8,128)S(1)} %sweeps.1.mine_ref), channel_id=1, source_target_pairs={{0,4},{4,0},{8,12},{12,8},{16,20},{20,16},{24,28},{28,24},{1,5},{5... | collective-permute-start | bytes 49160 | tf_op jit(solution)/shard_map/finish/ppermute | solution.py:446
  46.2 0.0 copy-done.4
  46.2 0.7 %update.1 = f32[5,4096]{1,0:T(8,128)} custom-call(s32[1]{0:T(128)} %bitcast.me_ref, f32[5,4096]{1,0:T(8,128)S(1)} %copy-done.4, f32[5,8,128]{2,1,0:T(8,128)S(1)} %get-tuple-element.63.refs_0_, f32[5,8,128]{2,1,0:T(8,128)S(1)} %collective-permute-done.7.refs_1_, f32[5,8,128]{2,1,0:T(8,128)S(1)} %collective-permute-done.8.refs_2_, ...), custom_call_target="tpu_custom_call" | custom-call | flops 100000000 | tf_op jit(solution)/shard_map/update/pallas_call | solution.py:532
  46.9 0.1 collective-permute-done.16.theirs_ref
  47.0 0.0 copy-done.7
  47.0 0.7 %finish.1 = f32[32,128]{1,0:T(8,128)} custom-call(s32[1]{0:T(128)} %bitcast.1.sky_ref, f32[32,128]{1,0:T(8,128)S(1)} %sweeps.1.mine_ref, f32[32,128]{1,0:T(8,128)S(1)} %collective-permute-done.16.theirs_ref, f32[32,128]{1,0:T(8,128)S(1)} %bitcast.15), custom_call_target="tpu_custom_call" | custom-call | flops 100000000 | tf_op jit(solution)/shard_map/finish/pallas_call | solution.py:570
  (1 shorter events, 0.0 us)
Async XLA Ops:
  0.6 12.3 %copy-start.1 = (s32[8192]{0:T(1024)S(1)}, s32[8192]{0:T(1024)}, u32[]{:S(2)}) copy-start(s32[8192]{0:T(1024)} %param.13) | copy-start | bytes 98308
  8.8 5.4 %copy-start = (f32[64,8,128]{2,1,0:T(8,128)S(1)}, f32[64,8,128]{2,1,0:T(8,128)}, u32[]{:S(2)}) copy-start(f32[64,8,128]{2,1,0:T(8,128)} %get-tuple-element.37.keep_ref) | copy-start | bytes 786436
  8.8 8.9 %copy-start.9 = (f32[21,8,128]{2,1,0:T(8,128)S(1)}, f32[21,8,128]{2,1,0:T(8,128)}, u32[]{:S(2)}) copy-start(f32[21,8,128]{2,1,0:T(8,128)} %get-tuple-element.52.refs_0_) | copy-start | bytes 258052
  8.8 5.4 %collective-permute-start = (f32[64,8,128]{2,1,0:T(8,128)}, f32[64,8,128]{2,1,0:T(8,128)S(1)}, u32[]{:S(2)}, u32[]{:S(2)}) collective-permute-start(f32[64,8,128]{2,1,0:T(8,128)} %get-tuple-element.38), channel_id=1, source_target_pairs={{0,4},{4,0},{8,12},{12,8},{16,20},{20,16},{24,28},{28,24},{1,5},{5... | collective-permute-start | bytes 786440 | tf_op jit(solution)/shard_map/halves/ppermute | solution.py:446
  9.6 7.2 %collective-permute-start.1 = (f32[21,8,128]{2,1,0:T(8,128)}, f32[21,8,128]{2,1,0:T(8,128)S(1)}, u32[]{:S(2)}, u32[]{:S(2)}) collective-permute-start(f32[21,8,128]{2,1,0:T(8,128)} %get-tuple-element.49), channel_id=1, source_target_pairs={{0,3},{1,2},{2,1},{3,0},{4,7},{5,6},{6,5},{7,4},{8,11},{9,10},{10,... | collective-permute-start | bytes 258056 | tf_op jit(solution)/shard_map/ppermute | solution.py:441
  9.7 7.9 %collective-permute-start.2 = (f32[21,8,128]{2,1,0:T(8,128)}, f32[21,8,128]{2,1,0:T(8,128)S(1)}, u32[]{:S(2)}, u32[]{:S(2)}) collective-permute-start(f32[21,8,128]{2,1,0:T(8,128)} %get-tuple-element.50), channel_id=1, source_target_pairs={{0,2},{1,3},{2,0},{3,1},{4,6},{5,7},{6,4},{7,5},{8,10},{9,11},{10,... | collective-permute-start | bytes 258056 | tf_op jit(solution)/shard_map/ppermute | solution.py:441
  12.9 4.7 %collective-permute-start.3 = (f32[21,8,128]{2,1,0:T(8,128)}, f32[21,8,128]{2,1,0:T(8,128)S(1)}, u32[]{:S(2)}, u32[]{:S(2)}) collective-permute-start(f32[21,8,128]{2,1,0:T(8,128)} %get-tuple-element.51), channel_id=1, source_target_pairs={{0,1},{1,0},{2,3},{3,2},{4,5},{5,4},{6,7},{7,6},{8,9},{9,8},{10,11... | collective-permute-start | bytes 258056 | tf_op jit(solution)/shard_map/ppermute | solution.py:441
  14.3 8.6 %collective-permute-start.4 = (f32[16,8,128]{2,1,0:T(8,128)S(1)}, f32[16,8,128]{2,1,0:T(8,128)S(1)}, u32[]{:S(2)}, u32[]{:S(2)}) collective-permute-start(f32[16,8,128]{2,1,0:T(8,128)S(1)} %get-tuple-element.40), channel_id=1, source_target_pairs={{0,24},{4,28},{8,16},{12,20},{16,8},{20,12},{24,0},{28,4},{1,25},{... | collective-permute-start | bytes 196616 | tf_op jit(solution)/shard_map/ppermute | solution.py:450
  16.5 6.4 %collective-permute-start.5 = (f32[16,8,128]{2,1,0:T(8,128)S(1)}, f32[16,8,128]{2,1,0:T(8,128)S(1)}, u32[]{:S(2)}, u32[]{:S(2)}) collective-permute-start(f32[16,8,128]{2,1,0:T(8,128)S(1)} %get-tuple-element.41), channel_id=1, source_target_pairs={{0,16},{4,20},{8,24},{12,28},{16,0},{20,4},{24,8},{28,12},{1,17},{... | collective-permute-start | bytes 196616 | tf_op jit(solution)/shard_map/ppermute | solution.py:450
  16.7 6.1 %collective-permute-start.6 = (f32[16,8,128]{2,1,0:T(8,128)S(1)}, f32[16,8,128]{2,1,0:T(8,128)S(1)}, u32[]{:S(2)}, u32[]{:S(2)}) collective-permute-start(f32[16,8,128]{2,1,0:T(8,128)S(1)} %get-tuple-element.42), channel_id=1, source_target_pairs={{0,8},{4,12},{8,0},{12,4},{16,24},{20,28},{24,16},{28,20},{1,9},{5... | collective-permute-start | bytes 196616 | tf_op jit(solution)/shard_map/ppermute | solution.py:450
  17.8 6.2 %collective-permute-start.7 = (f32[5,8,128]{2,1,0:T(8,128)S(1)}, f32[5,8,128]{2,1,0:T(8,128)S(1)}, u32[]{:S(2)}, u32[]{:S(2)}) collective-permute-start(f32[5,8,128]{2,1,0:T(8,128)S(1)} %get-tuple-element.63.refs_0_), channel_id=1, source_target_pairs={{0,3},{1,2},{2,1},{3,0},{4,7},{5,6},{6,5},{7,4},{8,11},{9,10},{10,... | collective-permute-start | bytes 61448 | tf_op jit(solution)/shard_map/ppermute | solution.py:441
  20.0 4.3 %collective-permute-start.8 = (f32[5,8,128]{2,1,0:T(8,128)S(1)}, f32[5,8,128]{2,1,0:T(8,128)S(1)}, u32[]{:S(2)}, u32[]{:S(2)}) collective-permute-start(f32[5,8,128]{2,1,0:T(8,128)S(1)} %get-tuple-element.63.refs_0_), channel_id=1, source_target_pairs={{0,2},{1,3},{2,0},{3,1},{4,6},{5,7},{6,4},{7,5},{8,10},{9,11},{10,... | collective-permute-start | bytes 61448 | tf_op jit(solution)/shard_map/ppermute | solution.py:441
  22.9 2.9 %collective-permute-start.9 = (f32[5,8,128]{2,1,0:T(8,128)S(1)}, f32[5,8,128]{2,1,0:T(8,128)S(1)}, u32[]{:S(2)}, u32[]{:S(2)}) collective-permute-start(f32[5,8,128]{2,1,0:T(8,128)S(1)} %get-tuple-element.63.refs_0_), channel_id=1, source_target_pairs={{0,1},{1,0},{2,3},{3,2},{4,5},{5,4},{6,7},{7,6},{8,9},{9,8},{10,11... | collective-permute-start | bytes 61448 | tf_op jit(solution)/shard_map/ppermute | solution.py:441
  22.9 2.9 %copy-start.2 = (bf16[32,8192]{1,0:T(8,128)(2,1)S(1)}, bf16[32,8192]{1,0:T(8,128)(2,1)}, u32[]{:S(2)}) copy-start(bf16[32,8192]{1,0:T(8,128)(2,1)} %att_ref.1) | copy-start | bytes 1572868
  22.9 2.9 %copy-start.3 = (bf16[5,8192]{1,0:T(8,128)(2,1)S(1)}, bf16[5,8192]{1,0:T(8,128)(2,1)}, u32[]{:S(2)}) copy-start(bf16[5,8192]{1,0:T(8,128)(2,1)} %sp_ref.1) | copy-start | bytes 245764
  22.9 2.9 %copy-start.5 = (f32[8192]{0:T(1024)S(1)}, f32[8192]{0:T(1024)}, u32[]{:S(2)}) copy-start(f32[8192]{0:T(1024)} %param.10) | copy-start | bytes 98308
  22.9 2.9 %copy-start.6 = (f32[8192]{0:T(1024)S(1)}, f32[8192]{0:T(1024)}, u32[]{:S(2)}) copy-start(f32[8192]{0:T(1024)} %param.9) | copy-start | bytes 98308
  22.9 2.9 %copy-start.8 = (s32[64]{0:T(128)S(1)}, s32[64]{0:T(128)}, u32[]{:S(2)}) copy-start(s32[64]{0:T(128)} %win_ref.3) | copy-start | bytes 772
  28.1 18.1 %copy-start.4 = (f32[5,4096]{1,0:T(8,128)S(1)}, f32[5,4096]{1,0:T(8,128)}, u32[]{:S(2)}) copy-start(f32[5,4096]{1,0:T(8,128)} %sources_ref.1) | copy-start | bytes 245764
  28.1 18.9 %copy-start.7 = (f32[128,32]{0,1:T(8,128)S(1)}, f32[128,32]{0,1:T(8,128)}, u32[]{:S(2)}) copy-start(f32[128,32]{0,1:T(8,128)} %param.16) | copy-start | bytes 49156
  28.1 3.2 %collective-permute-start.10 = (f32[32,128]{1,0:T(8,128)S(1)}, f32[32,128]{1,0:T(8,128)S(1)}, u32[]{:S(2)}, u32[]{:S(2)}) collective-permute-start(f32[32,128]{1,0:T(8,128)S(1)} %right_sides.1.mine_ref), channel_id=1, source_target_pairs={{0,4},{4,0},{8,12},{12,8},{16,20},{20,16},{24,28},{28,24},{1,5},{5... | collective-permute-start | bytes 49160 | tf_op jit(solution)/shard_map/send/ppermute | solution.py:446
  31.5 4.1 %collective-permute-start.11 = (f32[18,8,128]{2,1,0:T(8,128)S(1)}, f32[18,8,128]{2,1,0:T(8,128)S(1)}, u32[]{:S(2)}, u32[]{:S(2)}) collective-permute-start(f32[18,8,128]{2,1,0:T(8,128)S(1)} %send.1.refs_0_), channel_id=1, source_target_pairs={{0,24},{4,28},{8,16},{12,20},{16,8},{20,12},{24,0},{28,4},{1,25},{... | collective-permute-start | bytes 221192 | tf_op jit(solution)/shard_map/ppermute | solution.py:450
  33.6 3.8 %collective-permute-start.12 = (f32[18,8,128]{2,1,0:T(8,128)S(1)}, f32[18,8,128]{2,1,0:T(8,128)S(1)}, u32[]{:S(2)}, u32[]{:S(2)}) collective-permute-start(f32[18,8,128]{2,1,0:T(8,128)S(1)} %send.1.refs_0_), channel_id=1, source_target_pairs={{0,16},{4,20},{8,24},{12,28},{16,0},{20,4},{24,8},{28,12},{1,17},{... | collective-permute-start | bytes 221192 | tf_op jit(solution)/shard_map/ppermute | solution.py:450
  33.9 3.7 %collective-permute-start.13 = (f32[18,8,128]{2,1,0:T(8,128)S(1)}, f32[18,8,128]{2,1,0:T(8,128)S(1)}, u32[]{:S(2)}, u32[]{:S(2)}) collective-permute-start(f32[18,8,128]{2,1,0:T(8,128)S(1)} %send.1.refs_0_), channel_id=1, source_target_pairs={{0,8},{4,12},{8,0},{12,4},{16,24},{20,28},{24,16},{28,20},{1,9},{5... | collective-permute-start | bytes 221192 | tf_op jit(solution)/shard_map/ppermute | solution.py:450
  37.5 4.7 %collective-permute-start.14 = (f32[10,8,128]{2,1,0:T(8,128)S(1)}, f32[10,8,128]{2,1,0:T(8,128)S(1)}, u32[]{:S(2)}, u32[]{:S(2)}) collective-permute-start(f32[10,8,128]{2,1,0:T(8,128)S(1)} %get-tuple-element.70), channel_id=1, source_target_pairs={{4,5},{1,2},{6,7},{12,13},{9,10},{14,15},{20,21},{17,18},{22,23},{... | collective-permute-start | bytes 122888 | tf_op jit(solution)/shard_map/ppermute | solution.py:555
  39.5 3.0 %collective-permute-start.15 = (f32[10,8,128]{2,1,0:T(8,128)S(1)}, f32[10,8,128]{2,1,0:T(8,128)S(1)}, u32[]{:S(2)}, u32[]{:S(2)}) collective-permute-start(f32[10,8,128]{2,1,0:T(8,128)S(1)} %get-tuple-element.71), channel_id=1, source_target_pairs={{0,4},{4,0},{8,12},{12,8},{16,20},{20,16},{24,28},{28,24},{1,5},{5... | collective-permute-start | bytes 122888 | tf_op jit(solution)/shard_map/ppermute | solution.py:446
  43.5 3.5 %collective-permute-start.16 = (f32[32,128]{1,0:T(8,128)S(1)}, f32[32,128]{1,0:T(8,128)S(1)}, u32[]{:S(2)}, u32[]{:S(2)}) collective-permute-start(f32[32,128]{1,0:T(8,128)S(1)} %sweeps.1.mine_ref), channel_id=1, source_target_pairs={{0,4},{4,0},{8,12},{12,8},{16,20},{20,16},{24,28},{28,24},{1,5},{5... | collective-permute-start | bytes 49160 | tf_op jit(solution)/shard_map/finish/ppermute | solution.py:446

commit v7 on v6

--- a/solution.py
+++ b/solution.py
@@ -226,10 +226,14 @@
     ties_ref[2] = placed(before, own, after)
 
 
+def lower_blocks(groups):
+    return [(g, h) for g in range(groups) for h in range(g + 1)]
+
+
 def invert_kernel(sky_ref, ties_ref, *refs):
     parts, (out_ref, flat) = refs[:-2], refs[-2:]
-    own = out_ref.shape[0]
-    knots = math.isqrt(out_ref.shape[1] * LANES)
+    own, cell_rows, _ = parts[0].shape
+    knots = math.isqrt(cell_rows * LANES)
     groups = knots // 8
     total = parts[0][...]
     for part in parts[1:]:
@@ -264,8 +268,8 @@
             ]
         for i in range(STEP):
             rows[mine] = jnp.where(offset == first + i, pivots[i], rows[mine])
-    flat[...] = -jnp.concatenate(rows, axis=0).T
-    out_ref[...] = flat[0 : own * 8, :].reshape(own, 8, LANES)
+    for at, (g, h) in enumerate(lower_blocks(groups)):
+        out_ref[at] = -rows[g][8 * h : 8 * (h + 1)]
 
 
 def low_kernel(half, src_ref, out_ref):
@@ -328,13 +332,13 @@
 
 
 def send_kernel(sky_ref, inv_ref, mine_ref, theirs_ref, out_ref):
-    own = inv_ref.shape[0]
+    kept = inv_ref.shape[0]
     core = lax.rem(sky_ref[0], CORES)
     total = mine_ref[...] + theirs_ref[...]
     total = jnp.where(core == 0, total, pltpu.roll(total, HALF, 1))
     packed = narrow(total)
-    out_ref[0:own] = inv_ref[...]
-    out_ref[own:] = packed.reshape(packed.shape[0] // 8, 8, LANES)
+    out_ref[0:kept] = inv_ref[...]
+    out_ref[kept:] = packed.reshape(packed.shape[0] // 8, 8, LANES)
 
 
 def narrow(x):
@@ -350,13 +354,16 @@
 def rim_kernel(sky_ref, *refs):
     chips = len(refs) - 3
     parts, (inner_ref, outer_ref, main_ref) = refs[:chips], refs[chips:]
-    own = parts[0].shape[0] - (main_ref.shape[0] - HALF)
+    own = HALF // chips
+    kept = parts[0].shape[0] - (main_ref.shape[0] - HALF)
     core, chip = lax.rem(sky_ref[0], CORES), sky_ref[0] // CORES
-    sides = parts[0][own:]
+    sides = parts[0][kept:]
     for part in parts[1:]:
-        sides = sides + part[own:]
+        sides = sides + part[kept:]
+    blank = jnp.zeros((LANES - kept * 8, LANES), F32)
     for part, mask in zip(parts, masks(chips)):
-        main_ref[pl.ds((chip ^ mask) * own, own)] = part[0:own]
+        turned = jnp.concatenate([part[0:kept].reshape(kept * 8, LANES), blank], axis=0).T
+        main_ref[pl.ds((chip ^ mask) * own, own)] = turned[0 : own * 8].reshape(own, 8, LANES)
     main_ref[HALF:] = sides
     inner_ref[0:8] = main_ref[pl.ds((1 - core) * (HALF - 8), 8)]
     outer_ref[0:8] = main_ref[pl.ds(core * (HALF - 8), 8)]
@@ -364,9 +371,8 @@
     outer_ref[8:] = sides
 
 
-def sweeps_kernel(sky_ref, main_ref, outer_ref, inner_ref, ties_ref, out_ref, flat, cells, vector):
+def sweeps_kernel(sky_ref, main_ref, outer_ref, inner_ref, ties_ref, out_ref, flat, turns, cells, vector):
     knots = out_ref.shape[0]
-    groups = LANES // knots
     core = lax.rem(sky_ref[0], CORES)
     low = jnp.where(core == 0, outer_ref[...], inner_ref[...])
     high = jnp.where(core == 0, inner_ref[...], outer_ref[...])
@@ -375,9 +381,14 @@
     flat[HALF * 8 : HALF * 8 + 64, :] = high[0:8].reshape(64, LANES)
     flat[LANES * 8 - 64 : LANES * 8, :] = low[0:8].reshape(64, LANES)
     for r in range(8):
-        turned = flat[pl.ds(r, LANES, stride=8), :].T
-        for g in range(groups):
-            cells[(8 * g + r) * knots : (8 * g + r + 1) * knots, :] = turned[g * knots : (g + 1) * knots]
+        turns[r * LANES : (r + 1) * LANES, :] = flat[pl.ds(r, LANES, stride=8), :].T
+    for at, (g, h) in enumerate(lower_blocks(knots // 8)):
+        for r in range(8):
+            to = (8 * g + r) * knots + 8 * h
+            cells[to : to + 8, :] = turns[r * LANES + 8 * at : r * LANES + 8 * (at + 1), :]
+            if g != h:
+                to = (8 * h + r) * knots + 8 * g
+                cells[to : to + 8, :] = turns[pl.ds(8 * at + r, 8, stride=LANES), :]
 
     def wide(x):
         return widen(x.reshape(knots // 2, LANES))
@@ -508,7 +519,7 @@
     with jax.named_scope("invert"):
         inverse = call(
             invert_kernel,
-            jax.ShapeDtypeStruct((own, cell_rows, LANES), F32),
+            jax.ShapeDtypeStruct((len(lower_blocks(knots // 8)), 8, LANES), F32),
             [smem()] + [vmem()] * (1 + chips),
             [pltpu.VMEM((LANES, LANES), F32)],
             micros=3,
@@ -539,7 +550,7 @@
         sides = knots // 2 // 8
         sent = call(
             send_kernel,
-            jax.ShapeDtypeStruct((own + sides, 8, LANES), F32),
+            jax.ShapeDtypeStruct((inverse.shape[0] + sides, 8, LANES), F32),
             [smem()] + [vmem()] * 3,
         )(sky, inverse, part, other_core(part))
     got = other_chips([sent] * chips)
@@ -561,6 +572,7 @@
             [smem()] + [vmem()] * 4,
             [
                 pltpu.VMEM((cell_rows * LANES, LANES), F32),
+                pltpu.VMEM((cell_rows * LANES, LANES), F32),
                 pltpu.VMEM((knots * knots, LANES), F32),
                 pltpu.VMEM((knots, LANES), F32),
             ],

time: 47.9 us -> 47.9 us (level)
  the two profiles are of different devices: /device:TPU:17 before, /device:TPU:13 now
where the time goes in v7:
time: 47.9 us; the launch traced here: 47.6 us
  starting transfers between devices  22.7 us (47%)
  Pallas kernels  15.7 us (33%)
  waiting for transfers between devices  8.36 us (17%)
  between operations  0.83 us (2%)
    pallas_call x1, Pallas kernels, on_device(): call(functools.partial(sums_kernel, hi_count), [block] * peers + [half] *...  8.13 us
    ppermute x4, starting transfers between devices, other_core(): return lax.ppermute(x, 'sky', [(i, i ^ 1) for i in range(devices)])  7.05 us
    ppermute x6, starting transfers between devices, swapped(): lax.ppermute(block, 'tm', [(i, i ^ mask) for i in range(peers)])  6.68 us
    ppermute x6, starting transfers between devices, other_chips(): lax.ppermute(block, 'sky', [(i, i ^ CORES * mask) for i in range(devices)])  6.32 us
    ppermute x6, waiting for transfers between devices, swapped(): lax.ppermute(block, 'tm', [(i, i ^ mask) for i in range(peers)])  3.55 us
    ppermute x6, waiting for transfers between devices, other_chips(): lax.ppermute(block, 'sky', [(i, i ^ CORES * mask) for i in range(devices)])  2.98 us
    ppermute x1, starting transfers between devices, on_device(): lax.ppermute(outer, ('sky', 'tm'), list(zip(upper + lower, lower + upper)))  2.65 us
    pallas_call x1, Pallas kernels, on_device(): call(functools.partial(rhs_kernel, hi_count), jax.ShapeDtypeStruct((knots...  2.29 us
  transfers between devices with their start and end apart: 17, of which 10 were waited for; matrix products, arithmetic and copies ran while one was open for 0% of the time, Pallas kernels for 7%

profile of v7, /device:TPU:13, one launch (start us, length us, event | category | flops | bytes accessed | tf_op | source)
XLA Modules:
  0.0 47.6 jit_solution(5195784289886721775)
XLA Ops:
  0.6 0.0 copy-start.1
  0.6 8.1 %sums.1 = (f32[21,8,128]{2,1,0:T(8,128)}, f32[21,8,128]{2,1,0:T(8,128)}, f32[21,8,128]{2,1,0:T(8,128)}, f32[21,8,128]{2,1,0:T(8,128)}, f32[64,8,128]{2,1,0:T(8,128)}, /*index=5*/f32[64,8,128]{2,1,0:T(8,128)}) custom-call(s32[1]{0:T(128)} %bitcast.me_ref, s32[1]{0:T(128)} %bitcast.1.sky_ref, s32[64]{0:T(128)} %win_ref.3, s32[64,128]{1,0:T(8,128)} %bitcast.8, ...), custom_call_target="tpu_custom_call" | custom-call | flops 8999999488 | tf_op jit(solution)/shard_map/sums/pallas_call | solution.py:468
  8.8 0.0 copy-start
  8.8 0.0 copy-start.9
  8.8 0.7 %collective-permute-start = (f32[64,8,128]{2,1,0:T(8,128)}, f32[64,8,128]{2,1,0:T(8,128)S(1)}, u32[]{:S(2)}, u32[]{:S(2)}) collective-permute-start(f32[64,8,128]{2,1,0:T(8,128)} %get-tuple-element.38), channel_id=1, source_target_pairs={{0,4},{4,0},{8,12},{12,8},{16,20},{20,16},{24,28},{28,24},{1,5},{5... | collective-permute-start | bytes 786440 | tf_op jit(solution)/shard_map/halves/ppermute | solution.py:457
  9.6 1.3 %collective-permute-start.1 = (f32[21,8,128]{2,1,0:T(8,128)}, f32[21,8,128]{2,1,0:T(8,128)S(1)}, u32[]{:S(2)}, u32[]{:S(2)}) collective-permute-start(f32[21,8,128]{2,1,0:T(8,128)} %get-tuple-element.49), channel_id=1, source_target_pairs={{0,3},{1,2},{2,1},{3,0},{4,7},{5,6},{6,5},{7,4},{8,11},{9,10},{10,... | collective-permute-start | bytes 258056 | tf_op jit(solution)/shard_map/ppermute | solution.py:452
  10.9 1.0 %collective-permute-start.2 = (f32[21,8,128]{2,1,0:T(8,128)}, f32[21,8,128]{2,1,0:T(8,128)S(1)}, u32[]{:S(2)}, u32[]{:S(2)}) collective-permute-start(f32[21,8,128]{2,1,0:T(8,128)} %get-tuple-element.50), channel_id=1, source_target_pairs={{0,2},{1,3},{2,0},{3,1},{4,6},{5,7},{6,4},{7,5},{8,10},{9,11},{10,... | collective-permute-start | bytes 258056 | tf_op jit(solution)/shard_map/ppermute | solution.py:452
  11.9 1.2 %collective-permute-start.3 = (f32[21,8,128]{2,1,0:T(8,128)}, f32[21,8,128]{2,1,0:T(8,128)S(1)}, u32[]{:S(2)}, u32[]{:S(2)}) collective-permute-start(f32[21,8,128]{2,1,0:T(8,128)} %get-tuple-element.51), channel_id=1, source_target_pairs={{0,1},{1,0},{2,3},{3,2},{4,5},{5,4},{6,7},{7,6},{8,9},{9,8},{10,11... | collective-permute-start | bytes 258056 | tf_op jit(solution)/shard_map/ppermute | solution.py:452
  13.1 0.0 copy-done.1
  13.1 1.2 %one_hot.1.low_ref = bf16[256,8192]{1,0:T(8,128)(2,1)S(1)} custom-call(s32[64,128]{1,0:T(8,128)S(1)} %bitcast.9), custom_call_target="tpu_custom_call" | custom-call | flops 1000000000 | tf_op jit(solution)/shard_map/one_hot/pallas_call | solution.py:499
  14.3 0.0 collective-permute-done.got_ref
  14.3 0.0 copy-done
  14.3 0.1 halves.1
  14.4 1.2 %collective-permute-start.4 = (f32[16,8,128]{2,1,0:T(8,128)S(1)}, f32[16,8,128]{2,1,0:T(8,128)S(1)}, u32[]{:S(2)}, u32[]{:S(2)}) collective-permute-start(f32[16,8,128]{2,1,0:T(8,128)S(1)} %get-tuple-element.40), channel_id=1, source_target_pairs={{0,24},{4,28},{8,16},{12,20},{16,8},{20,12},{24,0},{28,4},{1,25},{... | collective-permute-start | bytes 196616 | tf_op jit(solution)/shard_map/ppermute | solution.py:461
  15.6 1.2 %collective-permute-start.5 = (f32[16,8,128]{2,1,0:T(8,128)S(1)}, f32[16,8,128]{2,1,0:T(8,128)S(1)}, u32[]{:S(2)}, u32[]{:S(2)}) collective-permute-start(f32[16,8,128]{2,1,0:T(8,128)S(1)} %get-tuple-element.41), channel_id=1, source_target_pairs={{0,16},{4,20},{8,24},{12,28},{16,0},{20,4},{24,8},{28,12},{1,17},{... | collective-permute-start | bytes 196616 | tf_op jit(solution)/shard_map/ppermute | solution.py:461
  16.8 0.7 %collective-permute-done.1.refs_1_ = f32[21,8,128]{2,1,0:T(8,128)S(1)} collective-permute-done((f32[21,8,128]{2,1,0:T(8,128)}, f32[21,8,128]{2,1,0:T(8,128)S(1)}, u32[]{:S(2)}, u32[]{:S(2)}) %collective-permute-start.1) | collective-permute-done | bytes 86048 | tf_op jit(solution)/shard_map/ppermute | solution.py:452
  17.6 1.2 %collective-permute-start.6 = (f32[16,8,128]{2,1,0:T(8,128)S(1)}, f32[16,8,128]{2,1,0:T(8,128)S(1)}, u32[]{:S(2)}, u32[]{:S(2)}) collective-permute-start(f32[16,8,128]{2,1,0:T(8,128)S(1)} %get-tuple-element.42), channel_id=1, source_target_pairs={{0,8},{4,12},{8,0},{12,4},{16,24},{20,28},{24,16},{28,20},{1,9},{5... | collective-permute-start | bytes 196616 | tf_op jit(solution)/shard_map/ppermute | solution.py:461
  18.8 0.0 collective-permute-done.2.refs_2_
  18.8 0.9 %collective-permute-done.3.refs_3_ = f32[21,8,128]{2,1,0:T(8,128)S(1)} collective-permute-done((f32[21,8,128]{2,1,0:T(8,128)}, f32[21,8,128]{2,1,0:T(8,128)S(1)}, u32[]{:S(2)}, u32[]{:S(2)}) %collective-permute-start.3) | collective-permute-done | bytes 86048 | tf_op jit(solution)/shard_map/ppermute | solution.py:452
  19.6 0.0 copy-done.9
  19.6 0.2 solve.1
  19.8 0.0 collective-permute-start.7
  19.8 3.0 %collective-permute-start.8 = (f32[5,8,128]{2,1,0:T(8,128)S(1)}, f32[5,8,128]{2,1,0:T(8,128)S(1)}, u32[]{:S(2)}, u32[]{:S(2)}) collective-permute-start(f32[5,8,128]{2,1,0:T(8,128)S(1)} %get-tuple-element.63.refs_0_), channel_id=1, source_target_pairs={{0,2},{1,3},{2,0},{3,1},{4,6},{5,7},{6,4},{7,5},{8,10},{9,11},{10,... | collective-permute-start | bytes 61448 | tf_op jit(solution)/shard_map/ppermute | solution.py:452
  22.9 0.0 collective-permute-done.4.refs_1_
  22.9 0.1 collective-permute-start.9
  23.0 0.0 collective-permute-done.5.refs_2_
  23.0 0.0 collective-permute-done.6.refs_3_
  23.0 0.0 copy-start.2
  23.0 0.0 copy-start.3
  23.0 0.0 copy-start.5
  23.0 0.0 copy-start.6
  23.0 0.0 copy-start.8
  23.0 1.0 %invert.1.inv_ref = f32[10,8,128]{2,1,0:T(8,128)S(1)} custom-call(s32[1]{0:T(128)} %bitcast.1.sky_ref, f32[3,8,128]{2,1,0:T(8,128)S(1)} %get-tuple-element.56.ties_ref, f32[16,8,128]{2,1,0:T(8,128)S(1)} %get-tuple-element.39.refs_0_, f32[16,8,128]{2,1,0:T(8,128)S(1)} %collective-permute-done.4.refs_1_, f32[16,8,128]{2,1,0:T(8,128)S(1)} %collective-permute-done.5.refs_2_, ...), custom_call_target="tpu_custom_call" | custom-call | flops 3000000000 | tf_op jit(solution)/shard_map/invert/pallas_call | solution.py:520
  24.0 0.0 collective-permute-done.7.refs_1_
  24.0 0.2 collective-permute-done.8.refs_2_
  24.2 1.8 %collective-permute-done.9.refs_3_ = f32[5,8,128]{2,1,0:T(8,128)S(1)} collective-permute-done((f32[5,8,128]{2,1,0:T(8,128)S(1)}, f32[5,8,128]{2,1,0:T(8,128)S(1)}, u32[]{:S(2)}, u32[]{:S(2)}) %collective-permute-start.9) | collective-permute-done | bytes 20512 | tf_op jit(solution)/shard_map/ppermute | solution.py:452
  26.0 0.0 copy-done.2
  26.0 0.0 copy-done.3
  26.0 0.0 copy-done.5
  26.0 0.0 copy-done.6
  26.0 0.0 copy-done.8
  26.0 2.3 %right_sides.1.mine_ref = f32[32,128]{1,0:T(8,128)S(1)} custom-call(s32[1]{0:T(128)} %bitcast.me_ref, s32[64]{0:T(128)S(1)} %copy-done.8, bf16[256,8192]{1,0:T(8,128)(2,1)S(1)} %one_hot.1.low_ref, s32[64,128]{1,0:T(8,128)S(1)} %bitcast.10, f32[64,128]{1,0:T(8,128)S(1)} %bitcast.12, f32[64,128]{1,0:T(8,128)S(1)} %bitcast.14, bf16[5,8192]{1,0:T(8,128)(2,1)S(1)} %copy-done.3, ...), custom_call_target="tpu_custom_call" | custom-call | flops 6000000000 | tf_op jit(solution)/shard_map/right_sides/pallas_call | solution.py:529
  28.3 0.0 copy-start.7
  28.4 2.1 %collective-permute-start.10 = (f32[32,128]{1,0:T(8,128)S(1)}, f32[32,128]{1,0:T(8,128)S(1)}, u32[]{:S(2)}, u32[]{:S(2)}) collective-permute-start(f32[32,128]{1,0:T(8,128)S(1)} %right_sides.1.mine_ref), channel_id=1, source_target_pairs={{0,4},{4,0},{8,12},{12,8},{16,20},{20,16},{24,28},{28,24},{1,5},{5... | collective-permute-start | bytes 49160 | tf_op jit(solution)/shard_map/send/ppermute | solution.py:457
  30.5 0.8 %collective-permute-done.10.theirs_ref = f32[32,128]{1,0:T(8,128)S(1)} collective-permute-done((f32[32,128]{1,0:T(8,128)S(1)}, f32[32,128]{1,0:T(8,128)S(1)}, u32[]{:S(2)}, u32[]{:S(2)}) %collective-permute-start.10) | collective-permute-done | bytes 16416 | tf_op jit(solution)/shard_map/send/ppermute | solution.py:457
  31.3 0.1 send.1.refs_0_
  31.4 1.2 %collective-permute-start.11 = (f32[12,8,128]{2,1,0:T(8,128)S(1)}, f32[12,8,128]{2,1,0:T(8,128)S(1)}, u32[]{:S(2)}, u32[]{:S(2)}) collective-permute-start(f32[12,8,128]{2,1,0:T(8,128)S(1)} %send.1.refs_0_), channel_id=1, source_target_pairs={{0,24},{4,28},{8,16},{12,20},{16,8},{20,12},{24,0},{28,4},{1,25},{... | collective-permute-start | bytes 147464 | tf_op jit(solution)/shard_map/ppermute | solution.py:461
  32.6 1.2 %collective-permute-start.12 = (f32[12,8,128]{2,1,0:T(8,128)S(1)}, f32[12,8,128]{2,1,0:T(8,128)S(1)}, u32[]{:S(2)}, u32[]{:S(2)}) collective-permute-start(f32[12,8,128]{2,1,0:T(8,128)S(1)} %send.1.refs_0_), channel_id=1, source_target_pairs={{0,16},{4,20},{8,24},{12,28},{16,0},{20,4},{24,8},{28,12},{1,17},{... | collective-permute-start | bytes 147464 | tf_op jit(solution)/shard_map/ppermute | solution.py:461
  33.8 0.3 collective-permute-start.13
  34.1 1.2 %collective-permute-done.11.refs_1_ = f32[12,8,128]{2,1,0:T(8,128)S(1)} collective-permute-done((f32[12,8,128]{2,1,0:T(8,128)S(1)}, f32[12,8,128]{2,1,0:T(8,128)S(1)}, u32[]{:S(2)}, u32[]{:S(2)}) %collective-permute-start.11) | collective-permute-done | bytes 49184 | tf_op jit(solution)/shard_map/ppermute | solution.py:461
  35.3 1.5 %collective-permute-done.12.refs_2_ = f32[12,8,128]{2,1,0:T(8,128)S(1)} collective-permute-done((f32[12,8,128]{2,1,0:T(8,128)S(1)}, f32[12,8,128]{2,1,0:T(8,128)S(1)}, u32[]{:S(2)}, u32[]{:S(2)}) %collective-permute-start.12) | collective-permute-done | bytes 49184 | tf_op jit(solution)/shard_map/ppermute | solution.py:461
  36.8 0.2 collective-permute-done.13.refs_3_
  37.1 0.1 rims.1
  37.2 2.6 %collective-permute-start.14 = (f32[10,8,128]{2,1,0:T(8,128)S(1)}, f32[10,8,128]{2,1,0:T(8,128)S(1)}, u32[]{:S(2)}, u32[]{:S(2)}) collective-permute-start(f32[10,8,128]{2,1,0:T(8,128)S(1)} %get-tuple-element.70), channel_id=1, source_target_pairs={{4,5},{1,2},{6,7},{12,13},{9,10},{14,15},{20,21},{17,18},{22,23},{... | collective-permute-start | bytes 122888 | tf_op jit(solution)/shard_map/ppermute | solution.py:566
  39.9 2.7 %collective-permute-start.15 = (f32[10,8,128]{2,1,0:T(8,128)S(1)}, f32[10,8,128]{2,1,0:T(8,128)S(1)}, u32[]{:S(2)}, u32[]{:S(2)}) collective-permute-start(f32[10,8,128]{2,1,0:T(8,128)S(1)} %get-tuple-element.71), channel_id=1, source_target_pairs={{0,4},{4,0},{8,12},{12,8},{16,20},{20,16},{24,28},{28,24},{1,5},{5... | collective-permute-start | bytes 122888 | tf_op jit(solution)/shard_map/ppermute | solution.py:457
  42.5 0.0 collective-permute-done.14.outer_ref
  42.5 0.9 %collective-permute-done.15.inner_ref = f32[10,8,128]{2,1,0:T(8,128)S(1)} collective-permute-done((f32[10,8,128]{2,1,0:T(8,128)S(1)}, f32[10,8,128]{2,1,0:T(8,128)S(1)}, u32[]{:S(2)}, u32[]{:S(2)}) %collective-permute-start.15) | collective-permute-done | bytes 40992 | tf_op jit(solution)/shard_map/ppermute | solution.py:457
  43.4 1.2 %sweeps.1.mine_ref = f32[32,128]{1,0:T(8,128)S(1)} custom-call(s32[1]{0:T(128)} %bitcast.1.sky_ref, f32[66,8,128]{2,1,0:T(8,128)S(1)} %get-tuple-element.69.main_ref, f32[10,8,128]{2,1,0:T(8,128)S(1)} %collective-permute-done.14.outer_ref, f32[10,8,128]{2,1,0:T(8,128)S(1)} %collective-permute-done.15.inner_ref, f32[3,8,128]{2,1,0:T(8,128)S(1)} %get-tuple-element.56.ties_ref), custom_call_target="tpu_custom_call" | custom-call | flops 1000000000 | tf_op jit(solution)/shard_map/sweeps/pallas_call | solution.py:569
  44.6 1.5 %collective-permute-start.16 = (f32[32,128]{1,0:T(8,128)S(1)}, f32[32,128]{1,0:T(8,128)S(1)}, u32[]{:S(2)}, u32[]{:S(2)}) collective-permute-start(f32[32,128]{1,0:T(8,128)S(1)} %sweeps.1.mine_ref), channel_id=1, source_target_pairs={{0,4},{4,0},{8,12},{12,8},{16,20},{20,16},{24,28},{28,24},{1,5},{5... | collective-permute-start | bytes 49160 | tf_op jit(solution)/shard_map/finish/ppermute | solution.py:457
  46.1 0.0 copy-done.4
  46.1 0.7 %update.1 = f32[5,4096]{1,0:T(8,128)} custom-call(s32[1]{0:T(128)} %bitcast.me_ref, f32[5,4096]{1,0:T(8,128)S(1)} %copy-done.4, f32[5,8,128]{2,1,0:T(8,128)S(1)} %get-tuple-element.63.refs_0_, f32[5,8,128]{2,1,0:T(8,128)S(1)} %collective-permute-done.7.refs_1_, f32[5,8,128]{2,1,0:T(8,128)S(1)} %collective-permute-done.8.refs_2_, ...), custom_call_target="tpu_custom_call" | custom-call | flops 100000000 | tf_op jit(solution)/shard_map/update/pallas_call | solution.py:543
  46.8 0.1 collective-permute-done.16.theirs_ref
  47.0 0.0 copy-done.7
  47.0 0.7 %finish.1 = f32[32,128]{1,0:T(8,128)} custom-call(s32[1]{0:T(128)} %bitcast.1.sky_ref, f32[32,128]{1,0:T(8,128)S(1)} %sweeps.1.mine_ref, f32[32,128]{1,0:T(8,128)S(1)} %collective-permute-done.16.theirs_ref, f32[32,128]{1,0:T(8,128)S(1)} %bitcast.15), custom_call_target="tpu_custom_call" | custom-call | flops 100000000 | tf_op jit(solution)/shard_map/finish/pallas_call | solution.py:582
  (1 shorter events, 0.0 us)
Async XLA Ops:
  0.6 12.4 %copy-start.1 = (s32[8192]{0:T(1024)S(1)}, s32[8192]{0:T(1024)}, u32[]{:S(2)}) copy-start(s32[8192]{0:T(1024)} %param.13) | copy-start | bytes 98308
  8.8 5.5 %copy-start = (f32[64,8,128]{2,1,0:T(8,128)S(1)}, f32[64,8,128]{2,1,0:T(8,128)}, u32[]{:S(2)}) copy-start(f32[64,8,128]{2,1,0:T(8,128)} %get-tuple-element.37.keep_ref) | copy-start | bytes 786436
  8.8 10.8 %copy-start.9 = (f32[21,8,128]{2,1,0:T(8,128)S(1)}, f32[21,8,128]{2,1,0:T(8,128)}, u32[]{:S(2)}) copy-start(f32[21,8,128]{2,1,0:T(8,128)} %get-tuple-element.52.refs_0_) | copy-start | bytes 258052
  8.8 5.5 %collective-permute-start = (f32[64,8,128]{2,1,0:T(8,128)}, f32[64,8,128]{2,1,0:T(8,128)S(1)}, u32[]{:S(2)}, u32[]{:S(2)}) collective-permute-start(f32[64,8,128]{2,1,0:T(8,128)} %get-tuple-element.38), channel_id=1, source_target_pairs={{0,4},{4,0},{8,12},{12,8},{16,20},{20,16},{24,28},{28,24},{1,5},{5... | collective-permute-start | bytes 786440 | tf_op jit(solution)/shard_map/halves/ppermute | solution.py:457
  9.6 8.0 %collective-permute-start.1 = (f32[21,8,128]{2,1,0:T(8,128)}, f32[21,8,128]{2,1,0:T(8,128)S(1)}, u32[]{:S(2)}, u32[]{:S(2)}) collective-permute-start(f32[21,8,128]{2,1,0:T(8,128)} %get-tuple-element.49), channel_id=1, source_target_pairs={{0,3},{1,2},{2,1},{3,0},{4,7},{5,6},{6,5},{7,4},{8,11},{9,10},{10,... | collective-permute-start | bytes 258056 | tf_op jit(solution)/shard_map/ppermute | solution.py:452
  10.9 7.9 %collective-permute-start.2 = (f32[21,8,128]{2,1,0:T(8,128)}, f32[21,8,128]{2,1,0:T(8,128)S(1)}, u32[]{:S(2)}, u32[]{:S(2)}) collective-permute-start(f32[21,8,128]{2,1,0:T(8,128)} %get-tuple-element.50), channel_id=1, source_target_pairs={{0,2},{1,3},{2,0},{3,1},{4,6},{5,7},{6,4},{7,5},{8,10},{9,11},{10,... | collective-permute-start | bytes 258056 | tf_op jit(solution)/shard_map/ppermute | solution.py:452
  11.9 7.8 %collective-permute-start.3 = (f32[21,8,128]{2,1,0:T(8,128)}, f32[21,8,128]{2,1,0:T(8,128)S(1)}, u32[]{:S(2)}, u32[]{:S(2)}) collective-permute-start(f32[21,8,128]{2,1,0:T(8,128)} %get-tuple-element.51), channel_id=1, source_target_pairs={{0,1},{1,0},{2,3},{3,2},{4,5},{5,4},{6,7},{7,6},{8,9},{9,8},{10,11... | collective-permute-start | bytes 258056 | tf_op jit(solution)/shard_map/ppermute | solution.py:452
  14.4 8.5 %collective-permute-start.4 = (f32[16,8,128]{2,1,0:T(8,128)S(1)}, f32[16,8,128]{2,1,0:T(8,128)S(1)}, u32[]{:S(2)}, u32[]{:S(2)}) collective-permute-start(f32[16,8,128]{2,1,0:T(8,128)S(1)} %get-tuple-element.40), channel_id=1, source_target_pairs={{0,24},{4,28},{8,16},{12,20},{16,8},{20,12},{24,0},{28,4},{1,25},{... | collective-permute-start | bytes 196616 | tf_op jit(solution)/shard_map/ppermute | solution.py:461
  15.6 7.4 %collective-permute-start.5 = (f32[16,8,128]{2,1,0:T(8,128)S(1)}, f32[16,8,128]{2,1,0:T(8,128)S(1)}, u32[]{:S(2)}, u32[]{:S(2)}) collective-permute-start(f32[16,8,128]{2,1,0:T(8,128)S(1)} %get-tuple-element.41), channel_id=1, source_target_pairs={{0,16},{4,20},{8,24},{12,28},{16,0},{20,4},{24,8},{28,12},{1,17},{... | collective-permute-start | bytes 196616 | tf_op jit(solution)/shard_map/ppermute | solution.py:461
  17.6 5.4 %collective-permute-start.6 = (f32[16,8,128]{2,1,0:T(8,128)S(1)}, f32[16,8,128]{2,1,0:T(8,128)S(1)}, u32[]{:S(2)}, u32[]{:S(2)}) collective-permute-start(f32[16,8,128]{2,1,0:T(8,128)S(1)} %get-tuple-element.42), channel_id=1, source_target_pairs={{0,8},{4,12},{8,0},{12,4},{16,24},{20,28},{24,16},{28,20},{1,9},{5... | collective-permute-start | bytes 196616 | tf_op jit(solution)/shard_map/ppermute | solution.py:461
  19.8 4.2 %collective-permute-start.7 = (f32[5,8,128]{2,1,0:T(8,128)S(1)}, f32[5,8,128]{2,1,0:T(8,128)S(1)}, u32[]{:S(2)}, u32[]{:S(2)}) collective-permute-start(f32[5,8,128]{2,1,0:T(8,128)S(1)} %get-tuple-element.63.refs_0_), channel_id=1, source_target_pairs={{0,3},{1,2},{2,1},{3,0},{4,7},{5,6},{6,5},{7,4},{8,11},{9,10},{10,... | collective-permute-start | bytes 61448 | tf_op jit(solution)/shard_map/ppermute | solution.py:452
  19.8 4.4 %collective-permute-start.8 = (f32[5,8,128]{2,1,0:T(8,128)S(1)}, f32[5,8,128]{2,1,0:T(8,128)S(1)}, u32[]{:S(2)}, u32[]{:S(2)}) collective-permute-start(f32[5,8,128]{2,1,0:T(8,128)S(1)} %get-tuple-element.63.refs_0_), channel_id=1, source_target_pairs={{0,2},{1,3},{2,0},{3,1},{4,6},{5,7},{6,4},{7,5},{8,10},{9,11},{10,... | collective-permute-start | bytes 61448 | tf_op jit(solution)/shard_map/ppermute | solution.py:452
  22.9 3.1 %collective-permute-start.9 = (f32[5,8,128]{2,1,0:T(8,128)S(1)}, f32[5,8,128]{2,1,0:T(8,128)S(1)}, u32[]{:S(2)}, u32[]{:S(2)}) collective-permute-start(f32[5,8,128]{2,1,0:T(8,128)S(1)} %get-tuple-element.63.refs_0_), channel_id=1, source_target_pairs={{0,1},{1,0},{2,3},{3,2},{4,5},{5,4},{6,7},{7,6},{8,9},{9,8},{10,11... | collective-permute-start | bytes 61448 | tf_op jit(solution)/shard_map/ppermute | solution.py:452
  23.0 3.0 %copy-start.2 = (bf16[32,8192]{1,0:T(8,128)(2,1)S(1)}, bf16[32,8192]{1,0:T(8,128)(2,1)}, u32[]{:S(2)}) copy-start(bf16[32,8192]{1,0:T(8,128)(2,1)} %att_ref.1) | copy-start | bytes 1572868
  23.0 3.0 %copy-start.3 = (bf16[5,8192]{1,0:T(8,128)(2,1)S(1)}, bf16[5,8192]{1,0:T(8,128)(2,1)}, u32[]{:S(2)}) copy-start(bf16[5,8192]{1,0:T(8,128)(2,1)} %sp_ref.1) | copy-start | bytes 245764
  23.0 3.0 %copy-start.5 = (f32[8192]{0:T(1024)S(1)}, f32[8192]{0:T(1024)}, u32[]{:S(2)}) copy-start(f32[8192]{0:T(1024)} %param.10) | copy-start | bytes 98308
  23.0 3.0 %copy-start.6 = (f32[8192]{0:T(1024)S(1)}, f32[8192]{0:T(1024)}, u32[]{:S(2)}) copy-start(f32[8192]{0:T(1024)} %param.9) | copy-start | bytes 98308
  23.0 3.0 %copy-start.8 = (s32[64]{0:T(128)S(1)}, s32[64]{0:T(128)}, u32[]{:S(2)}) copy-start(s32[64]{0:T(128)} %win_ref.3) | copy-start | bytes 772
  28.3 17.8 %copy-start.4 = (f32[5,4096]{1,0:T(8,128)S(1)}, f32[5,4096]{1,0:T(8,128)}, u32[]{:S(2)}) copy-start(f32[5,4096]{1,0:T(8,128)} %sources_ref.1) | copy-start | bytes 245764
  28.3 18.6 %copy-start.7 = (f32[128,32]{0,1:T(8,128)S(1)}, f32[128,32]{0,1:T(8,128)}, u32[]{:S(2)}) copy-start(f32[128,32]{0,1:T(8,128)} %param.16) | copy-start | bytes 49156
  28.4 3.0 %collective-permute-start.10 = (f32[32,128]{1,0:T(8,128)S(1)}, f32[32,128]{1,0:T(8,128)S(1)}, u32[]{:S(2)}, u32[]{:S(2)}) collective-permute-start(f32[32,128]{1,0:T(8,128)S(1)} %right_sides.1.mine_ref), channel_id=1, source_target_pairs={{0,4},{4,0},{8,12},{12,8},{16,20},{20,16},{24,28},{28,24},{1,5},{5... | collective-permute-start | bytes 49160 | tf_op jit(solution)/shard_map/send/ppermute | solution.py:457
  31.4 3.9 %collective-permute-start.11 = (f32[12,8,128]{2,1,0:T(8,128)S(1)}, f32[12,8,128]{2,1,0:T(8,128)S(1)}, u32[]{:S(2)}, u32[]{:S(2)}) collective-permute-start(f32[12,8,128]{2,1,0:T(8,128)S(1)} %send.1.refs_0_), channel_id=1, source_target_pairs={{0,24},{4,28},{8,16},{12,20},{16,8},{20,12},{24,0},{28,4},{1,25},{... | collective-permute-start | bytes 147464 | tf_op jit(solution)/shard_map/ppermute | solution.py:461
  32.6 4.2 %collective-permute-start.12 = (f32[12,8,128]{2,1,0:T(8,128)S(1)}, f32[12,8,128]{2,1,0:T(8,128)S(1)}, u32[]{:S(2)}, u32[]{:S(2)}) collective-permute-start(f32[12,8,128]{2,1,0:T(8,128)S(1)} %send.1.refs_0_), channel_id=1, source_target_pairs={{0,16},{4,20},{8,24},{12,28},{16,0},{20,4},{24,8},{28,12},{1,17},{... | collective-permute-start | bytes 147464 | tf_op jit(solution)/shard_map/ppermute | solution.py:461
  33.8 3.2 %collective-permute-start.13 = (f32[12,8,128]{2,1,0:T(8,128)S(1)}, f32[12,8,128]{2,1,0:T(8,128)S(1)}, u32[]{:S(2)}, u32[]{:S(2)}) collective-permute-start(f32[12,8,128]{2,1,0:T(8,128)S(1)} %send.1.refs_0_), channel_id=1, source_target_pairs={{0,8},{4,12},{8,0},{12,4},{16,24},{20,28},{24,16},{28,20},{1,9},{5... | collective-permute-start | bytes 147464 | tf_op jit(solution)/shard_map/ppermute | solution.py:461
  37.2 5.3 %collective-permute-start.14 = (f32[10,8,128]{2,1,0:T(8,128)S(1)}, f32[10,8,128]{2,1,0:T(8,128)S(1)}, u32[]{:S(2)}, u32[]{:S(2)}) collective-permute-start(f32[10,8,128]{2,1,0:T(8,128)S(1)} %get-tuple-element.70), channel_id=1, source_target_pairs={{4,5},{1,2},{6,7},{12,13},{9,10},{14,15},{20,21},{17,18},{22,23},{... | collective-permute-start | bytes 122888 | tf_op jit(solution)/shard_map/ppermute | solution.py:566
  39.9 3.5 %collective-permute-start.15 = (f32[10,8,128]{2,1,0:T(8,128)S(1)}, f32[10,8,128]{2,1,0:T(8,128)S(1)}, u32[]{:S(2)}, u32[]{:S(2)}) collective-permute-start(f32[10,8,128]{2,1,0:T(8,128)S(1)} %get-tuple-element.71), channel_id=1, source_target_pairs={{0,4},{4,0},{8,12},{12,8},{16,20},{20,16},{24,28},{28,24},{1,5},{5... | collective-permute-start | bytes 122888 | tf_op jit(solution)/shard_map/ppermute | solution.py:457
  44.6 2.4 %collective-permute-start.16 = (f32[32,128]{1,0:T(8,128)S(1)}, f32[32,128]{1,0:T(8,128)S(1)}, u32[]{:S(2)}, u32[]{:S(2)}) collective-permute-start(f32[32,128]{1,0:T(8,128)S(1)} %sweeps.1.mine_ref), channel_id=1, source_target_pairs={{0,4},{4,0},{8,12},{12,8},{16,20},{20,16},{24,28},{28,24},{1,5},{5... | collective-permute-start | bytes 49160 | tf_op jit(solution)/shard_map/finish/ppermute | solution.py:457
